TPU v7x, 32 devices: a whole 2x2x4 slice. The times are simulated.
32 devices in a mesh: fine: 8 (over z, x), coarse: 4 (over y, core).
Axes of the slice: x: 2, y: 2, z: 4, core: 2. Of those that a mesh axis runs over, the one named last changes fastest.
Arguments:
- rhs: float32 [65536], P(('fine', 'coarse')), may hold values from -6 to 6
- fine_values: bfloat16 [7, 64, 65536], P(None, None, ('fine', 'coarse')), may hold values from -0.0501 to 1.05
- fine_columns: int32 [7, 1024], P(None, ('fine', 'coarse')), may hold values from 0 to 63, as said below
- smoother: bfloat16 [64, 65536], P(None, ('fine', 'coarse')), may hold values from -0.0601 to 1.0625
- reaction: float32 [65536], P(('fine', 'coarse')), may hold values from 0.2 to 2
- pit_counts: int32 [32], P(('fine', 'coarse')), may hold values from 1 to 32, 288 in all
- weights: float32 [65536], P(('fine', 'coarse')), may hold values from 0.04 to 0.4
- coarse_order: int32 [1024], P(('fine', 'coarse')), may hold values from 0 to 1023, each once
- coarse_values: bfloat16 [7, 64, 1024], P(None, None, 'coarse'), may hold values from -0.0501 to 1.05
- coarse_rows: int32 [7, 16], P(None, 'coarse'), may hold values from 0 to 15, as said below
- coarse_inverse: bfloat16 [64, 1024], P(None, 'coarse'), may hold values from -0.0301 to 0.5313
Outputs:
- solution: float32 [65536], P(('fine', 'coarse'))
- correction: float32 [1024], P('coarse')
Inputs may be any that keep to these rules, and one draw needn't show every extreme that they name: fine_columns[0, a] = a % 32 + 16, the aggregate itself. `coarse_order`: each coarse unknown once. coarse_rows[0, j] = j.
All inputs are finite; a program needn't handle non-finite values. No bound on the sum of `pit_counts` on one device may be relied on, other than what follows from the above.
Results may differ from a plain program's by a relative error of at most 0.0003.
Values sent between devices are 32-bit elements; how exact they have to be, the bound alone decides.
No kernel may reach another device: no remote copies, remote signals or barrier semaphores. Data moves between devices by JAX's collectives and lax.ppermute only.
A program may use at most 64 MiB of HBM per device.

v0:
```python
import jax
import jax.numpy as jnp
from jax import lax
from jax.sharding import PartitionSpec as P

AGGREGATE_CELLS = 64
FINE_NBRS = 7
COARSE_NBRS = 7
SWEEPS = 4
HALO = 16


def with_halo(block, sides, width):
    for axis, dim in sides:
        count = lax.axis_size(axis)
        forward = [(i, i + 1) for i in range(count - 1)]
        backward = [(target, source) for source, target in forward]
        low = lax.ppermute(
            lax.slice_in_dim(block, block.shape[dim] - width, None, axis=dim), axis, forward
        )
        high = lax.ppermute(lax.slice_in_dim(block, 0, width, axis=dim), axis, backward)
        block = jnp.concatenate([low, block, high], axis=dim)
    return block


def shards(
    rhs,
    fine_values,
    fine_columns,
    smoother,
    reaction,
    pit_counts,
    weights,
    coarse_order,
    coarse_values,
    coarse_rows,
    coarse_inverse,
):
    blocks = rhs.shape[0] // AGGREGATE_CELLS
    local_ids = jnp.arange(blocks, dtype=jnp.int32)
    pit_aggs = (local_ids < pit_counts[0]).astype(jnp.float32)
    pit_react = jnp.repeat(pit_aggs, AGGREGATE_CELLS) * reaction

    def smooth(input_vector):
        inverse_f = smoother.astype(jnp.float32).reshape(AGGREGATE_CELLS, blocks, AGGREGATE_CELLS)
        return jnp.einsum(
            "oni,ni->no",
            inverse_f,
            input_vector.reshape(blocks, AGGREGATE_CELLS),
            precision=lax.Precision.HIGHEST,
        ).reshape(-1)

    def fine_apply(input_vector):
        padded = with_halo(input_vector, ((("fine", "coarse"), 0),), HALO * AGGREGATE_CELLS)
        picked = padded.reshape(blocks + 2 * HALO, AGGREGATE_CELLS)[fine_columns]
        fine_value_entries = fine_values.astype(jnp.float32).reshape(
            FINE_NBRS, AGGREGATE_CELLS, blocks, AGGREGATE_CELLS
        )
        result = jnp.einsum(
            "kobi,kbi->bo", fine_value_entries, picked, precision=lax.Precision.HIGHEST
        ).reshape(-1)
        return result + pit_react * input_vector

    smoothed = smooth(rhs)
    residual = rhs - fine_apply(smoothed)
    restricted = jnp.sum((weights * residual).reshape(blocks, AGGREGATE_CELLS), axis=1)
    own_dofs = coarse_inverse.shape[1]
    own_blocks = own_dofs // AGGREGATE_CELLS
    groups = lax.axis_size("coarse")
    all_dofs = own_dofs * groups
    group_index = lax.axis_index("coarse")
    partial_value = jax.ops.segment_sum(restricted, coarse_order, num_segments=all_dofs)
    coarse_full = lax.psum(partial_value, ("fine", "coarse"))
    coarse_right_side = lax.dynamic_slice_in_dim(coarse_full, group_index * own_dofs, own_dofs)

    def coarse_scale(input_vector):
        inverse_f = coarse_inverse.astype(jnp.float32).reshape(
            AGGREGATE_CELLS, own_blocks, AGGREGATE_CELLS
        )
        return jnp.einsum(
            "oji,ji->jo",
            inverse_f,
            input_vector.reshape(own_blocks, AGGREGATE_CELLS),
            precision=lax.Precision.HIGHEST,
        ).reshape(-1)

    dof_rows = (
        coarse_rows[:, None, :] * AGGREGATE_CELLS
        + jnp.arange(AGGREGATE_CELLS, dtype=jnp.int32)[None, :, None]
    )
    correction = coarse_scale(coarse_right_side)
    for sweep_no in range(SWEEPS - 1):
        coarse_fine_value_entries = coarse_values.astype(jnp.float32).reshape(
            COARSE_NBRS, AGGREGATE_CELLS, own_blocks, AGGREGATE_CELLS
        )
        block_product = jnp.einsum(
            "vfmd,md->vfm",
            coarse_fine_value_entries,
            correction.reshape(own_blocks, AGGREGATE_CELLS),
            precision=lax.Precision.HIGHEST,
        )
        partial_image = jax.ops.segment_sum(
            block_product.reshape(-1), dof_rows.reshape(-1), num_segments=all_dofs
        )
        image_full = lax.psum(partial_image, "coarse")
        image_own = lax.dynamic_slice_in_dim(image_full, group_index * own_dofs, own_dofs)
        correction = correction + coarse_scale(coarse_right_side - image_own)
    everywhere = lax.all_gather(correction, "coarse", axis=0, tiled=True)
    corrected = smoothed + weights * jnp.repeat(everywhere[coarse_order], AGGREGATE_CELLS)
    solution = corrected + smooth(rhs - fine_apply(corrected))
    return (solution, correction)


def solution(mesh):
    in_specs = (
        P(("fine", "coarse")),
        P(None, None, ("fine", "coarse")),
        P(None, ("fine", "coarse")),
        P(None, ("fine", "coarse")),
        P(("fine", "coarse")),
        P(("fine", "coarse")),
        P(("fine", "coarse")),
        P(("fine", "coarse")),
        P(None, None, "coarse"),
        P(None, "coarse"),
        P(None, "coarse"),
    )
    out_specs = (P(("fine", "coarse")), P("coarse"))
    return jax.shard_map(shards, mesh=mesh, in_specs=in_specs, out_specs=out_specs, check_vma=False)
```

profile of v0, /device:TPU:8, one launch (start us, length us, event | category | flops | bytes accessed | tf_op | source)
XLA Modules:
  0.0 156.8 jit_solution(6635344408380562747)
XLA Ops:
  0.6 1.2 copy.59
  1.9 0.8 reshape.202
  3.2 3.7 %collective-permute-start.1 = (f32[1024]{0:T(1024)S(1)}, f32[1024]{0:T(1024)S(1)}, u32[]{:S(2)}, u32[]{:S(2)}) collective-permute-start(f32[1024]{0:T(1024)S(1)} %slice.21), channel_id=1, source_target_pairs={{1,0},{2,1},{3,2},{4,3},{5,4},{6,5},{7,6},{8,7},{9,8},{10,9},{11,1... | collective-permute-start | bytes 12296 | tf_op jit(solution)/shard_map/ppermute | solution.py:21
  7.0 1.9 %collective-permute-start = (f32[1024]{0:T(1024)S(1)}, f32[1024]{0:T(1024)S(1)}, u32[]{:S(2)}, u32[]{:S(2)}) collective-permute-start(f32[1024]{0:T(1024)S(1)} %slice.19), channel_id=1, source_target_pairs={{0,1},{1,2},{2,3},{3,4},{4,5},{5,6},{6,7},{7,8},{8,9},{9,10},{10,1... | collective-permute-start | bytes 12296 | tf_op jit(solution)/shard_map/ppermute | solution.py:18
  8.9 0.7 compare_select_fusion
  10.3 0.7 broadcast_multiply_fusion
  11.1 0.7 compare_select_fusion.1
  11.9 6.5 %reshape.116 = bf16[7,64,32,64]{3,2,1,0:T(8,128)(2,1)} reshape(bf16[7,64,2048]{2,1,0:T(8,128)(2,1)} %param.12) | data formatting | bytes 3670016 | tf_op jit(solution)/shard_map/reshape | solution.py:56
  18.4 7.2 %copy.21 = bf16[7,64,32,64]{1,3,0,2:T(8,128)(2,1)} copy(bf16[7,64,32,64]{3,2,1,0:T(8,128)(2,1)} %reshape.116) | data formatting | bytes 3670016 | tf_op jit(solution)/shard_map/reshape | solution.py:56
  26.4 0.7 gather_fusion
  27.1 4.3 %fusion.5 = f32[32,1,64,1]{2,1,3,0:T(1,128)S(1)} fusion(bf16[7,64,32,64]{1,3,0,2:T(8,128)(2,1)} %copy.21, f32[7,32,64,1]{2,1,0,3:T(8,128)S(1)} %bitcast.81), kind=kOutput, calls=%fused_computation.16 | convolution fusion | flops 11010048 | bytes 1900544 | tf_op jit(solution)/shard_map/kobi,kbi->bo/dot_general | solution.py:59
  31.7 0.9 scatter_custom_fusion
  32.6 39.7 %psum.28 = f32[1024]{0:T(1024)S(1)} all-reduce(f32[1024]{0:T(1024)S(1)} %scatter_custom_fusion), channel_id=1, replica_groups=mesh['fine'=8,'coarse'=4] {'fine','coarse'}, use_global_device_ids=true, to_apply=%region_2.0 | all-reduce | flops 1024 | bytes 8192 | tf_op jit(solution)/shard_map/psum | solution.py:73
  72.6 0.6 fusion
  73.4 12.9 %scatter_custom_fusion.1 = f32[1024]{0:T(1024)S(1)} fusion(s32[1792]{0:T(1024)S(1)} %reshape.168, f32[1792]{0:T(1024)S(1)} %reshape.170, f32[]{:T(128)} %constant.6.clone.1), kind=kCustom, calls=%fused_computation.31 | custom fusion | flops 1792 | bytes 4100 | tf_op jit(solution)/shard_map/scatter-add | solution.py:102
  86.3 6.2 %psum.29 = f32[1024]{0:T(1024)S(1)} all-reduce(f32[1024]{0:T(1024)S(1)} %scatter_custom_fusion.1), channel_id=1, replica_groups=mesh['fine'=8,'coarse'=4] {'coarse'}, use_global_device_ids=true, to_apply=%region_4.0 | all-reduce | flops 1024 | bytes 8192 | tf_op jit(solution)/shard_map/psum | solution.py:105
  92.8 0.6 fusion.1
  93.5 12.9 %scatter_custom_fusion.2 = f32[1024]{0:T(1024)S(1)} fusion(s32[1792]{0:T(1024)S(1)} %reshape.168, f32[1792]{0:T(1024)S(1)} %reshape.178, f32[]{:T(128)} %constant.6.clone.1), kind=kCustom, calls=%fused_computation.29 | custom fusion | flops 1792 | bytes 4100 | tf_op jit(solution)/shard_map/scatter-add | solution.py:102
  106.4 6.9 %psum.30 = f32[1024]{0:T(1024)S(1)} all-reduce(f32[1024]{0:T(1024)S(1)} %scatter_custom_fusion.2), channel_id=1, replica_groups=mesh['fine'=8,'coarse'=4] {'coarse'}, use_global_device_ids=true, to_apply=%region_6.0 | all-reduce | flops 1024 | bytes 8192 | tf_op jit(solution)/shard_map/psum | solution.py:105
  113.7 0.6 fusion.2
  114.4 12.9 %scatter_custom_fusion.3 = f32[1024]{0:T(1024)S(1)} fusion(s32[1792]{0:T(1024)S(1)} %reshape.168, f32[1792]{0:T(1024)S(1)} %reshape.186, f32[]{:T(128)} %constant.6.clone.1), kind=kCustom, calls=%fused_computation.27 | custom fusion | flops 1792 | bytes 4100 | tf_op jit(solution)/shard_map/scatter-add | solution.py:102
  127.3 5.8 %psum.31 = f32[1024]{0:T(1024)S(1)} all-reduce(f32[1024]{0:T(1024)S(1)} %scatter_custom_fusion.3), channel_id=1, replica_groups=mesh['fine'=8,'coarse'=4] {'coarse'}, use_global_device_ids=true, to_apply=%region_8.0 | all-reduce | flops 1024 | bytes 8192 | tf_op jit(solution)/shard_map/psum | solution.py:105
  133.5 5.1 %all-gather = f32[4,1,256]{2,1,0:T(1,128)S(1)} all-gather(f32[1,1,256]{2,1,0:T(1,128)S(1)} %reshape.199), channel_id=1, replica_groups=mesh['fine'=8,'coarse'=4] {'coarse'}, dimensions={0}, use_global_device_ids=true | all-gather | bytes 5120 | tf_op jit(solution)/shard_map/all_gather | solution.py:108
  138.5 0.7 gather_fusion.1
  139.4 4.2 %collective-permute-start.3 = (f32[1024]{0:T(1024)S(1)}, f32[1024]{0:T(1024)S(1)}, u32[]{:S(2)}, u32[]{:S(2)}) collective-permute-start(f32[1024]{0:T(1024)S(1)} %get-tuple-element.7), channel_id=1, source_target_pairs={{1,0},{2,1},{3,2},{4,3},{5,4},{6,5},{7,6},{8,7},{9,8},{10,9},{11,1... | collective-permute-start | bytes 12296 | tf_op jit(solution)/shard_map/ppermute | solution.py:21
  143.6 1.9 %collective-permute-start.2 = (f32[1024]{0:T(1024)S(1)}, f32[1024]{0:T(1024)S(1)}, u32[]{:S(2)}, u32[]{:S(2)}) collective-permute-start(f32[1024]{0:T(1024)S(1)} %get-tuple-element.6), channel_id=1, source_target_pairs={{0,1},{1,2},{2,3},{3,4},{4,5},{5,6},{6,7},{7,8},{8,9},{9,10},{10,1... | collective-permute-start | bytes 12296 | tf_op jit(solution)/shard_map/ppermute | solution.py:18
  145.5 0.6 add.94
  146.2 4.1 %collective-permute-done.2 = f32[1024]{0:T(1024)S(1)} collective-permute-done((f32[1024]{0:T(1024)S(1)}, f32[1024]{0:T(1024)S(1)}, u32[]{:S(2)}, u32[]{:S(2)}) %collective-permute-start.2) | collective-permute-done | bytes 4128 | tf_op jit(solution)/shard_map/ppermute | solution.py:18
  150.4 0.7 gather_fusion.2
  151.1 4.3 %fusion.3 = f32[32,1,64,1]{2,1,3,0:T(1,128)S(1)} fusion(bf16[7,64,32,64]{1,3,0,2:T(8,128)(2,1)} %copy.21, f32[7,32,64,1]{2,1,0,3:T(8,128)S(1)} %bitcast.80), kind=kOutput, calls=%fused_computation.14 | convolution fusion | flops 11010048 | bytes 1900544 | tf_op jit(solution)/shard_map/kobi,kbi->bo/dot_general | solution.py:59
  155.6 0.5 fusion.22
  156.2 0.6 add.99
  (64 shorter events, 4.3 us)
Async XLA Ops:
  3.2 23.1 %collective-permute-start.1 = (f32[1024]{0:T(1024)S(1)}, f32[1024]{0:T(1024)S(1)}, u32[]{:S(2)}, u32[]{:S(2)}) collective-permute-start(f32[1024]{0:T(1024)S(1)} %slice.21), channel_id=1, source_target_pairs={{1,0},{2,1},{3,2},{4,3},{5,4},{6,5},{7,6},{8,7},{9,8},{10,9},{11,1... | collective-permute-start | bytes 12296 | tf_op jit(solution)/shard_map/ppermute | solution.py:21
  7.0 19.3 %collective-permute-start = (f32[1024]{0:T(1024)S(1)}, f32[1024]{0:T(1024)S(1)}, u32[]{:S(2)}, u32[]{:S(2)}) collective-permute-start(f32[1024]{0:T(1024)S(1)} %slice.19), channel_id=1, source_target_pairs={{0,1},{1,2},{2,3},{3,4},{4,5},{5,6},{6,7},{7,8},{8,9},{9,10},{10,1... | collective-permute-start | bytes 12296 | tf_op jit(solution)/shard_map/ppermute | solution.py:18
  18.4 7.4 %copy-start.2 = (bf16[64,256]{1,0:T(8,128)(2,1)S(1)}, bf16[64,256]{1,0:T(8,128)(2,1)}, u32[]{:S(2)}) copy-start(bf16[64,256]{1,0:T(8,128)(2,1)} %param.21) | copy-start | bytes 98308
  18.4 7.7 %copy-start = (bf16[7,64,256]{2,1,0:T(8,128)(2,1)S(1)}, bf16[7,64,256]{2,1,0:T(8,128)(2,1)}, u32[]{:S(2)}) copy-start(bf16[7,64,256]{2,1,0:T(8,128)(2,1)} %param.19) | copy-start | bytes 688132
  25.6 5.8 %copy-start.1 = (f32[2048]{0:T(1024)S(1)}, f32[2048]{0:T(1024)}, u32[]{:S(2)}) copy-start(f32[2048]{0:T(1024)} %param.11) | copy-start | bytes 24580
  25.6 5.8 %copy-start.3 = (f32[2048]{0:T(1024)S(1)}, f32[2048]{0:T(1024)}, u32[]{:S(2)}) copy-start(f32[2048]{0:T(1024)} %param.17) | copy-start | bytes 24580
  25.6 5.9 %copy-start.4 = (f32[2048]{0:T(1024)S(1)}, f32[2048]{0:T(1024)}, u32[]{:S(2)}) copy-start(f32[2048]{0:T(1024)} %param.15) | copy-start | bytes 24580
  139.4 6.8 %collective-permute-start.3 = (f32[1024]{0:T(1024)S(1)}, f32[1024]{0:T(1024)S(1)}, u32[]{:S(2)}, u32[]{:S(2)}) collective-permute-start(f32[1024]{0:T(1024)S(1)} %get-tuple-element.7), channel_id=1, source_target_pairs={{1,0},{2,1},{3,2},{4,3},{5,4},{6,5},{7,6},{8,7},{9,8},{10,9},{11,1... | collective-permute-start | bytes 12296 | tf_op jit(solution)/shard_map/ppermute | solution.py:21
  143.6 6.7 %collective-permute-start.2 = (f32[1024]{0:T(1024)S(1)}, f32[1024]{0:T(1024)S(1)}, u32[]{:S(2)}, u32[]{:S(2)}) collective-permute-start(f32[1024]{0:T(1024)S(1)} %get-tuple-element.6), channel_id=1, source_target_pairs={{0,1},{1,2},{2,3},{3,4},{4,5},{5,6},{6,7},{7,8},{8,9},{9,10},{10,1... | collective-permute-start | bytes 12296 | tf_op jit(solution)/shard_map/ppermute | solution.py:18
where the time goes:
time: 158 us; the launch traced here: 157 us
  blocking collectives  63.6 us (40%)
  other arithmetic  44.4 us (28%)
  local copies, waits for them, and re-layouts  21.1 us (13%)
  starting transfers between devices  11.7 us (7%)
  matrix products  10.3 us (7%)
  waiting for transfers between devices  4.16 us (3%)
    psum x1, blocking collectives, shards(): coarse_full = lax.psum(partial_value, ('fine', 'coarse'))  39.7 us
    scatter-add x3, other arithmetic, shards(): jax.ops.segment_sum(block_product.reshape(-1), dof_rows.reshape(-1), num_...  38.7 us
    psum x3, blocking collectives, shards(): image_full = lax.psum(partial_image, 'coarse')  18.8 us
    reshape x2, local copies, waits for them, and re-layouts, fine_apply(): fine_values.astype(jnp.float32)  13.7 us
    dot_general x2, matrix products, fine_apply(): jnp.einsum('kobi,kbi->bo', fine_value_entries, picked, precision=lax.Prec...  8.59 us
    ppermute x2, starting transfers between devices, with_halo(): lax.ppermute(lax.slice_in_dim(block, 0, width, axis=dim), axis, backward)  7.89 us
    all_gather x1, blocking collectives, shards(): everywhere = lax.all_gather(correction, 'coarse', axis=0, tiled=True)  5.06 us
    ppermute x2, waiting for transfers between devices, with_halo(): lax.ppermute(lax.slice_in_dim(block, block.shape[dim] - width, None, axis...  4.15 us
  transfers between devices with their start and end apart: 4, of which 1 were waited for; matrix products, arithmetic and copies ran while one was open for 11% of the time, Pallas kernels for 0%

commit v1 on v0

v1 whole, which is shorter than its diff:
```python
import functools

import jax
import jax.numpy as jnp
from jax import lax
from jax.experimental import pallas as pl
from jax.experimental.pallas import tpu as pltpu
from jax.sharding import PartitionSpec as P

CELLS = 64
LANES = 128
HALO_ROWS = 8
SWEEPS = 4
BOTH = ("fine", "coarse")
f32, bf16, i32 = jnp.float32, jnp.bfloat16, jnp.int32
VMEM_LIMIT = 24 * 1024 * 1024


def iota(shape, axis):
    return lax.broadcasted_iota(i32, shape, axis)


def split(x):
    high = x.astype(bf16)
    return high, (x - high.astype(f32)).astype(bf16)


def dot(a, b):
    return lax.dot_general(a, b, (((1,), (0,)), ((), ())), preferred_element_type=f32)


def dot_t(a, b):
    return lax.dot_general(a, b, (((1,), (1,)), ((), ())), preferred_element_type=f32)


def cell_sums(high_ref, low_ref):
    width = high_ref.shape[1]
    pairs = width // LANES
    row, lane = iota((2 * pairs, width), 0), iota((2 * pairs, width), 1)
    member = (lane // CELLS == 2 * (row % pairs) + row // pairs).astype(bf16)
    sums = dot_t(member, high_ref[...]) + dot_t(member, low_ref[...])
    return jnp.concatenate([sums[:pairs], sums[pairs:]], axis=1)


def apply_smoother(vector, smoother_ref, high_ref, low_ref):
    for p in range(vector.shape[0]):
        cols = pl.ds(p * LANES, LANES)
        product = smoother_ref[:, cols].astype(f32) * vector[p : p + 1, :]
        high_ref[:, cols], low_ref[:, cols] = split(product)
    return cell_sums(high_ref, low_ref)


def apply_fine(window, fine_ref, columns_ref, picked_ref, high_ref, low_ref):
    nbrs, _, width = fine_ref.shape
    pairs = width // LANES
    rows = window.shape[0]
    both = jnp.concatenate([window, pltpu.roll(window, CELLS, 1)], axis=0)
    high, low = split(both)
    table = jnp.concatenate([high, low], axis=0)
    aggs = columns_ref.shape[1]
    at, who = iota((pairs, aggs), 1), iota((pairs, aggs), 0)
    entry = iota((pairs, 4 * rows), 1) % (2 * rows)
    halves = []
    for half in range(2):
        parts = []
        for k in range(nbrs):
            chosen = jnp.where(at == 2 * who + half, columns_ref[k : k + 1, :].astype(f32), 0.0)
            block = jnp.sum(chosen, axis=1, keepdims=True).astype(i32)
            place = block // 2 + jnp.where(block % 2 == half, 0, rows)
            parts.append((entry == place).astype(bf16))
        halves.append(dot(jnp.concatenate(parts, axis=0), table))
    lane = iota(halves[0].shape, 1)
    picked_ref[...] = jnp.where(lane < CELLS, halves[0], halves[1])
    for p in range(pairs):
        cols = pl.ds(p * LANES, LANES)
        total = None
        for k in range(nbrs):
            term = fine_ref[k, :, cols].astype(f32) * picked_ref[pl.ds(k * pairs + p, 1), :]
            total = term if total is None else total + term
        high_ref[:, cols], low_ref[:, cols] = split(total)
    return cell_sums(high_ref, low_ref)


def as_columns(row, pairs):
    shape = (pairs, row.shape[1])
    at, who = iota(shape, 1), iota(shape, 0)
    return [
        jnp.sum(jnp.where(at == 2 * who + half, row, 0.0), axis=1, keepdims=True)
        for half in range(2)
    ]


def by_half(columns, shape):
    return jnp.where(iota(shape, 1) < CELLS, columns[0], columns[1])


def start_kernel(rhs_ref, weights_ref, order_ref, smoother_ref, near_ref, onward_ref, own_ref, high_ref, low_ref):
    pairs = rhs_ref.shape[0]
    smoothed = apply_smoother(rhs_ref[...], smoother_ref, high_ref, low_ref)
    order = by_half(as_columns(order_ref[...].astype(f32), pairs), (pairs, LANES))
    even = lax.axis_index("coarse") % 2 == 0
    for i, part in enumerate((smoothed, weights_ref[...], order)):
        own_ref[i] = part
        bottom, top = part[:HALO_ROWS], part[pairs - HALO_ROWS :]
        near_ref[i] = jnp.where(even, top, bottom)
        onward_ref[i] = jnp.where(even, bottom, top)


def window_of(near_ref, far_ref, own_ref, device, devices):
    even = device % 2 == 0
    near, far = near_ref[...], far_ref[...]
    low = jnp.where(device == 0, 0.0, jnp.where(even, far, near))
    high = jnp.where(device == devices - 1, 0.0, jnp.where(even, near, far))
    return [jnp.concatenate([low[i], own_ref[i], high[i]], axis=0) for i in range(3)]


def device_index():
    return lax.axis_index("fine") * lax.axis_size("coarse") + lax.axis_index("coarse")


def reaction_of(reaction_ref, counts_ref):
    shape = reaction_ref.shape
    agg = 2 * iota(shape, 0) + iota(shape, 1) // CELLS
    return jnp.where(agg < counts_ref[0], reaction_ref[...], 0.0)


def residual_kernel(
    devices, counts_ref, near_ref, far_ref, own_ref, rhs_ref, reaction_ref, columns_ref, fine_ref,
    out_ref, picked_ref, high_ref, low_ref,
):
    smoothed, _, _ = window_of(near_ref, far_ref, own_ref, device_index(), devices)
    image = apply_fine(smoothed, fine_ref, columns_ref, picked_ref, high_ref, low_ref)
    image = image + reaction_of(reaction_ref, counts_ref) * own_ref[0]
    weighted = own_ref[1] * (rhs_ref[...] - image)
    pairs = weighted.shape[0]
    shape = (pairs, LANES)
    lane, who = iota(shape, 1), iota(shape, 0)
    row = jnp.zeros((1, LANES), f32)
    for half in range(2):
        inside = lane // CELLS == half
        restricted = jnp.sum(jnp.where(inside, weighted, 0.0), axis=1, keepdims=True)
        order = jnp.max(jnp.where(inside, own_ref[2], 0.0), axis=1, keepdims=True)
        spread = jnp.where(lane == 2 * who + half, restricted, 0.0)
        spread = spread + jnp.where(lane == 2 * (pairs + who) + half, order, 0.0)
        row = row + jnp.sum(spread, axis=0, keepdims=True)
    out_ref[...] = jnp.broadcast_to(row, out_ref.shape)


def finish(corr, own_ref, window, rhs_ref, reaction_ref, counts_ref, columns_ref, fine_ref, smoother_ref,
           out_ref, picked_ref, high_ref, low_ref):
    smoothed, weights, _ = window
    corrected = smoothed + weights * corr
    pairs = rhs_ref.shape[0]
    mine = corrected[HALO_ROWS : HALO_ROWS + pairs]
    image = apply_fine(corrected, fine_ref, columns_ref, picked_ref, high_ref, low_ref)
    image = image + reaction_of(reaction_ref, counts_ref) * mine
    out_ref[...] = mine + apply_smoother(rhs_ref[...] - image, smoother_ref, high_ref, low_ref)


def pack_kernel(rows_ref, values_ref, inverse_ref, out_ref):
    nbrs, own_blocks = rows_ref.shape
    deep = values_ref.shape[0]
    out_ref[pl.ds(0, deep), :] = values_ref[...].astype(f32)
    out_ref[pl.ds(deep, CELLS), :] = inverse_ref[...].astype(f32)
    shape = (8, out_ref.shape[1])
    lane = iota(shape, 1)
    rows = jnp.zeros(shape, f32)
    for k in range(nbrs):
        for j in range(own_blocks):
            here = (lane // 32 == k) & (lane % 16 == j)
            rows = jnp.where(here, rows_ref[k, j].astype(f32), rows)
    out_ref[pl.ds(deep + CELLS, 8), :] = rows


def solve_kernel(
    devices, counts_ref, gathered_ref, near_ref, far_ref, own_ref, rhs_ref, reaction_ref, columns_ref, fine_ref,
    smoother_ref, part0_ref, part1_ref, part2_ref, part3_ref,
    out_ref, correction_ref, blocks_ref, inverse_ref, picked_ref, high_ref, low_ref,
):
    part_refs = (part0_ref, part1_ref, part2_ref, part3_ref)
    me = lax.axis_index("coarse")
    parts = len(part_refs)
    width = part0_ref.shape[1]
    own_blocks = width // CELLS
    groups = parts * own_blocks
    unknowns = groups * CELLS
    nbrs = (part0_ref.shape[0] - 8) // CELLS - 1
    deep = nbrs * CELLS
    for i, ref in enumerate(part_refs):
        blocks_ref[i] = ref[pl.ds(0, deep), :].astype(bf16)
        inverse_ref[i] = ref[pl.ds(deep, CELLS), :].astype(bf16)

    def place(group):
        return jnp.bitwise_xor(group // own_blocks, me) * own_blocks + group % own_blocks

    lane = iota((1, width), 1)
    target = jnp.zeros((1, width), f32)
    for i, ref in enumerate(part_refs):
        rows = ref[pl.ds(deep + CELLS, 8), :][0:1, :]
        rows = jnp.where((lane % 16 < own_blocks) & (lane < 32 * nbrs), rows, 0.0)
        target = target + (rows if i == 0 else pltpu.roll(rows, i * own_blocks, 1))
    target = place(target.astype(i32))
    scatter = ((iota((groups, width), 0) == target) & (lane < 32 * nbrs)).astype(bf16)[:, : 32 * nbrs]

    gathered = gathered_ref[...]
    devs = gathered.shape[0]
    lane = iota((8, LANES), 1)
    lefts, rights = [], []
    for start in range(0, devs, 32):
        value = jnp.zeros((8, LANES), f32)
        order = jnp.zeros((8, LANES), f32)
        for i in range(4):
            piece = gathered[start + 8 * i : start + 8 * i + 8]
            here = lane // 32 == i
            value = jnp.where(here, pltpu.roll(piece, 32 * i, 1) if i else piece, value)
            order = jnp.where(here, pltpu.roll(piece, (32 * i + 96) % LANES, 1) if i != 1 else piece, order)
        order = order.astype(i32)
        group, unit = place(order // CELLS), order % CELLS
        for s in range(8):
            left = jnp.where(iota((groups, LANES), 0) == group[s : s + 1], value[s : s + 1], 0.0)
            lefts.append(jnp.concatenate(split(left), axis=0))
            rights.append((iota((CELLS, LANES), 0) == unit[s : s + 1]).astype(bf16))
    right_side = dot_t(jnp.concatenate(lefts, axis=1), jnp.concatenate(rights, axis=1))
    right_side = right_side[:groups] + right_side[groups:]

    own_block = iota((groups, unknowns), 1) // CELLS == iota((groups, unknowns), 0)

    def spread(x):
        wide = jnp.concatenate([x] * (LANES // CELLS), axis=1)
        wide = jnp.concatenate([wide] * (unknowns // LANES), axis=1)
        return jnp.concatenate(split(jnp.where(own_block, wide, 0.0)), axis=0)

    def product(x, ref):
        wide = spread(x)
        total = None
        for i in range(parts):
            term = dot_t(wide[:, i * width : (i + 1) * width], ref[i])
            total = term if total is None else total + term
        return total[:groups] + total[groups:]

    correction = product(right_side, inverse_ref)
    for _ in range(SWEEPS - 1):
        sums = product(correction, blocks_ref)
        pieces = []
        for k in range(nbrs):
            pieces += split(sums[:, k * CELLS : (k + 1) * CELLS])
        image = jnp.zeros((groups, CELLS), f32)
        high, low = pieces[0::2], pieces[1::2]
        stacked = jnp.concatenate([p for pair in zip(high, low) for p in pair], axis=0)
        image = dot(scatter, stacked)
        correction = correction + product(right_side - image, inverse_ref)
    correction_ref[...] = correction[:own_blocks]

    window = window_of(near_ref, far_ref, own_ref, device_index(), devices)
    order = window[2].astype(i32)
    rows = order.shape[0]
    unit = jnp.concatenate([order[:, :CELLS], order[:, CELLS:]], axis=0)
    pick = (iota(unit.shape, 1) == unit % CELLS).astype(bf16)
    values = dot_t(pick, jnp.concatenate(split(correction), axis=0))
    group = place(unit[:, : 2 * groups] // CELLS)
    values = jnp.sum(jnp.where(iota(values.shape, 1) % groups == group, values, 0.0), axis=1, keepdims=True)
    corr = by_half([values[:rows], values[rows:]], (rows, LANES))
    finish(corr, own_ref, window, rhs_ref, reaction_ref, counts_ref, columns_ref, fine_ref, smoother_ref,
           out_ref, picked_ref, high_ref, low_ref)


def finish_kernel(
    devices, counts_ref, corr_ref, near_ref, far_ref, own_ref, rhs_ref, reaction_ref, columns_ref, fine_ref,
    smoother_ref, out_ref, picked_ref, high_ref, low_ref,
):
    window = window_of(near_ref, far_ref, own_ref, device_index(), devices)
    finish(corr_ref[...], own_ref, window, rhs_ref, reaction_ref, counts_ref, columns_ref, fine_ref, smoother_ref,
           out_ref, picked_ref, high_ref, low_ref)


def call(kernel, out_shape, smem=(), scratch=(), count=0):
    specs = [pl.BlockSpec(memory_space=pltpu.SMEM if i in smem else pltpu.VMEM) for i in range(count)]
    return pl.pallas_call(
        kernel,
        out_shape=out_shape,
        in_specs=specs,
        out_specs=jax.tree.map(lambda _: pl.BlockSpec(memory_space=pltpu.VMEM), out_shape),
        scratch_shapes=list(scratch),
        compiler_params=pltpu.CompilerParams(vmem_limit_bytes=VMEM_LIMIT),
    )


def shape_of(*dims):
    return jax.ShapeDtypeStruct(dims, f32)


def coarse_by_parts(restricted, coarse_order, coarse_values, coarse_rows, coarse_inverse):
    own = coarse_inverse.shape[1]
    own_blocks = own // CELLS
    total = own * lax.axis_size("coarse")
    start = lax.axis_index("coarse") * own
    side = jnp.zeros((total,), f32).at[coarse_order].add(restricted)
    side = lax.dynamic_slice_in_dim(lax.psum(side, BOTH), start, own)
    values = coarse_values.astype(f32).reshape(-1, CELLS, own_blocks, CELLS)
    inverse = coarse_inverse.astype(f32).reshape(CELLS, own_blocks, CELLS)

    def scale(x):
        x = x.reshape(own_blocks, CELLS)
        return jnp.einsum("oji,ji->jo", inverse, x, precision=lax.Precision.HIGHEST).reshape(-1)

    correction = scale(side)
    for _ in range(SWEEPS - 1):
        x = correction.reshape(own_blocks, CELLS)
        sums = jnp.einsum("vfmd,md->vmf", values, x, precision=lax.Precision.HIGHEST)
        image = jax.ops.segment_sum(
            sums.reshape(-1, CELLS), coarse_rows.reshape(-1), num_segments=total // CELLS
        ).reshape(-1)
        image = lax.dynamic_slice_in_dim(lax.psum(image, "coarse"), start, own)
        correction = correction + scale(side - image)
    return correction, lax.all_gather(correction, "coarse", axis=0, tiled=True)


def shards(
    devices, rhs, fine_values, fine_columns, smoother, reaction, pit_counts, weights, coarse_order,
    coarse_values, coarse_rows, coarse_inverse,
):
    cells = rhs.shape[0]
    pairs = cells // LANES
    aggs = 2 * pairs
    nbrs = fine_columns.shape[0]
    parts = lax.axis_size("coarse")
    rhs, reaction, weights = (x.reshape(pairs, LANES) for x in (rhs, reaction, weights))
    rows = pairs + 2 * HALO_ROWS
    products = [pltpu.VMEM((CELLS, cells), bf16)] * 2
    scratch = [pltpu.VMEM((nbrs * pairs, LANES), f32)] + products
    edge = shape_of(3, HALO_ROWS, LANES)

    near, onward, own = call(
        start_kernel, (edge, edge, shape_of(3, pairs, LANES)), scratch=products, count=4
    )(rhs, weights, coarse_order.reshape(1, aggs), smoother)

    partner = [(d, d ^ 1) for d in range(devices)]
    chain = []
    for d in range(devices):
        target = d + 2 if d % 2 == 0 else d - 2
        chain.append((d, target if 0 <= target < devices else d ^ 1))
    far = lax.ppermute(lax.ppermute(onward, BOTH, partner), BOTH, chain)
    near = lax.ppermute(near, BOTH, partner)

    copied = parts == 4 and devices % 32 == 0 and devices <= 64
    if copied:
        deep = coarse_values.shape[0] * CELLS
        width = coarse_inverse.shape[1]
        packed = call(pack_kernel, shape_of(deep + CELLS + 8, width), smem=(0,), count=3)(
            coarse_rows, coarse_values.reshape(deep, width), coarse_inverse
        )
        other = lax.ppermute(packed, "coarse", [(c, c ^ 2) for c in range(parts)])
        swap = [(c, c ^ 1) for c in range(parts)]
        pieces = (packed, lax.ppermute(packed, "coarse", swap), other, lax.ppermute(other, "coarse", swap))

    sent = call(
        functools.partial(residual_kernel, devices), shape_of(devices, LANES), smem=(0,), scratch=scratch, count=8
    )(pit_counts, near, far, own, rhs, reaction, fine_columns, fine_values)

    common = (near, far, own, rhs, reaction, fine_columns, fine_values, smoother)
    if copied:
        gathered = lax.all_to_all(sent, BOTH, 0, 0, tiled=True)
        result, correction = call(
            functools.partial(solve_kernel, devices),
            (shape_of(pairs, LANES), shape_of(width // CELLS, CELLS)),
            smem=(0,),
            scratch=[pltpu.VMEM((parts, deep, width), bf16), pltpu.VMEM((parts, CELLS, width), bf16)] + scratch,
            count=14,
        )(pit_counts, gathered, *common, *pieces)
        correction = correction.reshape(-1)
    else:
        correction, everywhere = coarse_by_parts(
            sent[0, :aggs], coarse_order, coarse_values, coarse_rows, coarse_inverse
        )
        index = device_index()
        low = jnp.where(index == 0, 0.0, jnp.where(index % 2 == 0, far[2], near[2]))
        high = jnp.where(index == devices - 1, 0.0, jnp.where(index % 2 == 0, near[2], far[2]))
        order = jnp.concatenate([low, own[2], high], axis=0).astype(i32)
        corr = jnp.repeat(everywhere[order[:, ::CELLS]], CELLS, axis=1)
        result = call(
            functools.partial(finish_kernel, devices), shape_of(pairs, LANES), smem=(0,), scratch=scratch, count=10
        )(pit_counts, corr, *common)
    return result.reshape(-1), correction


def solution(mesh):
    devices = mesh.shape["fine"] * mesh.shape["coarse"]
    in_specs = (
        P(BOTH),
        P(None, None, BOTH),
        P(None, BOTH),
        P(None, BOTH),
        P(BOTH),
        P(BOTH),
        P(BOTH),
        P(BOTH),
        P(None, None, "coarse"),
        P(None, "coarse"),
        P(None, "coarse"),
    )
    return jax.shard_map(
        functools.partial(shards, devices),
        mesh=mesh,
        in_specs=in_specs,
        out_specs=(P(BOTH), P("coarse")),
        check_vma=False,
    )
```

time: 158 us -> 51.1 us (0.32)
  the two profiles are of different devices: /device:TPU:8 before, /device:TPU:0 now
where the time goes in v1:
time: 51.1 us; the launch traced here: 50.6 us
  waiting for transfers between devices  13.6 us (27%)
  blocking collectives  13.6 us (27%)
  local copies, waits for them, and re-layouts  9.04 us (18%)
  Pallas kernels  7.7 us (15%)
  starting transfers between devices  5.38 us (11%)
  between operations  1.34 us (3%)
    all_to_all x1, blocking collectives, shards(): gathered = lax.all_to_all(sent, BOTH, 0, 0, tiled=True)  13.6 us
    ppermute x1, waiting for transfers between devices, shards(): other = lax.ppermute(packed, 'coarse', [(c, c ^ 2) for c in range(parts)])  12.1 us
    unnamed x23, local copies, waits for them, and re-layouts  8.39 us
    pallas_call x1, Pallas kernels, shards(): call(functools.partial(solve_kernel, devices), (shape_of(pairs, LANES), s...  5.43 us
    ppermute x1, starting transfers between devices, shards(): other = lax.ppermute(packed, 'coarse', [(c, c ^ 2) for c in range(parts)])  3.03 us
    ppermute x2, starting transfers between devices, shards(): far = lax.ppermute(lax.ppermute(onward, BOTH, partner), BOTH, chain)  2.27 us
    ppermute x2, waiting for transfers between devices, shards(): far = lax.ppermute(lax.ppermute(onward, BOTH, partner), BOTH, chain)  1.5 us
    pallas_call x1, Pallas kernels, shards(): call(functools.partial(residual_kernel, devices), shape_of(devices, LANES...  1.22 us
  transfers between devices with their start and end apart: 6, of which 3 were waited for; matrix products, arithmetic and copies ran while one was open for 0% of the time, Pallas kernels for 3%

profile of v1, /device:TPU:0, one launch (start us, length us, event | category | flops | bytes accessed | tf_op | source)
XLA Modules:
  0.0 50.6 jit_solution(1105708609000915787)
XLA Ops:
  0.6 0.0 copy-start.3
  0.6 0.8 %copy.15.rows_ref = s32[7,4]{1,0:T(8,128)S(1)} copy(s32[7,4]{0,1:T(4,128)} %param.20) | data formatting | bytes 224 | tf_op args[9]
  1.5 0.0 copy-start.4
  1.5 0.9 %copy-done.4 = bf16[7,64,256]{2,1,0:T(8,128)(2,1)S(1)} copy-done((bf16[7,64,256]{2,1,0:T(8,128)(2,1)S(1)}, bf16[7,64,256]{2,1,0:T(8,128)(2,1)}, u32[]{:S(2)}) %copy-start.4) | copy-done | bytes 229400
  2.4 0.8 %copy-done.7 = bf16[64,256]{1,0:T(8,128)(2,1)S(1)} copy-done((bf16[64,256]{1,0:T(8,128)(2,1)S(1)}, bf16[64,256]{1,0:T(8,128)(2,1)}, u32[]{:S(2)}) %copy-start.7) | copy-done | bytes 32792
  3.1 0.7 %shard_map.124.part0_ref = f32[520,256]{1,0:T(8,128)S(1)} custom-call(s32[7,4]{1,0:T(8,128)S(1)} %copy.15.rows_ref, bf16[448,256]{1,0:T(8,128)(2,1)S(1)} %bitcast.10, bf16[64,256]{1,0:T(8,128)(2,1)S(1)} %copy-done.7), custom_call_target="tpu_custom_call" | custom-call | tf_op jit(solution)/shard_map/pallas_call | solution.py:349
  3.8 3.0 %collective-permute-start.4 = (f32[520,256]{1,0:T(8,128)S(1)}, f32[520,256]{1,0:T(8,128)S(1)}, u32[]{:S(2)}, u32[]{:S(2)}) collective-permute-start(f32[520,256]{1,0:T(8,128)S(1)} %shard_map.124.part0_ref), channel_id=1, source_target_pairs={{0,2},{1,3},{2,0},{3,1},{4,6},{5,7},{6,4},{7,5},{8,10},{9,11},{10,... | collective-permute-start | bytes 1597448 | tf_op jit(solution)/shard_map/ppermute | solution.py:352
  6.8 0.0 collective-permute-start.3
  6.8 12.1 %collective-permute-done.4.part2_ref = f32[520,256]{1,0:T(8,128)S(1)} collective-permute-done((f32[520,256]{1,0:T(8,128)S(1)}, f32[520,256]{1,0:T(8,128)S(1)}, u32[]{:S(2)}, u32[]{:S(2)}) %collective-permute-start.4) | collective-permute-done | bytes 532512 | tf_op jit(solution)/shard_map/ppermute | solution.py:352
  18.9 0.0 collective-permute-start.5
  18.9 0.9 %copy-done.2 = bf16[64,2048]{1,0:T(8,128)(2,1)S(1)} copy-done((bf16[64,2048]{1,0:T(8,128)(2,1)S(1)}, bf16[64,2048]{1,0:T(8,128)(2,1)}, u32[]{:S(2)}) %copy-start.2) | copy-done | bytes 262168
  19.9 0.7 %copy-done.5 = f32[2048]{0:T(1024)S(1)} copy-done((f32[2048]{0:T(1024)S(1)}, f32[2048]{0:T(1024)}, u32[]{:S(2)}) %copy-start.5) | copy-done | bytes 8216
  20.6 0.7 %copy-done.9 = f32[2048]{0:T(1024)S(1)} copy-done((f32[2048]{0:T(1024)S(1)}, f32[2048]{0:T(1024)}, u32[]{:S(2)}) %copy-start.9) | copy-done | bytes 8216
  21.3 0.7 %copy-done.10 = s32[32]{0:T(128)S(1)} copy-done((s32[32]{0:T(128)S(1)}, s32[32]{0:T(128)}, u32[]{:S(2)}) %copy-start.10) | copy-done | bytes 152
  21.9 0.4 shard_map.122
  22.3 0.5 %collective-permute-start.1 = (f32[3,8,128]{2,1,0:T(8,128)S(1)}, f32[3,8,128]{2,1,0:T(8,128)S(1)}, u32[]{:S(2)}, u32[]{:S(2)}) collective-permute-start(f32[3,8,128]{2,1,0:T(8,128)S(1)} %get-tuple-element.8), channel_id=1, source_target_pairs={{0,1},{1,0},{2,3},{3,2},{4,5},{5,4},{6,7},{7,6},{8,9},{9,8},{10,11... | collective-permute-start | bytes 36872 | tf_op jit(solution)/shard_map/ppermute | solution.py:342
  22.9 0.1 collective-permute-start
  22.9 0.8 %collective-permute-done.1 = f32[3,8,128]{2,1,0:T(8,128)S(1)} collective-permute-done((f32[3,8,128]{2,1,0:T(8,128)S(1)}, f32[3,8,128]{2,1,0:T(8,128)S(1)}, u32[]{:S(2)}, u32[]{:S(2)}) %collective-permute-start.1) | collective-permute-done | bytes 12320 | tf_op jit(solution)/shard_map/ppermute | solution.py:342
  23.7 1.7 %collective-permute-start.2 = (f32[3,8,128]{2,1,0:T(8,128)S(1)}, f32[3,8,128]{2,1,0:T(8,128)S(1)}, u32[]{:S(2)}, u32[]{:S(2)}) collective-permute-start(f32[3,8,128]{2,1,0:T(8,128)S(1)} %collective-permute-done.1), channel_id=1, source_target_pairs={{0,2},{1,0},{2,4},{3,1},{4,6},{5,3},{6,8},{7,5},{8,10},{9,7},{10,1... | collective-permute-start | bytes 36872 | tf_op jit(solution)/shard_map/ppermute | solution.py:342
  26.1 0.0 collective-permute-done.near_ref
  26.1 0.7 %collective-permute-done.2.far_ref = f32[3,8,128]{2,1,0:T(8,128)S(1)} collective-permute-done((f32[3,8,128]{2,1,0:T(8,128)S(1)}, f32[3,8,128]{2,1,0:T(8,128)S(1)}, u32[]{:S(2)}, u32[]{:S(2)}) %collective-permute-start.2) | collective-permute-done | bytes 12320 | tf_op jit(solution)/shard_map/ppermute | solution.py:342
  26.9 1.5 %copy-done = bf16[7,64,2048]{2,1,0:T(8,128)(2,1)S(1)} copy-done((bf16[7,64,2048]{2,1,0:T(8,128)(2,1)S(1)}, bf16[7,64,2048]{2,1,0:T(8,128)(2,1)}, u32[]{:S(2)}) %copy-start) | copy-done | bytes 1835032
  28.4 0.7 %copy-done.6 = f32[2048]{0:T(1024)S(1)} copy-done((f32[2048]{0:T(1024)S(1)}, f32[2048]{0:T(1024)}, u32[]{:S(2)}) %copy-start.6) | copy-done | bytes 8216
  29.1 0.7 %copy-done.8 = s32[7,32]{1,0:T(8,128)S(1)} copy-done((s32[7,32]{1,0:T(8,128)S(1)}, s32[7,32]{1,0:T(8,128)}, u32[]{:S(2)}) %copy-start.8) | copy-done | bytes 920
  29.7 1.2 %shard_map.123 = f32[32,128]{1,0:T(8,128)S(1)} custom-call(s32[1]{0:T(128)S(6)} %copy.16.counts_ref, f32[3,8,128]{2,1,0:T(8,128)S(1)} %collective-permute-done.near_ref, f32[3,8,128]{2,1,0:T(8,128)S(1)} %collective-permute-done.2.far_ref, f32[3,16,128]{2,1,0:T(8,128)S(1)} %get-tuple-element.9.own_ref, f32[16,128]{1,0:T(8,128)S(1)} %bitcast.12, ...), custom_call_target="tpu_custom_call" | custom-call | tf_op jit(solution)/shard_map/pallas_call | solution.py:356
  31.0 13.6 %all_to_all.11 = f32[32,1,128]{2,1,0:T(1,128)S(1)} all-to-all(f32[32,1,128]{2,1,0:T(1,128)S(1)} %bitcast.15), channel_id=1, replica_groups=mesh['fine'=8,'coarse'=4] {'fine','coarse'}, dimensions={0} | all-to-all | bytes 32768 | tf_op jit(solution)/shard_map/all_to_all | solution.py:362
  44.5 0.0 collective-permute-done.3.part1_ref
  44.5 0.0 collective-permute-done.5.part3_ref
  44.5 0.0 copy-done.3
  44.6 0.0 copy-done.1
  44.6 5.4 %shard_map.125 = (f32[16,128]{1,0:T(8,128)}, f32[4,64]{1,0:T(4,128)S(1)}) custom-call(s32[1]{0:T(128)S(6)} %copy.16.counts_ref, f32[32,128]{1,0:T(8,128)S(1)} %bitcast.14, f32[3,8,128]{2,1,0:T(8,128)S(1)} %collective-permute-done.near_ref, f32[3,8,128]{2,1,0:T(8,128)S(1)} %collective-permute-done.2.far_ref, f32[3,16,128]{2,1,0:T(8,128)S(1)} %get-tuple-element.9.own_ref, ...), custom_call_target="tpu_custom_call" | custom-call | tf_op jit(solution)/shard_map/pallas_call | solution.py:363
  50.0 0.6 %reshape.33 = f32[256]{0:T(256)} reshape(f32[4,64]{1,0:T(4,128)S(1)} %get-tuple-element.11) | data formatting | bytes 2048 | tf_op jit(solution)/shard_map/reshape | solution.py:370
  (9 shorter events, 0.0 us)
Async XLA Ops:
  0.6 43.9 %copy-start.3 = (bf16[64,2048]{1,0:T(8,128)(2,1)S(1)}, bf16[64,2048]{1,0:T(8,128)(2,1)}, u32[]{:S(2)}) copy-start(bf16[64,2048]{1,0:T(8,128)(2,1)} %smoother_ref.3) | copy-start | bytes 786436
  1.5 0.9 %copy-start.4 = (bf16[7,64,256]{2,1,0:T(8,128)(2,1)S(1)}, bf16[7,64,256]{2,1,0:T(8,128)(2,1)}, u32[]{:S(2)}) copy-start(bf16[7,64,256]{2,1,0:T(8,128)(2,1)} %param.19) | copy-start | bytes 688132
  2.4 0.8 %copy-start.7 = (bf16[64,256]{1,0:T(8,128)(2,1)S(1)}, bf16[64,256]{1,0:T(8,128)(2,1)}, u32[]{:S(2)}) copy-start(bf16[64,256]{1,0:T(8,128)(2,1)} %inverse_ref.1) | copy-start | bytes 98308
  3.8 15.1 %collective-permute-start.4 = (f32[520,256]{1,0:T(8,128)S(1)}, f32[520,256]{1,0:T(8,128)S(1)}, u32[]{:S(2)}, u32[]{:S(2)}) collective-permute-start(f32[520,256]{1,0:T(8,128)S(1)} %shard_map.124.part0_ref), channel_id=1, source_target_pairs={{0,2},{1,3},{2,0},{3,1},{4,6},{5,7},{6,4},{7,5},{8,10},{9,11},{10,... | collective-permute-start | bytes 1597448 | tf_op jit(solution)/shard_map/ppermute | solution.py:352
  6.8 37.7 %collective-permute-start.3 = (f32[520,256]{1,0:T(8,128)S(1)}, f32[520,256]{1,0:T(8,128)S(1)}, u32[]{:S(2)}, u32[]{:S(2)}) collective-permute-start(f32[520,256]{1,0:T(8,128)S(1)} %shard_map.124.part0_ref), channel_id=1, source_target_pairs={{0,1},{1,0},{2,3},{3,2},{4,5},{5,4},{6,7},{7,6},{8,9},{9,8},{10,11... | collective-permute-start | bytes 1597448 | tf_op jit(solution)/shard_map/ppermute | solution.py:354
  18.9 25.6 %collective-permute-start.5 = (f32[520,256]{1,0:T(8,128)S(1)}, f32[520,256]{1,0:T(8,128)S(1)}, u32[]{:S(2)}, u32[]{:S(2)}) collective-permute-start(f32[520,256]{1,0:T(8,128)S(1)} %collective-permute-done.4.part2_ref), channel_id=1, source_target_pairs={{0,1},{1,0},{2,3},{3,2},{4,5},{5,4},{6,7},{7,6},{8,9},{9,8},{10,11... | collective-permute-start | bytes 1597448 | tf_op jit(solution)/shard_map/ppermute | solution.py:354
  18.9 1.0 %copy-start.2 = (bf16[64,2048]{1,0:T(8,128)(2,1)S(1)}, bf16[64,2048]{1,0:T(8,128)(2,1)}, u32[]{:S(2)}) copy-start(bf16[64,2048]{1,0:T(8,128)(2,1)} %smoother_ref.3) | copy-start | bytes 786436
  19.9 0.7 %copy-start.5 = (f32[2048]{0:T(1024)S(1)}, f32[2048]{0:T(1024)}, u32[]{:S(2)}) copy-start(f32[2048]{0:T(1024)} %param.11) | copy-start | bytes 24580
  20.6 0.7 %copy-start.9 = (f32[2048]{0:T(1024)S(1)}, f32[2048]{0:T(1024)}, u32[]{:S(2)}) copy-start(f32[2048]{0:T(1024)} %param.17) | copy-start | bytes 24580
  21.3 0.7 %copy-start.10 = (s32[32]{0:T(128)S(1)}, s32[32]{0:T(128)}, u32[]{:S(2)}) copy-start(s32[32]{0:T(128)} %param.18) | copy-start | bytes 388
  22.3 1.4 %collective-permute-start.1 = (f32[3,8,128]{2,1,0:T(8,128)S(1)}, f32[3,8,128]{2,1,0:T(8,128)S(1)}, u32[]{:S(2)}, u32[]{:S(2)}) collective-permute-start(f32[3,8,128]{2,1,0:T(8,128)S(1)} %get-tuple-element.8), channel_id=1, source_target_pairs={{0,1},{1,0},{2,3},{3,2},{4,5},{5,4},{6,7},{7,6},{8,9},{9,8},{10,11... | collective-permute-start | bytes 36872 | tf_op jit(solution)/shard_map/ppermute | solution.py:342
  22.9 3.2 %collective-permute-start = (f32[3,8,128]{2,1,0:T(8,128)S(1)}, f32[3,8,128]{2,1,0:T(8,128)S(1)}, u32[]{:S(2)}, u32[]{:S(2)}) collective-permute-start(f32[3,8,128]{2,1,0:T(8,128)S(1)} %get-tuple-element.7), channel_id=1, source_target_pairs={{0,1},{1,0},{2,3},{3,2},{4,5},{5,4},{6,7},{7,6},{8,9},{9,8},{10,11... | collective-permute-start | bytes 36872 | tf_op jit(solution)/shard_map/ppermute | solution.py:343
  23.7 3.1 %collective-permute-start.2 = (f32[3,8,128]{2,1,0:T(8,128)S(1)}, f32[3,8,128]{2,1,0:T(8,128)S(1)}, u32[]{:S(2)}, u32[]{:S(2)}) collective-permute-start(f32[3,8,128]{2,1,0:T(8,128)S(1)} %collective-permute-done.1), channel_id=1, source_target_pairs={{0,2},{1,0},{2,4},{3,1},{4,6},{5,3},{6,8},{7,5},{8,10},{9,7},{10,1... | collective-permute-start | bytes 36872 | tf_op jit(solution)/shard_map/ppermute | solution.py:342
  26.9 1.5 %copy-start = (bf16[7,64,2048]{2,1,0:T(8,128)(2,1)S(1)}, bf16[7,64,2048]{2,1,0:T(8,128)(2,1)}, u32[]{:S(2)}) copy-start(bf16[7,64,2048]{2,1,0:T(8,128)(2,1)} %fine_ref.3) | copy-start | bytes 5505028
  28.4 0.7 %copy-start.6 = (f32[2048]{0:T(1024)S(1)}, f32[2048]{0:T(1024)}, u32[]{:S(2)}) copy-start(f32[2048]{0:T(1024)} %param.15) | copy-start | bytes 24580
  29.0 0.7 %copy-start.8 = (s32[7,32]{1,0:T(8,128)S(1)}, s32[7,32]{1,0:T(8,128)}, u32[]{:S(2)}) copy-start(s32[7,32]{1,0:T(8,128)} %columns_ref.3) | copy-start | bytes 2692
  29.7 14.8 %copy-start.1 = (bf16[7,64,2048]{2,1,0:T(8,128)(2,1)S(1)}, bf16[7,64,2048]{2,1,0:T(8,128)(2,1)}, u32[]{:S(2)}) copy-start(bf16[7,64,2048]{2,1,0:T(8,128)(2,1)} %fine_ref.3) | copy-start | bytes 5505028

commit v2 on v1

--- a/solution.py
+++ b/solution.py
@@ -50,27 +50,32 @@
     return cell_sums(high_ref, low_ref)
 
 
-def apply_fine(window, fine_ref, columns_ref, picked_ref, high_ref, low_ref):
+def selection(columns, half_rows, pairs):
+    nbrs, aggs = columns.shape
+    at, who = iota((pairs, aggs), 1), iota((pairs, aggs), 0)
+    entry = iota((pairs, 4 * half_rows), 1) % (2 * half_rows)
+    parts = []
+    for half in range(2):
+        for k in range(nbrs):
+            chosen = jnp.where(at == 2 * who + half, columns[k : k + 1].astype(f32), 0.0)
+            block = jnp.sum(chosen, axis=1, keepdims=True).astype(i32)
+            place = block // 2 + jnp.where(block % 2 == half, 0, half_rows)
+            parts.append((entry == place).astype(bf16))
+    return jnp.concatenate(parts, axis=0)
+
+
+def pick(window, selected):
+    high, low = split(jnp.concatenate([window, pltpu.roll(window, CELLS, 1)], axis=0))
+    picked = dot(selected, jnp.concatenate([high, low], axis=0))
+    count = selected.shape[0] // 2
+    lane = iota((count, LANES), 1)
+    return jnp.where(lane < CELLS, picked[:count], picked[count:])
+
+
+def apply_fine(window, fine_ref, selected, picked_ref, high_ref, low_ref):
     nbrs, _, width = fine_ref.shape
     pairs = width // LANES
-    rows = window.shape[0]
-    both = jnp.concatenate([window, pltpu.roll(window, CELLS, 1)], axis=0)
-    high, low = split(both)
-    table = jnp.concatenate([high, low], axis=0)
-    aggs = columns_ref.shape[1]
-    at, who = iota((pairs, aggs), 1), iota((pairs, aggs), 0)
-    entry = iota((pairs, 4 * rows), 1) % (2 * rows)
-    halves = []
-    for half in range(2):
-        parts = []
-        for k in range(nbrs):
-            chosen = jnp.where(at == 2 * who + half, columns_ref[k : k + 1, :].astype(f32), 0.0)
-            block = jnp.sum(chosen, axis=1, keepdims=True).astype(i32)
-            place = block // 2 + jnp.where(block % 2 == half, 0, rows)
-            parts.append((entry == place).astype(bf16))
-        halves.append(dot(jnp.concatenate(parts, axis=0), table))
-    lane = iota(halves[0].shape, 1)
-    picked_ref[...] = jnp.where(lane < CELLS, halves[0], halves[1])
+    picked_ref[...] = pick(window, selected)
     for p in range(pairs):
         cols = pl.ds(p * LANES, LANES)
         total = None
@@ -94,7 +99,22 @@
     return jnp.where(iota(shape, 1) < CELLS, columns[0], columns[1])
 
 
-def start_kernel(rhs_ref, weights_ref, order_ref, smoother_ref, near_ref, onward_ref, own_ref, high_ref, low_ref):
+def fetch(sem_ref, *pairs):
+    copies = [pltpu.make_async_copy(src, dst, sem_ref.at[i]) for i, (src, dst) in enumerate(pairs)]
+    for copy in copies:
+        copy.start()
+    return copies
+
+
+def start_kernel(
+    rhs_any, weights_any, order_any, smoother_any, near_ref, onward_ref, own_ref,
+    rhs_ref, weights_ref, order_ref, smoother_ref, high_ref, low_ref, sem_ref,
+):
+    copies = fetch(
+        sem_ref, (smoother_any, smoother_ref), (rhs_any, rhs_ref), (weights_any, weights_ref), (order_any, order_ref)
+    )
+    for copy in copies:
+        copy.wait()
     pairs = rhs_ref.shape[0]
     smoothed = apply_smoother(rhs_ref[...], smoother_ref, high_ref, low_ref)
     order = by_half(as_columns(order_ref[...].astype(f32), pairs), (pairs, LANES))
@@ -118,21 +138,60 @@
     return lax.axis_index("fine") * lax.axis_size("coarse") + lax.axis_index("coarse")
 
 
-def reaction_of(reaction_ref, counts_ref):
-    shape = reaction_ref.shape
-    agg = 2 * iota(shape, 0) + iota(shape, 1) // CELLS
-    return jnp.where(agg < counts_ref[0], reaction_ref[...], 0.0)
+def prepare_kernel(
+    counts_ref, own_ref, rhs_any, reaction_any, columns_any, fine_any, selected_ref, weighed_ref, local_ref,
+    rhs_ref, reaction_ref, columns_ref, fine_ref, wide_ref, sem_ref,
+):
+    copies = fetch(
+        sem_ref, (fine_any, fine_ref), (columns_any, columns_ref), (rhs_any, rhs_ref), (reaction_any, reaction_ref)
+    )
+    for copy in copies[1:]:
+        copy.wait()
+    pairs = rhs_ref.shape[0]
+    nbrs, _, width = fine_ref.shape
+    weights = own_ref[1]
+    agg = 2 * iota((pairs, LANES), 0) + iota((pairs, LANES), 1) // CELLS
+    reaction = jnp.where(agg < counts_ref[0], reaction_ref[...], 0.0)
+    local_ref[0] = weights * rhs_ref[...]
+    local_ref[1] = weights * reaction
+    local_ref[2] = rhs_ref[...]
+    local_ref[3] = reaction
+    selected_ref[...] = selection(columns_ref[...], pairs + 2 * HALO_ROWS, pairs)
+    by_agg = jnp.concatenate([weights[:, :CELLS], weights[:, CELLS:]], axis=0)
+    row, lane = iota((2 * pairs, width), 0), iota((2 * pairs, width), 1)
+    member = (lane // CELLS == 2 * (row % pairs) + row // pairs).astype(bf16)
+    wide = None
+    for part in split(by_agg):
+        term = lax.dot_general(part, member, (((0,), (0,)), ((), ())), preferred_element_type=f32)
+        wide = term if wide is None else wide + term
+    wide_ref[...] = wide
+    copies[0].wait()
+    for p in range(pairs):
+        cols = pl.ds(p * LANES, LANES)
+        scale = wide_ref[:, cols]
+        for k in range(nbrs):
+            term = fine_ref[k, :, cols].astype(f32) * scale
+            total = term[:8]
+            for r in range(8, CELLS, 8):
+                total = total + term[r : r + 8]
+            weighed_ref[k * pairs + p] = total
 
 
 def residual_kernel(
-    devices, counts_ref, near_ref, far_ref, own_ref, rhs_ref, reaction_ref, columns_ref, fine_ref,
-    out_ref, picked_ref, high_ref, low_ref,
+    devices, near_ref, far_ref, own_ref, selected_ref, weighed_ref, local_ref, out_ref, picked_ref,
 ):
     smoothed, _, _ = window_of(near_ref, far_ref, own_ref, device_index(), devices)
-    image = apply_fine(smoothed, fine_ref, columns_ref, picked_ref, high_ref, low_ref)
-    image = image + reaction_of(reaction_ref, counts_ref) * own_ref[0]
-    weighted = own_ref[1] * (rhs_ref[...] - image)
-    pairs = weighted.shape[0]
+    picked_ref[...] = pick(smoothed, selected_ref[...])
+    pairs = own_ref.shape[1]
+    nbrs = picked_ref.shape[0] // pairs
+    images = []
+    for p in range(pairs):
+        total = None
+        for k in range(nbrs):
+            term = weighed_ref[k * pairs + p] * picked_ref[pl.ds(k * pairs + p, 1), :]
+            total = term if total is None else total + term
+        images.append(jnp.sum(total, axis=0, keepdims=True))
+    weighted = local_ref[0] - local_ref[1] * own_ref[0] - jnp.concatenate(images, axis=0)
     shape = (pairs, LANES)
     lane, who = iota(shape, 1), iota(shape, 0)
     row = jnp.zeros((1, LANES), f32)
@@ -146,37 +205,41 @@
     out_ref[...] = jnp.broadcast_to(row, out_ref.shape)
 
 
-def finish(corr, own_ref, window, rhs_ref, reaction_ref, counts_ref, columns_ref, fine_ref, smoother_ref,
-           out_ref, picked_ref, high_ref, low_ref):
-    smoothed, weights, _ = window
+def finish(corr, near_ref, far_ref, own_ref, local_ref, devices, selected_ref, fine_ref, smoother_ref, result_ref,
+           picked_ref, high_ref, low_ref):
+    smoothed, weights, _ = window_of(near_ref, far_ref, own_ref, device_index(), devices)
     corrected = smoothed + weights * corr
-    pairs = rhs_ref.shape[0]
+    pairs = own_ref.shape[1]
     mine = corrected[HALO_ROWS : HALO_ROWS + pairs]
-    image = apply_fine(corrected, fine_ref, columns_ref, picked_ref, high_ref, low_ref)
-    image = image + reaction_of(reaction_ref, counts_ref) * mine
-    out_ref[...] = mine + apply_smoother(rhs_ref[...] - image, smoother_ref, high_ref, low_ref)
-
-
-def pack_kernel(rows_ref, values_ref, inverse_ref, out_ref):
-    nbrs, own_blocks = rows_ref.shape
-    deep = values_ref.shape[0]
+    image = apply_fine(corrected, fine_ref, selected_ref[...], picked_ref, high_ref, low_ref)
+    image = image + local_ref[3] * mine
+    result_ref[...] = mine + apply_smoother(local_ref[2] - image, smoother_ref, high_ref, low_ref)
+
+
+def pack_kernel(rows_any, values_any, inverse_any, out_ref, rows_ref, values_ref, inverse_ref, sem_ref):
+    copies = fetch(sem_ref, (values_any, values_ref), (inverse_any, inverse_ref), (rows_any, rows_ref))
+    for copy in copies:
+        copy.wait()
+    own_blocks, nbrs = rows_ref.shape
+    deep, width = values_ref.shape
     out_ref[pl.ds(0, deep), :] = values_ref[...].astype(f32)
     out_ref[pl.ds(deep, CELLS), :] = inverse_ref[...].astype(f32)
-    shape = (8, out_ref.shape[1])
-    lane = iota(shape, 1)
-    rows = jnp.zeros(shape, f32)
+    lane, block = iota((own_blocks, width), 1), iota((own_blocks, width), 0)
+    rows = jnp.zeros((own_blocks, width), f32)
     for k in range(nbrs):
-        for j in range(own_blocks):
-            here = (lane // 32 == k) & (lane % 16 == j)
-            rows = jnp.where(here, rows_ref[k, j].astype(f32), rows)
-    out_ref[pl.ds(deep + CELLS, 8), :] = rows
+        here = (lane // 32 == k) & (lane % 16 == block)
+        rows = jnp.where(here, rows_ref[:, k : k + 1].astype(f32), rows)
+    out_ref[pl.ds(deep + CELLS, 8), :] = jnp.broadcast_to(jnp.sum(rows, axis=0, keepdims=True), (8, width))
 
 
 def solve_kernel(
-    devices, counts_ref, gathered_ref, near_ref, far_ref, own_ref, rhs_ref, reaction_ref, columns_ref, fine_ref,
-    smoother_ref, part0_ref, part1_ref, part2_ref, part3_ref,
-    out_ref, correction_ref, blocks_ref, inverse_ref, picked_ref, high_ref, low_ref,
+    devices, gathered_ref, near_ref, far_ref, own_ref, selected_ref, local_ref,
+    part0_ref, part1_ref, part2_ref, part3_ref, fine_any, smoother_any,
+    out_any, correction_any,
+    blocks_ref, inverse_ref, result_ref, correction_ref,
+    fine_ref, smoother_ref, picked_ref, high_ref, low_ref, sem_ref, out_sem_ref,
 ):
+    copies = fetch(sem_ref, (fine_any, fine_ref), (smoother_any, smoother_ref))
     part_refs = (part0_ref, part1_ref, part2_ref, part3_ref)
     me = lax.axis_index("coarse")
     parts = len(part_refs)
@@ -249,40 +312,58 @@
         stacked = jnp.concatenate([p for pair in zip(high, low) for p in pair], axis=0)
         image = dot(scatter, stacked)
         correction = correction + product(right_side - image, inverse_ref)
-    correction_ref[...] = correction[:own_blocks]
-
-    window = window_of(near_ref, far_ref, own_ref, device_index(), devices)
-    order = window[2].astype(i32)
+    for r in range(own_blocks // 2):
+        both = [correction[2 * r : 2 * r + 1], correction[2 * r + 1 : 2 * r + 2]]
+        correction_ref[r : r + 1, :] = jnp.concatenate(both, axis=1)
+    correction_copy = pltpu.make_async_copy(correction_ref, correction_any, out_sem_ref.at[0])
+    correction_copy.start()
+
+    order = window_of(near_ref, far_ref, own_ref, device_index(), devices)[2].astype(i32)
     rows = order.shape[0]
     unit = jnp.concatenate([order[:, :CELLS], order[:, CELLS:]], axis=0)
-    pick = (iota(unit.shape, 1) == unit % CELLS).astype(bf16)
-    values = dot_t(pick, jnp.concatenate(split(correction), axis=0))
+    chosen = (iota(unit.shape, 1) == unit % CELLS).astype(bf16)
+    values = dot_t(chosen, jnp.concatenate(split(correction), axis=0))
     group = place(unit[:, : 2 * groups] // CELLS)
     values = jnp.sum(jnp.where(iota(values.shape, 1) % groups == group, values, 0.0), axis=1, keepdims=True)
     corr = by_half([values[:rows], values[rows:]], (rows, LANES))
-    finish(corr, own_ref, window, rhs_ref, reaction_ref, counts_ref, columns_ref, fine_ref, smoother_ref,
-           out_ref, picked_ref, high_ref, low_ref)
+    for copy in copies:
+        copy.wait()
+    finish(corr, near_ref, far_ref, own_ref, local_ref, devices, selected_ref, fine_ref, smoother_ref, result_ref,
+           picked_ref, high_ref, low_ref)
+    result_copy = pltpu.make_async_copy(result_ref, out_any, out_sem_ref.at[1])
+    result_copy.start()
+    correction_copy.wait()
+    result_copy.wait()
 
 
 def finish_kernel(
-    devices, counts_ref, corr_ref, near_ref, far_ref, own_ref, rhs_ref, reaction_ref, columns_ref, fine_ref,
-    smoother_ref, out_ref, picked_ref, high_ref, low_ref,
+    devices, corr_ref, near_ref, far_ref, own_ref, selected_ref, local_ref, fine_any, smoother_any, result_ref,
+    fine_ref, smoother_ref, picked_ref, high_ref, low_ref, sem_ref,
 ):
-    window = window_of(near_ref, far_ref, own_ref, device_index(), devices)
-    finish(corr_ref[...], own_ref, window, rhs_ref, reaction_ref, counts_ref, columns_ref, fine_ref, smoother_ref,
-           out_ref, picked_ref, high_ref, low_ref)
-
-
-def call(kernel, out_shape, smem=(), scratch=(), count=0):
-    specs = [pl.BlockSpec(memory_space=pltpu.SMEM if i in smem else pltpu.VMEM) for i in range(count)]
-    return pl.pallas_call(
+    copies = fetch(sem_ref, (fine_any, fine_ref), (smoother_any, smoother_ref))
+    for copy in copies:
+        copy.wait()
+    finish(corr_ref[...], near_ref, far_ref, own_ref, local_ref, devices, selected_ref, fine_ref, smoother_ref,
+           result_ref, picked_ref, high_ref, low_ref)
+
+
+def call(kernel, out_shape, ins, outs=None, scratch=()):
+    spaces = dict(s=pltpu.SMEM, v=pltpu.VMEM, a=pl.ANY)
+    many = isinstance(out_shape, tuple)
+    specs = tuple(pl.BlockSpec(memory_space=spaces[c]) for c in outs or "v" * (len(out_shape) if many else 1))
+    run = pl.pallas_call(
         kernel,
         out_shape=out_shape,
-        in_specs=specs,
-        out_specs=jax.tree.map(lambda _: pl.BlockSpec(memory_space=pltpu.VMEM), out_shape),
+        in_specs=[pl.BlockSpec(memory_space=spaces[c]) for c in ins],
+        out_specs=specs if many else specs[0],
         scratch_shapes=list(scratch),
         compiler_params=pltpu.CompilerParams(vmem_limit_bytes=VMEM_LIMIT),
     )
+
+    def placed(*operands):
+        return run(*(pltpu.with_memory_space_constraint(x, pltpu.HBM) if c == "a" else x for x, c in zip(operands, ins)))
+
+    return placed
 
 
 def shape_of(*dims):
@@ -326,12 +407,17 @@
     parts = lax.axis_size("coarse")
     rhs, reaction, weights = (x.reshape(pairs, LANES) for x in (rhs, reaction, weights))
     rows = pairs + 2 * HALO_ROWS
+    vector = pltpu.VMEM((pairs, LANES), f32)
+    fine_buffer = pltpu.VMEM(fine_values.shape, bf16)
+    smoother_buffer = pltpu.VMEM(smoother.shape, bf16)
     products = [pltpu.VMEM((CELLS, cells), bf16)] * 2
-    scratch = [pltpu.VMEM((nbrs * pairs, LANES), f32)] + products
+    picked = pltpu.VMEM((nbrs * pairs, LANES), f32)
+    copies = pltpu.SemaphoreType.DMA((4,))
     edge = shape_of(3, HALO_ROWS, LANES)
 
     near, onward, own = call(
-        start_kernel, (edge, edge, shape_of(3, pairs, LANES)), scratch=products, count=4
+        start_kernel, (edge, edge, shape_of(3, pairs, LANES)), "aaaa",
+        scratch=[vector, vector, pltpu.VMEM((1, aggs), i32), smoother_buffer, *products, copies],
     )(rhs, weights, coarse_order.reshape(1, aggs), smoother)
 
     partner = [(d, d ^ 1) for d in range(devices)]
@@ -339,34 +425,53 @@
     for d in range(devices):
         target = d + 2 if d % 2 == 0 else d - 2
         chain.append((d, target if 0 <= target < devices else d ^ 1))
-    far = lax.ppermute(lax.ppermute(onward, BOTH, partner), BOTH, chain)
+    onward = lax.ppermute(onward, BOTH, partner)
     near = lax.ppermute(near, BOTH, partner)
+    far = lax.ppermute(onward, BOTH, chain)
 
     copied = parts == 4 and devices % 32 == 0 and devices <= 64
     if copied:
         deep = coarse_values.shape[0] * CELLS
         width = coarse_inverse.shape[1]
-        packed = call(pack_kernel, shape_of(deep + CELLS + 8, width), smem=(0,), count=3)(
-            coarse_rows, coarse_values.reshape(deep, width), coarse_inverse
+        coarse_values, _ = lax.optimization_barrier((coarse_values, own))
+        packed = call(pack_kernel, shape_of(deep + CELLS + 8, width), "aaa", scratch=[
+            pltpu.VMEM(coarse_rows.shape[::-1], i32), pltpu.VMEM((deep, width), bf16),
+            pltpu.VMEM(coarse_inverse.shape, bf16), copies,
+        ])(
+            coarse_rows.T, coarse_values.reshape(deep, width), coarse_inverse
         )
         other = lax.ppermute(packed, "coarse", [(c, c ^ 2) for c in range(parts)])
         swap = [(c, c ^ 1) for c in range(parts)]
-        pieces = (packed, lax.ppermute(packed, "coarse", swap), other, lax.ppermute(other, "coarse", swap))
+        beside = lax.ppermute(packed, "coarse", swap)
+
+    selected, weighed, local = call(
+        prepare_kernel,
+        (jax.ShapeDtypeStruct((aggs * nbrs, 4 * rows), bf16), shape_of(nbrs * pairs, 8, LANES), shape_of(4, pairs, LANES)),
+        "svaaaa",
+        scratch=[vector, vector, pltpu.VMEM(fine_columns.shape, i32), fine_buffer, pltpu.VMEM((CELLS, cells), f32), copies],
+    )(pit_counts, own, rhs, reaction, fine_columns, fine_values)
 
     sent = call(
-        functools.partial(residual_kernel, devices), shape_of(devices, LANES), smem=(0,), scratch=scratch, count=8
-    )(pit_counts, near, far, own, rhs, reaction, fine_columns, fine_values)
-
-    common = (near, far, own, rhs, reaction, fine_columns, fine_values, smoother)
+        functools.partial(residual_kernel, devices), shape_of(devices, LANES), "vvvvvv", scratch=[picked]
+    )(near, far, own, selected, weighed, local)
+
+    finish_scratch = [ fine_buffer, smoother_buffer, picked, *products, copies]
+    common = (near, far, own, selected, local)
+    fetched = (fine_values, smoother)
     if copied:
         gathered = lax.all_to_all(sent, BOTH, 0, 0, tiled=True)
+        other, gathered = lax.optimization_barrier((other, gathered))
+        pieces = (packed, beside, other, lax.ppermute(other, "coarse", swap))
         result, correction = call(
             functools.partial(solve_kernel, devices),
-            (shape_of(pairs, LANES), shape_of(width // CELLS, CELLS)),
-            smem=(0,),
-            scratch=[pltpu.VMEM((parts, deep, width), bf16), pltpu.VMEM((parts, CELLS, width), bf16)] + scratch,
-            count=14,
-        )(pit_counts, gathered, *common, *pieces)
+            (shape_of(pairs, LANES), shape_of(width // LANES, LANES)),
+            "vvvvvvvvvvaa",
+            outs="aa",
+            scratch=[
+                pltpu.VMEM((parts, deep, width), bf16), pltpu.VMEM((parts, CELLS, width), bf16),
+                vector, pltpu.VMEM((width // LANES, LANES), f32), *finish_scratch, pltpu.SemaphoreType.DMA((2,)),
+            ],
+        )(gathered, *common, *pieces, *fetched)
         correction = correction.reshape(-1)
     else:
         correction, everywhere = coarse_by_parts(
@@ -378,8 +483,8 @@
         order = jnp.concatenate([low, own[2], high], axis=0).astype(i32)
         corr = jnp.repeat(everywhere[order[:, ::CELLS]], CELLS, axis=1)
         result = call(
-            functools.partial(finish_kernel, devices), shape_of(pairs, LANES), smem=(0,), scratch=scratch, count=10
-        )(pit_counts, corr, *common)
+            functools.partial(finish_kernel, devices), shape_of(pairs, LANES), "vvvvvvaa", scratch=finish_scratch
+        )(corr, *common, *fetched)
     return result.reshape(-1), correction
 
 

time: 51.1 us -> 40.2 us (0.79)
  blocking collectives: 13.6 us -> 0 us
  local copies, waits for them, and re-layouts: 9.04 us -> 0 us
  starting transfers between devices: 5.38 us -> 10.6 us
  waiting for transfers between devices: 13.6 us -> 17 us
  Pallas kernels: 7.7 us -> 11 us
    all_to_all x1 -> x0, blocking collectives: 13.6 us -> none  [shards(): gathered = lax.all_to_all(sent, BOTH, 0, 0, tiled=True)]
    ppermute x1, waiting for transfers between devices: 12.1 us -> 0.01 us  [shards(): other = lax.ppermute(packed, 'coarse', [(c, c ^ 2) for c in range(parts)])]
    ppermute x4, waiting for transfers between devices: 1.51 us -> 10.2 us  [the longest x1 7.61 us: shards(): far = lax.ppermute(onward, BOTH, chain)]
    unnamed x23 -> x0, local copies, waits for them, and re-layouts: 8.39 us -> none
    all_to_all x0 -> x1, waiting for transfers between devices: none -> 6.83 us  [shards(): gathered = lax.all_to_all(sent, BOTH, 0, 0, tiled=True)]
    all_to_all x0 -> x1, starting transfers between devices: none -> 6.68 us  [shards(): gathered = lax.all_to_all(sent, BOTH, 0, 0, tiled=True)]
    pallas_call x4 -> x5, Pallas kernels: 7.7 us -> 11 us  [placed(): run(*(pltpu.with_memory_space_constraint(x, pltpu.HBM) if c == 'a' else x...]
    ppermute x4, starting transfers between devices: 2.27 us -> 0.4 us  [the longest x1 0.32 us: shards(): beside = lax.ppermute(packed, 'coarse', swap)]
  transfers between devices with their start and end apart: 6 -> 7, of which waited for: 3 -> 4; matrix products, arithmetic and copies ran while one was open for 0% -> 0% of each run, Pallas kernels for 3% -> 8%
where the time goes in v2:
time: 40.2 us; the launch traced here: 40 us
  waiting for transfers between devices  17 us (42%)
  Pallas kernels  11 us (27%)
  starting transfers between devices  10.6 us (26%)
  between operations  1.33 us (3%)
    pallas_call x5, Pallas kernels, placed(): run(*(pltpu.with_memory_space_constraint(x, pltpu.HBM) if c == 'a' else x...  11 us
    ppermute x1, waiting for transfers between devices, shards(): far = lax.ppermute(onward, BOTH, chain)  7.61 us
    all_to_all x1, waiting for transfers between devices, shards(): gathered = lax.all_to_all(sent, BOTH, 0, 0, tiled=True)  6.83 us
    all_to_all x1, starting transfers between devices, shards(): gathered = lax.all_to_all(sent, BOTH, 0, 0, tiled=True)  6.68 us
    ppermute x1, starting transfers between devices, shards(): other = lax.ppermute(packed, 'coarse', [(c, c ^ 2) for c in range(parts)])  3.03 us
    ppermute x1, waiting for transfers between devices, shards(): pieces = (packed, beside, other, lax.ppermute(other, 'coarse', swap))  1.91 us
  transfers between devices with their start and end apart: 7, of which 4 were waited for; matrix products, arithmetic and copies ran while one was open for 0% of the time, Pallas kernels for 8%

profile of v2, /device:TPU:0, one launch (start us, length us, event | category | flops | bytes accessed | tf_op | source)
XLA Modules:
  0.0 40.0 jit_solution(3108074821036328307)
XLA Ops:
  0.6 1.4 %shard_map.122 = (f32[3,8,128]{2,1,0:T(8,128)S(1)}, f32[3,8,128]{2,1,0:T(8,128)S(1)}, f32[3,16,128]{2,1,0:T(8,128)S(1)}) custom-call(f32[16,128]{1,0:T(8,128)} %bitcast.14, f32[16,128]{1,0:T(8,128)} %bitcast.17, s32[1,32]{1,0:T(1,128)} %bitcast.19, bf16[64,2048]{1,0:T(8,128)(2,1)} %smoother_any.3), custom_call_target="tpu_custom_call" | custom-call | tf_op jit(solution)/shard_map/pallas_call | solution.py:364
  2.0 1.1 %shard_map.123.part0_ref = f32[520,256]{1,0:T(8,128)S(1)} custom-call(s32[4,7]{1,0:T(4,128)} %bitcast.18, bf16[448,256]{1,0:T(8,128)(2,1)} %bitcast.13, bf16[64,256]{1,0:T(8,128)(2,1)} %inverse_any.1), custom_call_target="tpu_custom_call" | custom-call | tf_op jit(solution)/shard_map/pallas_call | solution.py:364
  3.1 3.0 %collective-permute-start = (f32[520,256]{1,0:T(8,128)S(1)}, f32[520,256]{1,0:T(8,128)S(1)}, u32[]{:S(2)}, u32[]{:S(2)}) collective-permute-start(f32[520,256]{1,0:T(8,128)S(1)} %shard_map.123.part0_ref), channel_id=1, source_target_pairs={{0,2},{1,3},{2,0},{3,1},{4,6},{5,7},{6,4},{7,5},{8,10},{9,11},{10,... | collective-permute-start | bytes 1597448 | tf_op jit(solution)/shard_map/ppermute | solution.py:443
  6.2 0.0 collective-permute-start.2
  6.2 0.5 %collective-permute-start.1 = (f32[3,8,128]{2,1,0:T(8,128)S(1)}, f32[3,8,128]{2,1,0:T(8,128)S(1)}, u32[]{:S(2)}, u32[]{:S(2)}) collective-permute-start(f32[3,8,128]{2,1,0:T(8,128)S(1)} %get-tuple-element.15), channel_id=1, source_target_pairs={{0,1},{1,0},{2,3},{3,2},{4,5},{5,4},{6,7},{7,6},{8,9},{9,8},{10,11... | collective-permute-start | bytes 36872 | tf_op jit(solution)/shard_map/ppermute | solution.py:429
  6.7 0.7 %collective-permute-done.2 = f32[3,8,128]{2,1,0:T(8,128)S(1)} collective-permute-done((f32[3,8,128]{2,1,0:T(8,128)S(1)}, f32[3,8,128]{2,1,0:T(8,128)S(1)}, u32[]{:S(2)}, u32[]{:S(2)}) %collective-permute-start.2) | collective-permute-done | bytes 12320 | tf_op jit(solution)/shard_map/ppermute | solution.py:428
  7.4 0.1 collective-permute-start.3
  8.1 2.1 %shard_map.124 = (bf16[224,128]{1,0:T(8,128)(2,1)S(1)}, f32[112,8,128]{2,1,0:T(8,128)S(1)}, f32[4,16,128]{2,1,0:T(8,128)S(1)}) custom-call(s32[1]{0:T(128)S(6)} %copy.14.counts_ref, f32[3,16,128]{2,1,0:T(8,128)S(1)} %get-tuple-element.13.own_ref, f32[16,128]{1,0:T(8,128)} %bitcast.15, f32[16,128]{1,0:T(8,128)} %bitcast.16, s32[7,32]{1,0:T(8,128)} %columns_any.1, ...), custom_call_target="tpu_custom_call" | custom-call | tf_op jit(solution)/shard_map/pallas_call | solution.py:364
  10.2 0.0 collective-permute-done.1.near_ref
  10.2 7.6 %collective-permute-done.3.far_ref = f32[3,8,128]{2,1,0:T(8,128)S(1)} collective-permute-done((f32[3,8,128]{2,1,0:T(8,128)S(1)}, f32[3,8,128]{2,1,0:T(8,128)S(1)}, u32[]{:S(2)}, u32[]{:S(2)}) %collective-permute-start.3) | collective-permute-done | bytes 12320 | tf_op jit(solution)/shard_map/ppermute | solution.py:430
  17.8 1.0 %shard_map.125 = f32[32,128]{1,0:T(8,128)} custom-call(f32[3,8,128]{2,1,0:T(8,128)S(1)} %collective-permute-done.1.near_ref, f32[3,8,128]{2,1,0:T(8,128)S(1)} %collective-permute-done.3.far_ref, f32[3,16,128]{2,1,0:T(8,128)S(1)} %get-tuple-element.13.own_ref, bf16[224,128]{1,0:T(8,128)(2,1)S(1)} %get-tuple-element.17.selected_ref, ...), custom_call_target="tpu_custom_call" | custom-call | tf_op jit(solution)/shard_map/pallas_call | solution.py:364
  18.8 6.7 %all-to-all-start = ((f32[32,1,128]{2,1,0:T(1,128)}), f32[32,1,128]{2,1,0:T(1,128)S(1)}, u32[]{:S(2)}, u32[]{:S(2)}) async-start(f32[32,1,128]{2,1,0:T(1,128)} %bitcast.7), calls=%async_computation | async-start | bytes 32768 | tf_op jit(solution)/shard_map/all_to_all | solution.py:462
  25.5 0.3 collective-permute-start.4
  25.8 6.8 %all-to-all-done = f32[32,1,128]{2,1,0:T(1,128)S(1)} async-done(((f32[32,1,128]{2,1,0:T(1,128)}), f32[32,1,128]{2,1,0:T(1,128)S(1)}, u32[]{:S(2)}, u32[]{:S(2)}) %all-to-all-start) | async-done | bytes 16416 | tf_op jit(solution)/shard_map/all_to_all | solution.py:462
  32.6 0.0 collective-permute-done.part2_ref
  32.6 0.0 collective-permute-start.5
  32.6 0.0 collective-permute-done.4.part1_ref
  32.6 1.9 %collective-permute-done.5.part3_ref = f32[520,256]{1,0:T(8,128)S(1)} collective-permute-done((f32[520,256]{1,0:T(8,128)S(1)}, f32[520,256]{1,0:T(8,128)S(1)}, u32[]{:S(2)}, u32[]{:S(2)}) %collective-permute-start.5) | collective-permute-done | bytes 532512 | tf_op jit(solution)/shard_map/ppermute | solution.py:464
  34.5 5.5 %shard_map.126 = (f32[16,128]{1,0:T(8,128)}, f32[2,128]{1,0:T(2,128)}) custom-call(f32[32,128]{1,0:T(8,128)S(1)} %bitcast.12, f32[3,8,128]{2,1,0:T(8,128)S(1)} %collective-permute-done.1.near_ref, f32[3,8,128]{2,1,0:T(8,128)S(1)} %collective-permute-done.3.far_ref, f32[3,16,128]{2,1,0:T(8,128)S(1)} %get-tuple-element.13.own_ref, ...), custom_call_target="tpu_custom_call" | custom-call | tf_op jit(solution)/shard_map/pallas_call | solution.py:364
Async XLA Ops:
  3.1 29.5 %collective-permute-start = (f32[520,256]{1,0:T(8,128)S(1)}, f32[520,256]{1,0:T(8,128)S(1)}, u32[]{:S(2)}, u32[]{:S(2)}) collective-permute-start(f32[520,256]{1,0:T(8,128)S(1)} %shard_map.123.part0_ref), channel_id=1, source_target_pairs={{0,2},{1,3},{2,0},{3,1},{4,6},{5,7},{6,4},{7,5},{8,10},{9,11},{10,... | collective-permute-start | bytes 1597448 | tf_op jit(solution)/shard_map/ppermute | solution.py:443
  6.2 1.2 %collective-permute-start.2 = (f32[3,8,128]{2,1,0:T(8,128)S(1)}, f32[3,8,128]{2,1,0:T(8,128)S(1)}, u32[]{:S(2)}, u32[]{:S(2)}) collective-permute-start(f32[3,8,128]{2,1,0:T(8,128)S(1)} %get-tuple-element.16), channel_id=1, source_target_pairs={{0,1},{1,0},{2,3},{3,2},{4,5},{5,4},{6,7},{7,6},{8,9},{9,8},{10,11... | collective-permute-start | bytes 36872 | tf_op jit(solution)/shard_map/ppermute | solution.py:428
  6.2 4.0 %collective-permute-start.1 = (f32[3,8,128]{2,1,0:T(8,128)S(1)}, f32[3,8,128]{2,1,0:T(8,128)S(1)}, u32[]{:S(2)}, u32[]{:S(2)}) collective-permute-start(f32[3,8,128]{2,1,0:T(8,128)S(1)} %get-tuple-element.15), channel_id=1, source_target_pairs={{0,1},{1,0},{2,3},{3,2},{4,5},{5,4},{6,7},{7,6},{8,9},{9,8},{10,11... | collective-permute-start | bytes 36872 | tf_op jit(solution)/shard_map/ppermute | solution.py:429
  7.4 10.4 %collective-permute-start.3 = (f32[3,8,128]{2,1,0:T(8,128)S(1)}, f32[3,8,128]{2,1,0:T(8,128)S(1)}, u32[]{:S(2)}, u32[]{:S(2)}) collective-permute-start(f32[3,8,128]{2,1,0:T(8,128)S(1)} %collective-permute-done.2), channel_id=1, source_target_pairs={{0,2},{1,0},{2,4},{3,1},{4,6},{5,3},{6,8},{7,5},{8,10},{9,7},{10,1... | collective-permute-start | bytes 36872 | tf_op jit(solution)/shard_map/ppermute | solution.py:430
  18.8 13.8 %all-to-all-start = ((f32[32,1,128]{2,1,0:T(1,128)}), f32[32,1,128]{2,1,0:T(1,128)S(1)}, u32[]{:S(2)}, u32[]{:S(2)}) async-start(f32[32,1,128]{2,1,0:T(1,128)} %bitcast.7), calls=%async_computation | async-start | bytes 32768 | tf_op jit(solution)/shard_map/all_to_all | solution.py:462
  25.5 7.2 %collective-permute-start.4 = (f32[520,256]{1,0:T(8,128)S(1)}, f32[520,256]{1,0:T(8,128)S(1)}, u32[]{:S(2)}, u32[]{:S(2)}) collective-permute-start(f32[520,256]{1,0:T(8,128)S(1)} %shard_map.123.part0_ref), channel_id=1, source_target_pairs={{0,1},{1,0},{2,3},{3,2},{4,5},{5,4},{6,7},{7,6},{8,9},{9,8},{10,11... | collective-permute-start | bytes 1597448 | tf_op jit(solution)/shard_map/ppermute | solution.py:445
  32.6 1.9 %collective-permute-start.5 = (f32[520,256]{1,0:T(8,128)S(1)}, f32[520,256]{1,0:T(8,128)S(1)}, u32[]{:S(2)}, u32[]{:S(2)}) collective-permute-start(f32[520,256]{1,0:T(8,128)S(1)} %collective-permute-done.part2_ref), channel_id=1, source_target_pairs={{0,1},{1,0},{2,3},{3,2},{4,5},{5,4},{6,7},{7,6},{8,9},{9,8},{10,11... | collective-permute-start | bytes 1597448 | tf_op jit(solution)/shard_map/ppermute | solution.py:464

commit v3 on v2

--- a/solution.py
+++ b/solution.py
@@ -11,6 +11,7 @@
 LANES = 128
 HALO_ROWS = 8
 SWEEPS = 4
+EARLY = 3
 BOTH = ("fine", "coarse")
 f32, bf16, i32 = jnp.float32, jnp.bfloat16, jnp.int32
 VMEM_LIMIT = 24 * 1024 * 1024
@@ -106,15 +107,7 @@
     return copies
 
 
-def start_kernel(
-    rhs_any, weights_any, order_any, smoother_any, near_ref, onward_ref, own_ref,
-    rhs_ref, weights_ref, order_ref, smoother_ref, high_ref, low_ref, sem_ref,
-):
-    copies = fetch(
-        sem_ref, (smoother_any, smoother_ref), (rhs_any, rhs_ref), (weights_any, weights_ref), (order_any, order_ref)
-    )
-    for copy in copies:
-        copy.wait()
+def start(rhs_ref, weights_ref, order_ref, smoother_ref, near_ref, onward_ref, own_ref, high_ref, low_ref):
     pairs = rhs_ref.shape[0]
     smoothed = apply_smoother(rhs_ref[...], smoother_ref, high_ref, low_ref)
     order = by_half(as_columns(order_ref[...].astype(f32), pairs), (pairs, LANES))
@@ -124,6 +117,55 @@
         bottom, top = part[:HALO_ROWS], part[pairs - HALO_ROWS :]
         near_ref[i] = jnp.where(even, top, bottom)
         onward_ref[i] = jnp.where(even, bottom, top)
+
+
+def start_kernel(
+    rhs_any, weights_any, order_any, smoother_any, near_ref, onward_ref, own_ref,
+    rhs_ref, weights_ref, order_ref, smoother_ref, high_ref, low_ref, sem_ref,
+):
+    copies = fetch(
+        sem_ref, (smoother_any, smoother_ref), (rhs_any, rhs_ref), (weights_any, weights_ref), (order_any, order_ref)
+    )
+    for copy in copies:
+        copy.wait()
+    start(rhs_ref, weights_ref, order_ref, smoother_ref, near_ref, onward_ref, own_ref, high_ref, low_ref)
+
+
+def start_pack_kernel(
+    rhs_any, weights_any, order_any, smoother_any, rows_any, values_any, inverse_any,
+    near_ref, onward_ref, own_ref, packed_ref, first_ref, second_ref,
+    rhs_ref, weights_ref, order_ref, smoother_ref, rows_ref, values_ref, inverse_ref, high_ref, low_ref, sem_ref,
+):
+    copies = fetch(
+        sem_ref, (smoother_any, smoother_ref), (rhs_any, rhs_ref), (weights_any, weights_ref), (order_any, order_ref),
+        (values_any, values_ref), (inverse_any, inverse_ref), (rows_any, rows_ref),
+    )
+    for copy in copies[:4]:
+        copy.wait()
+    start(rhs_ref, weights_ref, order_ref, smoother_ref, near_ref, onward_ref, own_ref, high_ref, low_ref)
+    for copy in copies[4:]:
+        copy.wait()
+    own_blocks, nbrs = rows_ref.shape
+    deep, width = values_ref.shape
+    lane, block = iota((own_blocks, width), 1), iota((own_blocks, width), 0)
+    rows = jnp.zeros((own_blocks, width), f32)
+    for k in range(nbrs):
+        here = (lane // 32 == k) & (lane % 16 == block)
+        rows = jnp.where(here, rows_ref[:, k : k + 1].astype(f32), rows)
+    rows = jnp.broadcast_to(jnp.sum(rows, axis=0, keepdims=True), (8, width))
+    early = first_ref.shape[0] - 8
+    first_ref[pl.ds(0, 8), :] = rows
+    packed_ref[pl.ds(0, 8), :] = rows
+    for r in range(0, deep, CELLS):
+        values = values_ref[pl.ds(r, CELLS), :].astype(f32)
+        packed_ref[pl.ds(8 + r, CELLS), :] = values
+        if r < early:
+            first_ref[pl.ds(8 + r, CELLS), :] = values
+        else:
+            second_ref[pl.ds(r - early, CELLS), :] = values
+    inverse = inverse_ref[...].astype(f32)
+    packed_ref[pl.ds(8 + deep, CELLS), :] = inverse
+    second_ref[pl.ds(deep - early, CELLS), :] = inverse
 
 
 def window_of(near_ref, far_ref, own_ref, device, devices):
@@ -216,50 +258,38 @@
     result_ref[...] = mine + apply_smoother(local_ref[2] - image, smoother_ref, high_ref, low_ref)
 
 
-def pack_kernel(rows_any, values_any, inverse_any, out_ref, rows_ref, values_ref, inverse_ref, sem_ref):
-    copies = fetch(sem_ref, (values_any, values_ref), (inverse_any, inverse_ref), (rows_any, rows_ref))
-    for copy in copies:
-        copy.wait()
-    own_blocks, nbrs = rows_ref.shape
-    deep, width = values_ref.shape
-    out_ref[pl.ds(0, deep), :] = values_ref[...].astype(f32)
-    out_ref[pl.ds(deep, CELLS), :] = inverse_ref[...].astype(f32)
-    lane, block = iota((own_blocks, width), 1), iota((own_blocks, width), 0)
-    rows = jnp.zeros((own_blocks, width), f32)
-    for k in range(nbrs):
-        here = (lane // 32 == k) & (lane % 16 == block)
-        rows = jnp.where(here, rows_ref[:, k : k + 1].astype(f32), rows)
-    out_ref[pl.ds(deep + CELLS, 8), :] = jnp.broadcast_to(jnp.sum(rows, axis=0, keepdims=True), (8, width))
-
-
 def solve_kernel(
     devices, gathered_ref, near_ref, far_ref, own_ref, selected_ref, local_ref,
-    part0_ref, part1_ref, part2_ref, part3_ref, fine_any, smoother_any,
+    mine_ref, beside_ref, first2_ref, second2_ref, first3_ref, second3_ref, fine_any, smoother_any,
     out_any, correction_any,
     blocks_ref, inverse_ref, result_ref, correction_ref,
     fine_ref, smoother_ref, picked_ref, high_ref, low_ref, sem_ref, out_sem_ref,
 ):
     copies = fetch(sem_ref, (fine_any, fine_ref), (smoother_any, smoother_ref))
-    part_refs = (part0_ref, part1_ref, part2_ref, part3_ref)
     me = lax.axis_index("coarse")
-    parts = len(part_refs)
-    width = part0_ref.shape[1]
+    parts = blocks_ref.shape[0]
+    deep, width = blocks_ref.shape[1:]
+    nbrs = deep // CELLS
     own_blocks = width // CELLS
     groups = parts * own_blocks
     unknowns = groups * CELLS
-    nbrs = (part0_ref.shape[0] - 8) // CELLS - 1
-    deep = nbrs * CELLS
-    for i, ref in enumerate(part_refs):
-        blocks_ref[i] = ref[pl.ds(0, deep), :].astype(bf16)
-        inverse_ref[i] = ref[pl.ds(deep, CELLS), :].astype(bf16)
+    early = first2_ref.shape[0] - 8
+    row_refs = (mine_ref, beside_ref, first2_ref, first3_ref)
+    for i, ref in enumerate((mine_ref, beside_ref)):
+        blocks_ref[i] = ref[pl.ds(8, deep), :].astype(bf16)
+        inverse_ref[i] = ref[pl.ds(8 + deep, CELLS), :].astype(bf16)
+    for i, first, second in ((2, first2_ref, second2_ref), (3, first3_ref, second3_ref)):
+        blocks_ref[i, pl.ds(0, early), :] = first[pl.ds(8, early), :].astype(bf16)
+        blocks_ref[i, pl.ds(early, deep - early), :] = second[pl.ds(0, deep - early), :].astype(bf16)
+        inverse_ref[i] = second[pl.ds(deep - early, CELLS), :].astype(bf16)
 
     def place(group):
         return jnp.bitwise_xor(group // own_blocks, me) * own_blocks + group % own_blocks
 
     lane = iota((1, width), 1)
     target = jnp.zeros((1, width), f32)
-    for i, ref in enumerate(part_refs):
-        rows = ref[pl.ds(deep + CELLS, 8), :][0:1, :]
+    for i, ref in enumerate(row_refs):
+        rows = ref[pl.ds(0, 8), :][0:1, :]
         rows = jnp.where((lane % 16 < own_blocks) & (lane < 32 * nbrs), rows, 0.0)
         target = target + (rows if i == 0 else pltpu.roll(rows, i * own_blocks, 1))
     target = place(target.astype(i32))
@@ -415,10 +445,31 @@
     copies = pltpu.SemaphoreType.DMA((4,))
     edge = shape_of(3, HALO_ROWS, LANES)
 
-    near, onward, own = call(
-        start_kernel, (edge, edge, shape_of(3, pairs, LANES)), "aaaa",
-        scratch=[vector, vector, pltpu.VMEM((1, aggs), i32), smoother_buffer, *products, copies],
-    )(rhs, weights, coarse_order.reshape(1, aggs), smoother)
+    copied = parts == 4 and devices % 32 == 0 and devices <= 64
+    start_shapes = (edge, edge, shape_of(3, pairs, LANES))
+    start_ins = (rhs, weights, coarse_order.reshape(1, aggs), smoother)
+    start_scratch = [vector, vector, pltpu.VMEM((1, aggs), i32), smoother_buffer]
+    if copied:
+        deep = coarse_values.shape[0] * CELLS
+        width = coarse_inverse.shape[1]
+        early = EARLY * CELLS
+        near, onward, own, packed, first, second = call(
+            start_pack_kernel,
+            (*start_shapes, shape_of(8 + deep + CELLS, width), shape_of(8 + early, width),
+             shape_of(deep - early + CELLS, width)),
+            "aaaaaaa",
+            scratch=[
+                *start_scratch, pltpu.VMEM(coarse_rows.shape[::-1], i32), pltpu.VMEM((deep, width), bf16),
+                pltpu.VMEM(coarse_inverse.shape, bf16), *products, pltpu.SemaphoreType.DMA((7,)),
+            ],
+        )(*start_ins, coarse_rows.T, coarse_values.reshape(deep, width), coarse_inverse)
+        swap = [(c, c ^ 1) for c in range(parts)]
+        across = [(c, c ^ 2) for c in range(parts)]
+        first2 = lax.ppermute(first, "coarse", across)
+    else:
+        near, onward, own = call(start_kernel, start_shapes, "aaaa", scratch=[*start_scratch, *products, copies])(
+            *start_ins
+        )
 
     partner = [(d, d ^ 1) for d in range(devices)]
     chain = []
@@ -427,23 +478,11 @@
         chain.append((d, target if 0 <= target < devices else d ^ 1))
     onward = lax.ppermute(onward, BOTH, partner)
     near = lax.ppermute(near, BOTH, partner)
+
+    if copied:
+        packed, onward = lax.optimization_barrier((packed, onward))
+        beside = lax.ppermute(packed, "coarse", swap)
     far = lax.ppermute(onward, BOTH, chain)
-
-    copied = parts == 4 and devices % 32 == 0 and devices <= 64
-    if copied:
-        deep = coarse_values.shape[0] * CELLS
-        width = coarse_inverse.shape[1]
-        coarse_values, _ = lax.optimization_barrier((coarse_values, own))
-        packed = call(pack_kernel, shape_of(deep + CELLS + 8, width), "aaa", scratch=[
-            pltpu.VMEM(coarse_rows.shape[::-1], i32), pltpu.VMEM((deep, width), bf16),
-            pltpu.VMEM(coarse_inverse.shape, bf16), copies,
-        ])(
-            coarse_rows.T, coarse_values.reshape(deep, width), coarse_inverse
-        )
-        other = lax.ppermute(packed, "coarse", [(c, c ^ 2) for c in range(parts)])
-        swap = [(c, c ^ 1) for c in range(parts)]
-        beside = lax.ppermute(packed, "coarse", swap)
-
     selected, weighed, local = call(
         prepare_kernel,
         (jax.ShapeDtypeStruct((aggs * nbrs, 4 * rows), bf16), shape_of(nbrs * pairs, 8, LANES), shape_of(4, pairs, LANES)),
@@ -451,6 +490,13 @@
         scratch=[vector, vector, pltpu.VMEM(fine_columns.shape, i32), fine_buffer, pltpu.VMEM((CELLS, cells), f32), copies],
     )(pit_counts, own, rhs, reaction, fine_columns, fine_values)
 
+    if copied:
+        first2, second, far, near, selected, beside = lax.optimization_barrier(
+            (first2, second, far, near, selected, beside)
+        )
+        second2 = lax.ppermute(second, "coarse", across)
+        first3 = lax.ppermute(first2, "coarse", swap)
+
     sent = call(
         functools.partial(residual_kernel, devices), shape_of(devices, LANES), "vvvvvv", scratch=[picked]
     )(near, far, own, selected, weighed, local)
@@ -459,13 +505,14 @@
     common = (near, far, own, selected, local)
     fetched = (fine_values, smoother)
     if copied:
+        first3, sent = lax.optimization_barrier((first3, sent))
         gathered = lax.all_to_all(sent, BOTH, 0, 0, tiled=True)
-        other, gathered = lax.optimization_barrier((other, gathered))
-        pieces = (packed, beside, other, lax.ppermute(other, "coarse", swap))
+        second2, gathered = lax.optimization_barrier((second2, gathered))
+        pieces = (packed, beside, first2, second2, first3, lax.ppermute(second2, "coarse", swap))
         result, correction = call(
             functools.partial(solve_kernel, devices),
             (shape_of(pairs, LANES), shape_of(width // LANES, LANES)),
-            "vvvvvvvvvvaa",
+            "vvvvvv" + "vvvvvv" + "aa",
             outs="aa",
             scratch=[
                 pltpu.VMEM((parts, deep, width), bf16), pltpu.VMEM((parts, CELLS, width), bf16),

time: 40.2 us -> 34.8 us (0.87)
  blocking collectives: 0 us -> 11.8 us
  waiting for transfers between devices: 17 us -> 6.16 us
  starting transfers between devices: 10.6 us -> 5.77 us
  Pallas kernels: 11 us -> 9.49 us
    all_to_all x0 -> x1, blocking collectives: none -> 11.8 us  [shards(): gathered = lax.all_to_all(sent, BOTH, 0, 0, tiled=True)]
    all_to_all x1 -> x0, waiting for transfers between devices: 6.83 us -> none  [shards(): gathered = lax.all_to_all(sent, BOTH, 0, 0, tiled=True)]
    all_to_all x1 -> x0, starting transfers between devices: 6.68 us -> none  [shards(): gathered = lax.all_to_all(sent, BOTH, 0, 0, tiled=True)]
    ppermute x1, waiting for transfers between devices: 7.61 us -> 2 us  [shards(): far = lax.ppermute(onward, BOTH, chain)]
    ppermute x2 -> x4, starting transfers between devices: 3.03 us -> 4.57 us  [the longest x1 2.68 us: shards(): first2 = lax.ppermute(first, 'coarse', across)]
    pallas_call x5 -> x4, Pallas kernels: 11 us -> 9.49 us  [placed(): run(*(pltpu.with_memory_space_constraint(x, pltpu.HBM) if c == 'a' else x...]
    ppermute x2 -> x4, waiting for transfers between devices: 1.92 us -> 3.32 us  [the longest x1 1.63 us: shards(): lax.ppermute(second2, 'coarse', swap)]
    ppermute x1, starting transfers between devices: 0.01 us -> 0.52 us  [shards(): onward = lax.ppermute(onward, BOTH, partner)]
  transfers between devices with their start and end apart: 7 -> 8, of which waited for: 4 -> 5; matrix products, arithmetic and copies ran while one was open for 0% -> 0% of each run, Pallas kernels for 8% -> 7%
where the time goes in v3:
time: 34.8 us; the launch traced here: 34.5 us
  blocking collectives  11.8 us (34%)
  Pallas kernels  9.49 us (27%)
  waiting for transfers between devices  6.16 us (18%)
  starting transfers between devices  5.77 us (17%)
  between operations  1.32 us (4%)
    all_to_all x1, blocking collectives, shards(): gathered = lax.all_to_all(sent, BOTH, 0, 0, tiled=True)  11.8 us
    pallas_call x4, Pallas kernels, placed(): run(*(pltpu.with_memory_space_constraint(x, pltpu.HBM) if c == 'a' else x...  9.49 us
    ppermute x1, starting transfers between devices, shards(): first2 = lax.ppermute(first, 'coarse', across)  2.68 us
    ppermute x1, waiting for transfers between devices, shards(): far = lax.ppermute(onward, BOTH, chain)  2 us
    ppermute x1, starting transfers between devices, shards(): second2 = lax.ppermute(second, 'coarse', across)  1.88 us
    ppermute x1, waiting for transfers between devices, shards(): lax.ppermute(second2, 'coarse', swap)  1.63 us
    ppermute x1, waiting for transfers between devices, shards(): first3 = lax.ppermute(first2, 'coarse', swap)  1.09 us
    ppermute x1, waiting for transfers between devices, shards(): onward = lax.ppermute(onward, BOTH, partner)  0.83 us
  transfers between devices with their start and end apart: 8, of which 5 were waited for; matrix products, arithmetic and copies ran while one was open for 0% of the time, Pallas kernels for 7%

profile of v3, /device:TPU:0, one launch (start us, length us, event | category | flops | bytes accessed | tf_op | source)
XLA Modules:
  0.0 34.5 jit_solution(5143507016263959739)
XLA Ops:
  0.6 1.6 %shard_map.122 = (f32[3,8,128]{2,1,0:T(8,128)S(1)}, f32[3,8,128]{2,1,0:T(8,128)S(1)}, f32[3,16,128]{2,1,0:T(8,128)S(1)}, f32[520,256]{1,0:T(8,128)S(1)}, f32[200,256]{1,0:T(8,128)S(1)}, /*index=5*/f32[320,256]{1,0:T(8,128)S(1)}) custom-call(f32[16,128]{1,0:T(8,128)} %bitcast.15, f32[16,128]{1,0:T(8,128)} %bitcast.17, s32[1,32]{1,0:T(1,128)} %bitcast.20, ...), custom_call_target="tpu_custom_call" | custom-call | tf_op jit(solution)/shard_map/pallas_call | solution.py:394
  2.2 0.5 %collective-permute-start.1 = (f32[3,8,128]{2,1,0:T(8,128)S(1)}, f32[3,8,128]{2,1,0:T(8,128)S(1)}, u32[]{:S(2)}, u32[]{:S(2)}) collective-permute-start(f32[3,8,128]{2,1,0:T(8,128)S(1)} %get-tuple-element.28), channel_id=1, source_target_pairs={{0,1},{1,0},{2,3},{3,2},{4,5},{5,4},{6,7},{7,6},{8,9},{9,8},{10,11... | collective-permute-start | bytes 36872 | tf_op jit(solution)/shard_map/ppermute | solution.py:479
  2.7 0.8 %collective-permute-done.1 = f32[3,8,128]{2,1,0:T(8,128)S(1)} collective-permute-done((f32[3,8,128]{2,1,0:T(8,128)S(1)}, f32[3,8,128]{2,1,0:T(8,128)S(1)}, u32[]{:S(2)}, u32[]{:S(2)}) %collective-permute-start.1) | collective-permute-done | bytes 12320 | tf_op jit(solution)/shard_map/ppermute | solution.py:479
  3.6 0.3 collective-permute-start.4
  3.9 2.7 %collective-permute-start = (f32[200,256]{1,0:T(8,128)S(1)}, f32[200,256]{1,0:T(8,128)S(1)}, u32[]{:S(2)}, u32[]{:S(2)}) collective-permute-start(f32[200,256]{1,0:T(8,128)S(1)} %get-tuple-element.25), channel_id=1, source_target_pairs={{0,2},{1,3},{2,0},{3,1},{4,6},{5,7},{6,4},{7,5},{8,10},{9,11},{10,... | collective-permute-start | bytes 614408 | tf_op jit(solution)/shard_map/ppermute | solution.py:468
  6.6 0.1 collective-permute-start.3
  6.7 0.3 collective-permute-start.2
  7.6 2.1 %shard_map.123 = (bf16[224,128]{1,0:T(8,128)(2,1)S(1)}, f32[112,8,128]{2,1,0:T(8,128)S(1)}, f32[4,16,128]{2,1,0:T(8,128)S(1)}) custom-call(s32[1]{0:T(128)S(6)} %copy.14.counts_ref, f32[3,16,128]{2,1,0:T(8,128)S(1)} %get-tuple-element.31.own_ref, f32[16,128]{1,0:T(8,128)} %bitcast.16, f32[16,128]{1,0:T(8,128)} %bitcast.18, s32[7,32]{1,0:T(8,128)} %columns_any.1, ...), custom_call_target="tpu_custom_call" | custom-call | tf_op jit(solution)/shard_map/pallas_call | solution.py:394
  9.7 0.0 collective-permute-done.3.near_ref
  9.7 2.0 %collective-permute-done.2.far_ref = f32[3,8,128]{2,1,0:T(8,128)S(1)} collective-permute-done((f32[3,8,128]{2,1,0:T(8,128)S(1)}, f32[3,8,128]{2,1,0:T(8,128)S(1)}, u32[]{:S(2)}, u32[]{:S(2)}) %collective-permute-start.2) | collective-permute-done | bytes 12320 | tf_op jit(solution)/shard_map/ppermute | solution.py:485
  11.7 0.6 %collective-permute-done.first2_ref = f32[200,256]{1,0:T(8,128)S(1)} collective-permute-done((f32[200,256]{1,0:T(8,128)S(1)}, f32[200,256]{1,0:T(8,128)S(1)}, u32[]{:S(2)}, u32[]{:S(2)}) %collective-permute-start) | collective-permute-done | bytes 204832 | tf_op jit(solution)/shard_map/ppermute | solution.py:468
  12.3 0.0 collective-permute-done.4.beside_ref
  12.3 1.9 %collective-permute-start.5 = (f32[320,256]{1,0:T(8,128)S(1)}, f32[320,256]{1,0:T(8,128)S(1)}, u32[]{:S(2)}, u32[]{:S(2)}) collective-permute-start(f32[320,256]{1,0:T(8,128)S(1)} %get-tuple-element.34), channel_id=1, source_target_pairs={{0,2},{1,3},{2,0},{3,1},{4,6},{5,7},{6,4},{7,5},{8,10},{9,11},{10,... | collective-permute-start | bytes 983048 | tf_op jit(solution)/shard_map/ppermute | solution.py:497
  14.2 0.0 collective-permute-start.6
  14.2 0.4 %shard_map.124 = f32[32,128]{1,0:T(8,128)S(1)} custom-call(f32[3,8,128]{2,1,0:T(8,128)S(1)} %collective-permute-done.3.near_ref, f32[3,8,128]{2,1,0:T(8,128)S(1)} %collective-permute-done.2.far_ref, f32[3,16,128]{2,1,0:T(8,128)S(1)} %get-tuple-element.31.own_ref, bf16[224,128]{1,0:T(8,128)(2,1)S(1)} %get-tuple-element.38.selected_ref, ...), custom_call_target="tpu_custom_call" | custom-call | tf_op jit(solution)/shard_map/pallas_call | solution.py:394
  14.6 1.1 %collective-permute-done.6.first3_ref = f32[200,256]{1,0:T(8,128)S(1)} collective-permute-done((f32[200,256]{1,0:T(8,128)S(1)}, f32[200,256]{1,0:T(8,128)S(1)}, u32[]{:S(2)}, u32[]{:S(2)}) %collective-permute-start.6) | collective-permute-done | bytes 204832 | tf_op jit(solution)/shard_map/ppermute | solution.py:498
  15.6 11.8 %all_to_all.12 = f32[32,1,128]{2,1,0:T(1,128)S(1)} all-to-all(f32[32,1,128]{2,1,0:T(1,128)S(1)} %bitcast.13), channel_id=1, replica_groups=mesh['fine'=8,'coarse'=4] {'fine','coarse'}, dimensions={0} | all-to-all | bytes 32768 | tf_op jit(solution)/shard_map/all_to_all | solution.py:509
  27.4 0.0 collective-permute-done.5.second2_ref
  27.4 0.0 collective-permute-start.7
  27.4 1.6 %collective-permute-done.7.second3_ref = f32[320,256]{1,0:T(8,128)S(1)} collective-permute-done((f32[320,256]{1,0:T(8,128)S(1)}, f32[320,256]{1,0:T(8,128)S(1)}, u32[]{:S(2)}, u32[]{:S(2)}) %collective-permute-start.7) | collective-permute-done | bytes 327712 | tf_op jit(solution)/shard_map/ppermute | solution.py:511
  29.1 5.5 %shard_map.125 = (f32[16,128]{1,0:T(8,128)}, f32[2,128]{1,0:T(2,128)}) custom-call(f32[32,128]{1,0:T(8,128)S(1)} %bitcast.12, f32[3,8,128]{2,1,0:T(8,128)S(1)} %collective-permute-done.3.near_ref, f32[3,8,128]{2,1,0:T(8,128)S(1)} %collective-permute-done.2.far_ref, f32[3,16,128]{2,1,0:T(8,128)S(1)} %get-tuple-element.31.own_ref, ...), custom_call_target="tpu_custom_call" | custom-call | tf_op jit(solution)/shard_map/pallas_call | solution.py:394
Async XLA Ops:
  2.2 1.4 %collective-permute-start.1 = (f32[3,8,128]{2,1,0:T(8,128)S(1)}, f32[3,8,128]{2,1,0:T(8,128)S(1)}, u32[]{:S(2)}, u32[]{:S(2)}) collective-permute-start(f32[3,8,128]{2,1,0:T(8,128)S(1)} %get-tuple-element.28), channel_id=1, source_target_pairs={{0,1},{1,0},{2,3},{3,2},{4,5},{5,4},{6,7},{7,6},{8,9},{9,8},{10,11... | collective-permute-start | bytes 36872 | tf_op jit(solution)/shard_map/ppermute | solution.py:479
  3.6 8.7 %collective-permute-start.4 = (f32[520,256]{1,0:T(8,128)S(1)}, f32[520,256]{1,0:T(8,128)S(1)}, u32[]{:S(2)}, u32[]{:S(2)}) collective-permute-start(f32[520,256]{1,0:T(8,128)S(1)} %get-tuple-element.33.mine_ref), channel_id=1, source_target_pairs={{0,1},{1,0},{2,3},{3,2},{4,5},{5,4},{6,7},{7,6},{8,9},{9,8},{10,11... | collective-permute-start | bytes 1597448 | tf_op jit(solution)/shard_map/ppermute | solution.py:484
  3.9 8.4 %collective-permute-start = (f32[200,256]{1,0:T(8,128)S(1)}, f32[200,256]{1,0:T(8,128)S(1)}, u32[]{:S(2)}, u32[]{:S(2)}) collective-permute-start(f32[200,256]{1,0:T(8,128)S(1)} %get-tuple-element.25), channel_id=1, source_target_pairs={{0,2},{1,3},{2,0},{3,1},{4,6},{5,7},{6,4},{7,5},{8,10},{9,11},{10,... | collective-permute-start | bytes 614408 | tf_op jit(solution)/shard_map/ppermute | solution.py:468
  6.6 3.1 %collective-permute-start.3 = (f32[3,8,128]{2,1,0:T(8,128)S(1)}, f32[3,8,128]{2,1,0:T(8,128)S(1)}, u32[]{:S(2)}, u32[]{:S(2)}) collective-permute-start(f32[3,8,128]{2,1,0:T(8,128)S(1)} %get-tuple-element.30), channel_id=1, source_target_pairs={{0,1},{1,0},{2,3},{3,2},{4,5},{5,4},{6,7},{7,6},{8,9},{9,8},{10,11... | collective-permute-start | bytes 36872 | tf_op jit(solution)/shard_map/ppermute | solution.py:480
  6.7 5.0 %collective-permute-start.2 = (f32[3,8,128]{2,1,0:T(8,128)S(1)}, f32[3,8,128]{2,1,0:T(8,128)S(1)}, u32[]{:S(2)}, u32[]{:S(2)}) collective-permute-start(f32[3,8,128]{2,1,0:T(8,128)S(1)} %collective-permute-done.1), channel_id=1, source_target_pairs={{0,2},{1,0},{2,4},{3,1},{4,6},{5,3},{6,8},{7,5},{8,10},{9,7},{10,1... | collective-permute-start | bytes 36872 | tf_op jit(solution)/shard_map/ppermute | solution.py:485
  12.3 15.1 %collective-permute-start.5 = (f32[320,256]{1,0:T(8,128)S(1)}, f32[320,256]{1,0:T(8,128)S(1)}, u32[]{:S(2)}, u32[]{:S(2)}) collective-permute-start(f32[320,256]{1,0:T(8,128)S(1)} %get-tuple-element.34), channel_id=1, source_target_pairs={{0,2},{1,3},{2,0},{3,1},{4,6},{5,7},{6,4},{7,5},{8,10},{9,11},{10,... | collective-permute-start | bytes 983048 | tf_op jit(solution)/shard_map/ppermute | solution.py:497
  14.2 1.5 %collective-permute-start.6 = (f32[200,256]{1,0:T(8,128)S(1)}, f32[200,256]{1,0:T(8,128)S(1)}, u32[]{:S(2)}, u32[]{:S(2)}) collective-permute-start(f32[200,256]{1,0:T(8,128)S(1)} %collective-permute-done.first2_ref), channel_id=1, source_target_pairs={{0,1},{1,0},{2,3},{3,2},{4,5},{5,4},{6,7},{7,6},{8,9},{9,8},{10,11... | collective-permute-start | bytes 614408 | tf_op jit(solution)/shard_map/ppermute | solution.py:498
  27.4 1.6 %collective-permute-start.7 = (f32[320,256]{1,0:T(8,128)S(1)}, f32[320,256]{1,0:T(8,128)S(1)}, u32[]{:S(2)}, u32[]{:S(2)}) collective-permute-start(f32[320,256]{1,0:T(8,128)S(1)} %collective-permute-done.5.second2_ref), channel_id=1, source_target_pairs={{0,1},{1,0},{2,3},{3,2},{4,5},{5,4},{6,7},{7,6},{8,9},{9,8},{10,11... | collective-permute-start | bytes 983048 | tf_op jit(solution)/shard_map/ppermute | solution.py:511

commit v4 on v3

--- a/solution.py
+++ b/solution.py
@@ -11,7 +11,7 @@
 LANES = 128
 HALO_ROWS = 8
 SWEEPS = 4
-EARLY = 3
+EARLY = 2
 BOTH = ("fine", "coarse")
 f32, bf16, i32 = jnp.float32, jnp.bfloat16, jnp.int32
 VMEM_LIMIT = 24 * 1024 * 1024
@@ -153,19 +153,19 @@
         here = (lane // 32 == k) & (lane % 16 == block)
         rows = jnp.where(here, rows_ref[:, k : k + 1].astype(f32), rows)
     rows = jnp.broadcast_to(jnp.sum(rows, axis=0, keepdims=True), (8, width))
-    early = first_ref.shape[0] - 8
-    first_ref[pl.ds(0, 8), :] = rows
-    packed_ref[pl.ds(0, 8), :] = rows
+    inverse = inverse_ref[...].astype(f32)
+    for ref in (packed_ref, first_ref):
+        ref[pl.ds(0, 8), :] = rows
+        ref[pl.ds(8, CELLS), :] = inverse
+    base = 8 + CELLS
+    early = first_ref.shape[0] - base
     for r in range(0, deep, CELLS):
         values = values_ref[pl.ds(r, CELLS), :].astype(f32)
-        packed_ref[pl.ds(8 + r, CELLS), :] = values
+        packed_ref[pl.ds(base + r, CELLS), :] = values
         if r < early:
-            first_ref[pl.ds(8 + r, CELLS), :] = values
+            first_ref[pl.ds(base + r, CELLS), :] = values
         else:
             second_ref[pl.ds(r - early, CELLS), :] = values
-    inverse = inverse_ref[...].astype(f32)
-    packed_ref[pl.ds(8 + deep, CELLS), :] = inverse
-    second_ref[pl.ds(deep - early, CELLS), :] = inverse
 
 
 def window_of(near_ref, far_ref, own_ref, device, devices):
@@ -273,15 +273,16 @@
     own_blocks = width // CELLS
     groups = parts * own_blocks
     unknowns = groups * CELLS
-    early = first2_ref.shape[0] - 8
+    base = 8 + CELLS
+    early = first2_ref.shape[0] - base
     row_refs = (mine_ref, beside_ref, first2_ref, first3_ref)
     for i, ref in enumerate((mine_ref, beside_ref)):
-        blocks_ref[i] = ref[pl.ds(8, deep), :].astype(bf16)
-        inverse_ref[i] = ref[pl.ds(8 + deep, CELLS), :].astype(bf16)
+        blocks_ref[i] = ref[pl.ds(base, deep), :].astype(bf16)
     for i, first, second in ((2, first2_ref, second2_ref), (3, first3_ref, second3_ref)):
-        blocks_ref[i, pl.ds(0, early), :] = first[pl.ds(8, early), :].astype(bf16)
-        blocks_ref[i, pl.ds(early, deep - early), :] = second[pl.ds(0, deep - early), :].astype(bf16)
-        inverse_ref[i] = second[pl.ds(deep - early, CELLS), :].astype(bf16)
+        blocks_ref[i, pl.ds(0, early), :] = first[pl.ds(base, early), :].astype(bf16)
+        blocks_ref[i, pl.ds(early, deep - early), :] = second[...].astype(bf16)
+    for i, ref in enumerate(row_refs):
+        inverse_ref[i] = ref[pl.ds(8, CELLS), :].astype(bf16)
 
     def place(group):
         return jnp.bitwise_xor(group // own_blocks, me) * own_blocks + group % own_blocks
@@ -455,8 +456,8 @@
         early = EARLY * CELLS
         near, onward, own, packed, first, second = call(
             start_pack_kernel,
-            (*start_shapes, shape_of(8 + deep + CELLS, width), shape_of(8 + early, width),
-             shape_of(deep - early + CELLS, width)),
+            (*start_shapes, shape_of(8 + CELLS + deep, width), shape_of(8 + CELLS + early, width),
+             shape_of(deep - early, width)),
             "aaaaaaa",
             scratch=[
                 *start_scratch, pltpu.VMEM(coarse_rows.shape[::-1], i32), pltpu.VMEM((deep, width), bf16),
@@ -479,9 +480,6 @@
     onward = lax.ppermute(onward, BOTH, partner)
     near = lax.ppermute(near, BOTH, partner)
 
-    if copied:
-        packed, onward = lax.optimization_barrier((packed, onward))
-        beside = lax.ppermute(packed, "coarse", swap)
     far = lax.ppermute(onward, BOTH, chain)
     selected, weighed, local = call(
         prepare_kernel,
@@ -491,9 +489,8 @@
     )(pit_counts, own, rhs, reaction, fine_columns, fine_values)
 
     if copied:
-        first2, second, far, near, selected, beside = lax.optimization_barrier(
-            (first2, second, far, near, selected, beside)
-        )
+        beside = lax.ppermute(packed, "coarse", swap)
+        first2, second, far, near, selected = lax.optimization_barrier((first2, second, far, near, selected))
         second2 = lax.ppermute(second, "coarse", across)
         first3 = lax.ppermute(first2, "coarse", swap)
 
@@ -505,9 +502,8 @@
     common = (near, far, own, selected, local)
     fetched = (fine_values, smoother)
     if copied:
-        first3, sent = lax.optimization_barrier((first3, sent))
         gathered = lax.all_to_all(sent, BOTH, 0, 0, tiled=True)
-        second2, gathered = lax.optimization_barrier((second2, gathered))
+        first3, second2, gathered = lax.optimization_barrier((first3, second2, gathered))
         pieces = (packed, beside, first2, second2, first3, lax.ppermute(second2, "coarse", swap))
         result, correction = call(
             functools.partial(solve_kernel, devices),

time: 34.8 us -> 32.5 us (0.934)
  waiting for transfers between devices: 6.16 us -> 3.47 us
    ppermute x1, waiting for transfers between devices: 2 us -> 0.57 us  [shards(): far = lax.ppermute(onward, BOTH, chain)]
    ppermute x1, waiting for transfers between devices: 1.09 us -> 0.01 us  [shards(): first3 = lax.ppermute(first2, 'coarse', swap)]
    ppermute x1, starting transfers between devices: 0.52 us -> 0.01 us  [shards(): onward = lax.ppermute(onward, BOTH, partner)]
    ppermute x1, starting transfers between devices: 0.06 us -> 0.51 us  [shards(): near = lax.ppermute(near, BOTH, partner)]
    ppermute x1, starting transfers between devices: 2.68 us -> 3.03 us  [shards(): first2 = lax.ppermute(first, 'coarse', across)]
  transfers between devices with their start and end apart: 8 -> 8, of which waited for: 5 -> 4; matrix products, arithmetic and copies ran while one was open for 0% -> 0% of each run, Pallas kernels for 7% -> 8%
where the time goes in v4:
time: 32.5 us; the launch traced here: 32.3 us
  blocking collectives  12 us (37%)
  Pallas kernels  9.49 us (29%)
  starting transfers between devices  6.01 us (18%)
  waiting for transfers between devices  3.47 us (11%)
  between operations  1.33 us (4%)
    all_to_all x1, blocking collectives, shards(): gathered = lax.all_to_all(sent, BOTH, 0, 0, tiled=True)  12 us
    pallas_call x4, Pallas kernels, placed(): run(*(pltpu.with_memory_space_constraint(x, pltpu.HBM) if c == 'a' else x...  9.49 us
    ppermute x1, starting transfers between devices, shards(): first2 = lax.ppermute(first, 'coarse', across)  3.03 us
    ppermute x1, starting transfers between devices, shards(): second2 = lax.ppermute(second, 'coarse', across)  1.88 us
    ppermute x1, waiting for transfers between devices, shards(): lax.ppermute(second2, 'coarse', swap)  1.61 us
    ppermute x1, waiting for transfers between devices, shards(): onward = lax.ppermute(onward, BOTH, partner)  0.67 us
  transfers between devices with their start and end apart: 8, of which 4 were waited for; matrix products, arithmetic and copies ran while one was open for 0% of the time, Pallas kernels for 8%

profile of v4, /device:TPU:0, one launch (start us, length us, event | category | flops | bytes accessed | tf_op | source)
XLA Modules:
  0.0 32.3 jit_solution(11188445308072035608)
XLA Ops:
  0.6 1.6 %shard_map.122 = (f32[3,8,128]{2,1,0:T(8,128)S(1)}, f32[3,8,128]{2,1,0:T(8,128)S(1)}, f32[3,16,128]{2,1,0:T(8,128)S(1)}, f32[520,256]{1,0:T(8,128)S(1)}, f32[200,256]{1,0:T(8,128)S(1)}, /*index=5*/f32[320,256]{1,0:T(8,128)S(1)}) custom-call(f32[16,128]{1,0:T(8,128)} %bitcast.15, f32[16,128]{1,0:T(8,128)} %bitcast.17, s32[1,32]{1,0:T(1,128)} %bitcast.20, ...), custom_call_target="tpu_custom_call" | custom-call | tf_op jit(solution)/shard_map/pallas_call | solution.py:395
  2.2 3.0 %collective-permute-start = (f32[200,256]{1,0:T(8,128)S(1)}, f32[200,256]{1,0:T(8,128)S(1)}, u32[]{:S(2)}, u32[]{:S(2)}) collective-permute-start(f32[200,256]{1,0:T(8,128)S(1)} %get-tuple-element.21), channel_id=1, source_target_pairs={{0,2},{1,3},{2,0},{3,1},{4,6},{5,7},{6,4},{7,5},{8,10},{9,11},{10,... | collective-permute-start | bytes 614408 | tf_op jit(solution)/shard_map/ppermute | solution.py:469
  5.2 0.0 collective-permute-start.1
  5.3 0.5 %collective-permute-start.3 = (f32[3,8,128]{2,1,0:T(8,128)S(1)}, f32[3,8,128]{2,1,0:T(8,128)S(1)}, u32[]{:S(2)}, u32[]{:S(2)}) collective-permute-start(f32[3,8,128]{2,1,0:T(8,128)S(1)} %get-tuple-element.24), channel_id=1, source_target_pairs={{0,1},{1,0},{2,3},{3,2},{4,5},{5,4},{6,7},{7,6},{8,9},{9,8},{10,11... | collective-permute-start | bytes 36872 | tf_op jit(solution)/shard_map/ppermute | solution.py:481
  5.8 0.7 %collective-permute-done.1 = f32[3,8,128]{2,1,0:T(8,128)S(1)} collective-permute-done((f32[3,8,128]{2,1,0:T(8,128)S(1)}, f32[3,8,128]{2,1,0:T(8,128)S(1)}, u32[]{:S(2)}, u32[]{:S(2)}) %collective-permute-start.1) | collective-permute-done | bytes 12320 | tf_op jit(solution)/shard_map/ppermute | solution.py:480
  6.4 0.1 collective-permute-start.2
  7.2 2.1 %shard_map.123 = (bf16[224,128]{1,0:T(8,128)(2,1)S(1)}, f32[112,8,128]{2,1,0:T(8,128)S(1)}, f32[4,16,128]{2,1,0:T(8,128)S(1)}) custom-call(s32[1]{0:T(128)S(6)} %copy.14.counts_ref, f32[3,16,128]{2,1,0:T(8,128)S(1)} %get-tuple-element.25.own_ref, f32[16,128]{1,0:T(8,128)} %bitcast.16, f32[16,128]{1,0:T(8,128)} %bitcast.18, s32[7,32]{1,0:T(8,128)} %columns_any.1, ...), custom_call_target="tpu_custom_call" | custom-call | tf_op jit(solution)/shard_map/pallas_call | solution.py:395
  9.3 0.0 collective-permute-done.3.near_ref
  9.3 0.6 %collective-permute-done.2.far_ref = f32[3,8,128]{2,1,0:T(8,128)S(1)} collective-permute-done((f32[3,8,128]{2,1,0:T(8,128)S(1)}, f32[3,8,128]{2,1,0:T(8,128)S(1)}, u32[]{:S(2)}, u32[]{:S(2)}) %collective-permute-start.2) | collective-permute-done | bytes 12320 | tf_op jit(solution)/shard_map/ppermute | solution.py:483
  9.8 0.6 %collective-permute-done.first2_ref = f32[200,256]{1,0:T(8,128)S(1)} collective-permute-done((f32[200,256]{1,0:T(8,128)S(1)}, f32[200,256]{1,0:T(8,128)S(1)}, u32[]{:S(2)}, u32[]{:S(2)}) %collective-permute-start) | collective-permute-done | bytes 204832 | tf_op jit(solution)/shard_map/ppermute | solution.py:469
  10.5 1.9 %collective-permute-start.5 = (f32[320,256]{1,0:T(8,128)S(1)}, f32[320,256]{1,0:T(8,128)S(1)}, u32[]{:S(2)}, u32[]{:S(2)}) collective-permute-start(f32[320,256]{1,0:T(8,128)S(1)} %get-tuple-element.28), channel_id=1, source_target_pairs={{0,2},{1,3},{2,0},{3,1},{4,6},{5,7},{6,4},{7,5},{8,10},{9,11},{10,... | collective-permute-start | bytes 983048 | tf_op jit(solution)/shard_map/ppermute | solution.py:494
  12.3 0.0 collective-permute-start.4
  12.3 0.5 %collective-permute-start.6 = (f32[520,256]{1,0:T(8,128)S(1)}, f32[520,256]{1,0:T(8,128)S(1)}, u32[]{:S(2)}, u32[]{:S(2)}) collective-permute-start(f32[520,256]{1,0:T(8,128)S(1)} %get-tuple-element.35.mine_ref), channel_id=1, source_target_pairs={{0,1},{1,0},{2,3},{3,2},{4,5},{5,4},{6,7},{7,6},{8,9},{9,8},{10,11... | collective-permute-start | bytes 1597448 | tf_op jit(solution)/shard_map/ppermute | solution.py:492
  12.8 0.4 %shard_map.124 = f32[32,128]{1,0:T(8,128)S(1)} custom-call(f32[3,8,128]{2,1,0:T(8,128)S(1)} %collective-permute-done.3.near_ref, f32[3,8,128]{2,1,0:T(8,128)S(1)} %collective-permute-done.2.far_ref, f32[3,16,128]{2,1,0:T(8,128)S(1)} %get-tuple-element.25.own_ref, bf16[224,128]{1,0:T(8,128)(2,1)S(1)} %get-tuple-element.31.selected_ref, ...), custom_call_target="tpu_custom_call" | custom-call | tf_op jit(solution)/shard_map/pallas_call | solution.py:395
  13.2 12.0 %all_to_all.12 = f32[32,1,128]{2,1,0:T(1,128)S(1)} all-to-all(f32[32,1,128]{2,1,0:T(1,128)S(1)} %bitcast.13), channel_id=1, replica_groups=mesh['fine'=8,'coarse'=4] {'fine','coarse'}, dimensions={0} | all-to-all | bytes 32768 | tf_op jit(solution)/shard_map/all_to_all | solution.py:505
  25.2 0.0 collective-permute-done.4.first3_ref
  25.2 0.0 collective-permute-done.5.second2_ref
  25.2 0.0 collective-permute-start.7
  25.2 0.0 collective-permute-done.6.beside_ref
  25.2 1.6 %collective-permute-done.7.second3_ref = f32[320,256]{1,0:T(8,128)S(1)} collective-permute-done((f32[320,256]{1,0:T(8,128)S(1)}, f32[320,256]{1,0:T(8,128)S(1)}, u32[]{:S(2)}, u32[]{:S(2)}) %collective-permute-start.7) | collective-permute-done | bytes 327712 | tf_op jit(solution)/shard_map/ppermute | solution.py:507
  26.8 5.5 %shard_map.125 = (f32[16,128]{1,0:T(8,128)}, f32[2,128]{1,0:T(2,128)}) custom-call(f32[32,128]{1,0:T(8,128)S(1)} %bitcast.12, f32[3,8,128]{2,1,0:T(8,128)S(1)} %collective-permute-done.3.near_ref, f32[3,8,128]{2,1,0:T(8,128)S(1)} %collective-permute-done.2.far_ref, f32[3,16,128]{2,1,0:T(8,128)S(1)} %get-tuple-element.25.own_ref, ...), custom_call_target="tpu_custom_call" | custom-call | tf_op jit(solution)/shard_map/pallas_call | solution.py:395
Async XLA Ops:
  2.2 8.2 %collective-permute-start = (f32[200,256]{1,0:T(8,128)S(1)}, f32[200,256]{1,0:T(8,128)S(1)}, u32[]{:S(2)}, u32[]{:S(2)}) collective-permute-start(f32[200,256]{1,0:T(8,128)S(1)} %get-tuple-element.21), channel_id=1, source_target_pairs={{0,2},{1,3},{2,0},{3,1},{4,6},{5,7},{6,4},{7,5},{8,10},{9,11},{10,... | collective-permute-start | bytes 614408 | tf_op jit(solution)/shard_map/ppermute | solution.py:469
  5.2 1.2 %collective-permute-start.1 = (f32[3,8,128]{2,1,0:T(8,128)S(1)}, f32[3,8,128]{2,1,0:T(8,128)S(1)}, u32[]{:S(2)}, u32[]{:S(2)}) collective-permute-start(f32[3,8,128]{2,1,0:T(8,128)S(1)} %get-tuple-element.23), channel_id=1, source_target_pairs={{0,1},{1,0},{2,3},{3,2},{4,5},{5,4},{6,7},{7,6},{8,9},{9,8},{10,11... | collective-permute-start | bytes 36872 | tf_op jit(solution)/shard_map/ppermute | solution.py:480
  5.3 4.0 %collective-permute-start.3 = (f32[3,8,128]{2,1,0:T(8,128)S(1)}, f32[3,8,128]{2,1,0:T(8,128)S(1)}, u32[]{:S(2)}, u32[]{:S(2)}) collective-permute-start(f32[3,8,128]{2,1,0:T(8,128)S(1)} %get-tuple-element.24), channel_id=1, source_target_pairs={{0,1},{1,0},{2,3},{3,2},{4,5},{5,4},{6,7},{7,6},{8,9},{9,8},{10,11... | collective-permute-start | bytes 36872 | tf_op jit(solution)/shard_map/ppermute | solution.py:481
  6.4 3.4 %collective-permute-start.2 = (f32[3,8,128]{2,1,0:T(8,128)S(1)}, f32[3,8,128]{2,1,0:T(8,128)S(1)}, u32[]{:S(2)}, u32[]{:S(2)}) collective-permute-start(f32[3,8,128]{2,1,0:T(8,128)S(1)} %collective-permute-done.1), channel_id=1, source_target_pairs={{0,2},{1,0},{2,4},{3,1},{4,6},{5,3},{6,8},{7,5},{8,10},{9,7},{10,1... | collective-permute-start | bytes 36872 | tf_op jit(solution)/shard_map/ppermute | solution.py:483
  10.5 14.8 %collective-permute-start.5 = (f32[320,256]{1,0:T(8,128)S(1)}, f32[320,256]{1,0:T(8,128)S(1)}, u32[]{:S(2)}, u32[]{:S(2)}) collective-permute-start(f32[320,256]{1,0:T(8,128)S(1)} %get-tuple-element.28), channel_id=1, source_target_pairs={{0,2},{1,3},{2,0},{3,1},{4,6},{5,7},{6,4},{7,5},{8,10},{9,11},{10,... | collective-permute-start | bytes 983048 | tf_op jit(solution)/shard_map/ppermute | solution.py:494
  12.3 12.9 %collective-permute-start.4 = (f32[200,256]{1,0:T(8,128)S(1)}, f32[200,256]{1,0:T(8,128)S(1)}, u32[]{:S(2)}, u32[]{:S(2)}) collective-permute-start(f32[200,256]{1,0:T(8,128)S(1)} %collective-permute-done.first2_ref), channel_id=1, source_target_pairs={{0,1},{1,0},{2,3},{3,2},{4,5},{5,4},{6,7},{7,6},{8,9},{9,8},{10,11... | collective-permute-start | bytes 614408 | tf_op jit(solution)/shard_map/ppermute | solution.py:495
  12.3 12.9 %collective-permute-start.6 = (f32[520,256]{1,0:T(8,128)S(1)}, f32[520,256]{1,0:T(8,128)S(1)}, u32[]{:S(2)}, u32[]{:S(2)}) collective-permute-start(f32[520,256]{1,0:T(8,128)S(1)} %get-tuple-element.35.mine_ref), channel_id=1, source_target_pairs={{0,1},{1,0},{2,3},{3,2},{4,5},{5,4},{6,7},{7,6},{8,9},{9,8},{10,11... | collective-permute-start | bytes 1597448 | tf_op jit(solution)/shard_map/ppermute | solution.py:492
  25.2 1.6 %collective-permute-start.7 = (f32[320,256]{1,0:T(8,128)S(1)}, f32[320,256]{1,0:T(8,128)S(1)}, u32[]{:S(2)}, u32[]{:S(2)}) collective-permute-start(f32[320,256]{1,0:T(8,128)S(1)} %collective-permute-done.5.second2_ref), channel_id=1, source_target_pairs={{0,1},{1,0},{2,3},{3,2},{4,5},{5,4},{6,7},{7,6},{8,9},{9,8},{10,11... | collective-permute-start | bytes 983048 | tf_op jit(solution)/shard_map/ppermute | solution.py:507

commit v5 on v4

--- a/solution.py
+++ b/solution.py
@@ -120,8 +120,8 @@
 
 
 def start_kernel(
-    rhs_any, weights_any, order_any, smoother_any, near_ref, onward_ref, own_ref,
-    rhs_ref, weights_ref, order_ref, smoother_ref, high_ref, low_ref, sem_ref,
+    rhs_any, weights_any, order_any, smoother_any, near_ref, onward_ref, own_ref, smoother_ref,
+    rhs_ref, weights_ref, order_ref, high_ref, low_ref, sem_ref,
 ):
     copies = fetch(
         sem_ref, (smoother_any, smoother_ref), (rhs_any, rhs_ref), (weights_any, weights_ref), (order_any, order_ref)
@@ -133,8 +133,8 @@
 
 def start_pack_kernel(
     rhs_any, weights_any, order_any, smoother_any, rows_any, values_any, inverse_any,
-    near_ref, onward_ref, own_ref, packed_ref, first_ref, second_ref,
-    rhs_ref, weights_ref, order_ref, smoother_ref, rows_ref, values_ref, inverse_ref, high_ref, low_ref, sem_ref,
+    near_ref, onward_ref, own_ref, smoother_ref, packed_ref, first_ref, second_ref,
+    rhs_ref, weights_ref, order_ref, rows_ref, values_ref, inverse_ref, high_ref, low_ref, sem_ref,
 ):
     copies = fetch(
         sem_ref, (smoother_any, smoother_ref), (rhs_any, rhs_ref), (weights_any, weights_ref), (order_any, order_ref),
@@ -147,12 +147,12 @@
         copy.wait()
     own_blocks, nbrs = rows_ref.shape
     deep, width = values_ref.shape
-    lane, block = iota((own_blocks, width), 1), iota((own_blocks, width), 0)
-    rows = jnp.zeros((own_blocks, width), f32)
-    for k in range(nbrs):
-        here = (lane // 32 == k) & (lane % 16 == block)
-        rows = jnp.where(here, rows_ref[:, k : k + 1].astype(f32), rows)
-    rows = jnp.broadcast_to(jnp.sum(rows, axis=0, keepdims=True), (8, width))
+    at, slot = iota((8, nbrs), 1), iota((8, nbrs), 0)
+    block = iota((8, width), 1) // CELLS
+    rows = jnp.zeros((8, width), f32)
+    for j in range(own_blocks):
+        targets = jnp.where(at == slot, rows_ref[j : j + 1, :].astype(f32), 0.0)
+        rows = jnp.where(block == j, jnp.sum(targets, axis=1, keepdims=True), rows)
     inverse = inverse_ref[...].astype(f32)
     for ref in (packed_ref, first_ref):
         ref[pl.ds(0, 8), :] = rows
@@ -181,8 +181,8 @@
 
 
 def prepare_kernel(
-    counts_ref, own_ref, rhs_any, reaction_any, columns_any, fine_any, selected_ref, weighed_ref, local_ref,
-    rhs_ref, reaction_ref, columns_ref, fine_ref, wide_ref, sem_ref,
+    counts_ref, own_ref, rhs_any, reaction_any, columns_any, fine_any, selected_ref, weighed_ref, local_ref, fine_ref,
+    rhs_ref, reaction_ref, columns_ref, wide_ref, sem_ref,
 ):
     copies = fetch(
         sem_ref, (fine_any, fine_ref), (columns_any, columns_ref), (rhs_any, rhs_ref), (reaction_any, reaction_ref)
@@ -258,47 +258,71 @@
     result_ref[...] = mine + apply_smoother(local_ref[2] - image, smoother_ref, high_ref, low_ref)
 
 
-def solve_kernel(
-    devices, gathered_ref, near_ref, far_ref, own_ref, selected_ref, local_ref,
-    mine_ref, beside_ref, first2_ref, second2_ref, first3_ref, second3_ref, fine_any, smoother_any,
-    out_any, correction_any,
-    blocks_ref, inverse_ref, result_ref, correction_ref,
-    fine_ref, smoother_ref, picked_ref, high_ref, low_ref, sem_ref, out_sem_ref,
-):
-    copies = fetch(sem_ref, (fine_any, fine_ref), (smoother_any, smoother_ref))
-    me = lax.axis_index("coarse")
-    parts = blocks_ref.shape[0]
-    deep, width = blocks_ref.shape[1:]
-    nbrs = deep // CELLS
+def place(group, own_blocks):
+    return jnp.bitwise_xor(group // own_blocks, lax.axis_index("coarse")) * own_blocks + group % own_blocks
+
+
+def pairs_of(x):
+    half = x.shape[0] // 2
+    return jnp.concatenate([x[:half], x[half:]], axis=1)
+
+
+def masked_rows(x, mask_lists, pair_at, held_ref):
+    pairs = x.shape[0]
+    high, low = split(x)
+    held_ref[pl.ds(0, pairs), :] = high.astype(f32)
+    held_ref[pl.ds(pairs, pairs), :] = low.astype(f32)
+    parts = []
+    for part in range(2):
+        rows = [
+            jnp.broadcast_to(held_ref[pl.ds(part * pairs + p, 1), :], (2 * pairs, LANES)).astype(bf16)
+            for p in range(pairs)
+        ]
+        parts.append(rows)
+    return jnp.concatenate(
+        [
+            jnp.concatenate([mask * rows[pair_at(c)] for c, mask in enumerate(masks)], axis=1)
+            for masks in mask_lists
+            for rows in parts
+        ],
+        axis=0,
+    )
+
+
+def inverse_product(x, inverse_ref, held_ref):
+    pairs = x.shape[0]
+    groups = 2 * pairs
+    row, lane = iota((groups, LANES), 0), iota((groups, LANES), 1)
+    masks = [((row % pairs == p) & (row // pairs == lane // CELLS)).astype(bf16) for p in range(pairs)]
+    sums = dot(masked_rows(x, [masks], lambda c: c, held_ref), inverse_ref[...])
+    return pairs_of(sums[:groups] + sums[groups:])
+
+
+def slot_pair(rows_ref, first, count):
+    turned = rows_ref[pl.ds(first, CELLS * count), :].astype(bf16).T
+    return turned if count == 2 else jnp.concatenate([turned, jnp.zeros_like(turned)], axis=1)
+
+
+def first_sweep_kernel(
+    gathered_ref, mine_ref, beside_ref, first2_ref, second2_ref, first3_ref,
+    side_ref, begun_ref, inverse_ref, target_ref, blocks_ref, held_ref,
+):
+    part_refs = (mine_ref, beside_ref, first2_ref, first3_ref)
+    width = mine_ref.shape[1]
     own_blocks = width // CELLS
-    groups = parts * own_blocks
-    unknowns = groups * CELLS
+    pairs = side_ref.shape[0]
+    groups = 2 * pairs
     base = 8 + CELLS
-    early = first2_ref.shape[0] - base
-    row_refs = (mine_ref, beside_ref, first2_ref, first3_ref)
-    for i, ref in enumerate((mine_ref, beside_ref)):
-        blocks_ref[i] = ref[pl.ds(base, deep), :].astype(bf16)
-    for i, first, second in ((2, first2_ref, second2_ref), (3, first3_ref, second3_ref)):
-        blocks_ref[i, pl.ds(0, early), :] = first[pl.ds(base, early), :].astype(bf16)
-        blocks_ref[i, pl.ds(early, deep - early), :] = second[...].astype(bf16)
-    for i, ref in enumerate(row_refs):
-        inverse_ref[i] = ref[pl.ds(8, CELLS), :].astype(bf16)
-
-    def place(group):
-        return jnp.bitwise_xor(group // own_blocks, me) * own_blocks + group % own_blocks
-
-    lane = iota((1, width), 1)
-    target = jnp.zeros((1, width), f32)
-    for i, ref in enumerate(row_refs):
-        rows = ref[pl.ds(0, 8), :][0:1, :]
-        rows = jnp.where((lane % 16 < own_blocks) & (lane < 32 * nbrs), rows, 0.0)
-        target = target + (rows if i == 0 else pltpu.roll(rows, i * own_blocks, 1))
-    target = place(target.astype(i32))
-    scatter = ((iota((groups, width), 0) == target) & (lane < 32 * nbrs)).astype(bf16)[:, : 32 * nbrs]
+    nbrs = (mine_ref.shape[0] - base) // CELLS
+    early = (first2_ref.shape[0] - base) // CELLS
+    for i, ref in enumerate(part_refs):
+        inverse_ref[pl.ds(i * width, width), :] = ref[pl.ds(8, CELLS), :].astype(bf16).T
 
     gathered = gathered_ref[...]
     devs = gathered.shape[0]
     lane = iota((8, LANES), 1)
+    row = iota((groups, LANES), 0)
+    number = 2 * (row % pairs) + row // pairs
     lefts, rights = [], []
     for start in range(0, devs, 32):
         value = jnp.zeros((8, LANES), f32)
@@ -309,43 +333,67 @@
             value = jnp.where(here, pltpu.roll(piece, 32 * i, 1) if i else piece, value)
             order = jnp.where(here, pltpu.roll(piece, (32 * i + 96) % LANES, 1) if i != 1 else piece, order)
         order = order.astype(i32)
-        group, unit = place(order // CELLS), order % CELLS
+        group, unit = place(order // CELLS, own_blocks), order % CELLS
         for s in range(8):
-            left = jnp.where(iota((groups, LANES), 0) == group[s : s + 1], value[s : s + 1], 0.0)
+            left = jnp.where(number == group[s : s + 1], value[s : s + 1], 0.0)
             lefts.append(jnp.concatenate(split(left), axis=0))
             rights.append((iota((CELLS, LANES), 0) == unit[s : s + 1]).astype(bf16))
-    right_side = dot_t(jnp.concatenate(lefts, axis=1), jnp.concatenate(rights, axis=1))
-    right_side = right_side[:groups] + right_side[groups:]
-
-    own_block = iota((groups, unknowns), 1) // CELLS == iota((groups, unknowns), 0)
-
-    def spread(x):
-        wide = jnp.concatenate([x] * (LANES // CELLS), axis=1)
-        wide = jnp.concatenate([wide] * (unknowns // LANES), axis=1)
-        return jnp.concatenate(split(jnp.where(own_block, wide, 0.0)), axis=0)
-
-    def product(x, ref):
-        wide = spread(x)
-        total = None
-        for i in range(parts):
-            term = dot_t(wide[:, i * width : (i + 1) * width], ref[i])
-            total = term if total is None else total + term
-        return total[:groups] + total[groups:]
-
-    correction = product(right_side, inverse_ref)
+    side = dot_t(jnp.concatenate(lefts, axis=1), jnp.concatenate(rights, axis=1))
+    side = pairs_of(side[:groups] + side[groups:])
+    side_ref[...] = side
+    begun_ref[...] = inverse_product(side, inverse_ref, held_ref)
+
+    row = iota((groups, width), 0)
+    number = 2 * (row % pairs) + row // pairs
+    twos = (nbrs + 1) // 2
+    half = twos * width * len(part_refs)
+    for i, ref in enumerate(part_refs):
+        targets = place(ref[pl.ds(0, 8), :].astype(i32), own_blocks)
+        for k in range(2 * twos):
+            cols = pl.ds(k % 2 * half + (i * twos + k // 2) * width, width)
+            chosen = number == targets[k : k + 1] if k < nbrs else jnp.zeros(row.shape, jnp.bool_)
+            target_ref[:, cols] = chosen.astype(bf16)
+        for q in range(twos):
+            rows = pl.ds((i * twos + q) * width, width)
+            count = min(2, nbrs - 2 * q)
+            if i < 2 or 2 * q < early:
+                blocks_ref[rows, :] = slot_pair(ref, base + 2 * q * CELLS, count)
+            elif i == 2:
+                blocks_ref[rows, :] = slot_pair(second2_ref, (2 * q - early) * CELLS, count)
+
+
+def solve_kernel(
+    devices, side_ref, begun_ref, inverse_ref, target_ref, blocks_ref, near_ref, far_ref, own_ref, selected_ref,
+    local_ref, second3_ref, fine_ref, smoother_ref,
+    out_any, correction_any,
+    last_ref, held_ref, result_ref, correction_ref,
+    picked_ref, high_ref, low_ref, out_sem_ref,
+):
+    width = second3_ref.shape[1]
+    own_blocks = width // CELLS
+    groups, half = target_ref.shape[0], target_ref.shape[1] // 2
+    pairs = groups // 2
+    late = second3_ref.shape[0] // CELLS
+    for q in range(0, late, 2):
+        last_ref[pl.ds(q // 2 * width, width), :] = slot_pair(second3_ref, q * CELLS, min(2, late - q))
+    per_part = half // LANES // (groups // own_blocks)
+    per_block = width // LANES
+
+    def pair_at(chunk):
+        return chunk // per_part * per_block + chunk % per_block
+
+    side = side_ref[...]
+    correction = begun_ref[...]
+    split_at = blocks_ref.shape[0]
     for _ in range(SWEEPS - 1):
-        sums = product(correction, blocks_ref)
-        pieces = []
-        for k in range(nbrs):
-            pieces += split(sums[:, k * CELLS : (k + 1) * CELLS])
-        image = jnp.zeros((groups, CELLS), f32)
-        high, low = pieces[0::2], pieces[1::2]
-        stacked = jnp.concatenate([p for pair in zip(high, low) for p in pair], axis=0)
-        image = dot(scatter, stacked)
-        correction = correction + product(right_side - image, inverse_ref)
-    for r in range(own_blocks // 2):
-        both = [correction[2 * r : 2 * r + 1], correction[2 * r + 1 : 2 * r + 2]]
-        correction_ref[r : r + 1, :] = jnp.concatenate(both, axis=1)
+        masks = [[target_ref[:, pl.ds(t * half + c, LANES)] for c in range(0, half, LANES)] for t in range(2)]
+        spread = masked_rows(correction, masks, pair_at, held_ref)
+        sums = dot(spread[:, :split_at], blocks_ref[...]) + dot(spread[:, split_at:], last_ref[...])
+        image = sums[:groups] + sums[groups : 2 * groups]
+        other = sums[2 * groups : 3 * groups] + sums[3 * groups :]
+        image = pairs_of(image[:, :CELLS] + other[:, CELLS:])
+        correction = correction + inverse_product(side - image, inverse_ref, held_ref)
+    correction_ref[...] = correction[: own_blocks // 2]
     correction_copy = pltpu.make_async_copy(correction_ref, correction_any, out_sem_ref.at[0])
     correction_copy.start()
 
@@ -353,12 +401,12 @@
     rows = order.shape[0]
     unit = jnp.concatenate([order[:, :CELLS], order[:, CELLS:]], axis=0)
     chosen = (iota(unit.shape, 1) == unit % CELLS).astype(bf16)
-    values = dot_t(chosen, jnp.concatenate(split(correction), axis=0))
-    group = place(unit[:, : 2 * groups] // CELLS)
+    by_block = jnp.concatenate([correction[:, :CELLS], correction[:, CELLS:]], axis=0)
+    values = dot_t(chosen, jnp.concatenate(split(by_block), axis=0))
+    group = place(unit[:, : 2 * groups] // CELLS, own_blocks)
+    group = group // 2 + group % 2 * pairs
     values = jnp.sum(jnp.where(iota(values.shape, 1) % groups == group, values, 0.0), axis=1, keepdims=True)
     corr = by_half([values[:rows], values[rows:]], (rows, LANES))
-    for copy in copies:
-        copy.wait()
     finish(corr, near_ref, far_ref, own_ref, local_ref, devices, selected_ref, fine_ref, smoother_ref, result_ref,
            picked_ref, high_ref, low_ref)
     result_copy = pltpu.make_async_copy(result_ref, out_any, out_sem_ref.at[1])
@@ -368,12 +416,9 @@
 
 
 def finish_kernel(
-    devices, corr_ref, near_ref, far_ref, own_ref, selected_ref, local_ref, fine_any, smoother_any, result_ref,
-    fine_ref, smoother_ref, picked_ref, high_ref, low_ref, sem_ref,
-):
-    copies = fetch(sem_ref, (fine_any, fine_ref), (smoother_any, smoother_ref))
-    for copy in copies:
-        copy.wait()
+    devices, corr_ref, near_ref, far_ref, own_ref, selected_ref, local_ref, fine_ref, smoother_ref, result_ref,
+    picked_ref, high_ref, low_ref,
+):
     finish(corr_ref[...], near_ref, far_ref, own_ref, local_ref, devices, selected_ref, fine_ref, smoother_ref,
            result_ref, picked_ref, high_ref, low_ref)
 
@@ -439,22 +484,22 @@
     rhs, reaction, weights = (x.reshape(pairs, LANES) for x in (rhs, reaction, weights))
     rows = pairs + 2 * HALO_ROWS
     vector = pltpu.VMEM((pairs, LANES), f32)
-    fine_buffer = pltpu.VMEM(fine_values.shape, bf16)
-    smoother_buffer = pltpu.VMEM(smoother.shape, bf16)
     products = [pltpu.VMEM((CELLS, cells), bf16)] * 2
     picked = pltpu.VMEM((nbrs * pairs, LANES), f32)
     copies = pltpu.SemaphoreType.DMA((4,))
     edge = shape_of(3, HALO_ROWS, LANES)
 
     copied = parts == 4 and devices % 32 == 0 and devices <= 64
-    start_shapes = (edge, edge, shape_of(3, pairs, LANES))
+    start_shapes = (
+        edge, edge, shape_of(3, pairs, LANES), jax.ShapeDtypeStruct(smoother.shape, bf16)
+    )
     start_ins = (rhs, weights, coarse_order.reshape(1, aggs), smoother)
-    start_scratch = [vector, vector, pltpu.VMEM((1, aggs), i32), smoother_buffer]
+    start_scratch = [vector, vector, pltpu.VMEM((1, aggs), i32)]
     if copied:
         deep = coarse_values.shape[0] * CELLS
         width = coarse_inverse.shape[1]
         early = EARLY * CELLS
-        near, onward, own, packed, first, second = call(
+        near, onward, own, smoother_here, packed, first, second = call(
             start_pack_kernel,
             (*start_shapes, shape_of(8 + CELLS + deep, width), shape_of(8 + CELLS + early, width),
              shape_of(deep - early, width)),
@@ -468,7 +513,7 @@
         across = [(c, c ^ 2) for c in range(parts)]
         first2 = lax.ppermute(first, "coarse", across)
     else:
-        near, onward, own = call(start_kernel, start_shapes, "aaaa", scratch=[*start_scratch, *products, copies])(
+        near, onward, own, smoother_here = call(start_kernel, start_shapes, "aaaa", scratch=[*start_scratch, *products, copies])(
             *start_ins
         )
 
@@ -481,11 +526,12 @@
     near = lax.ppermute(near, BOTH, partner)
 
     far = lax.ppermute(onward, BOTH, chain)
-    selected, weighed, local = call(
+    selected, weighed, local, fine_here = call(
         prepare_kernel,
-        (jax.ShapeDtypeStruct((aggs * nbrs, 4 * rows), bf16), shape_of(nbrs * pairs, 8, LANES), shape_of(4, pairs, LANES)),
+        (jax.ShapeDtypeStruct((aggs * nbrs, 4 * rows), bf16), shape_of(nbrs * pairs, 8, LANES), shape_of(4, pairs, LANES),
+         jax.ShapeDtypeStruct(fine_values.shape, bf16)),
         "svaaaa",
-        scratch=[vector, vector, pltpu.VMEM(fine_columns.shape, i32), fine_buffer, pltpu.VMEM((CELLS, cells), f32), copies],
+        scratch=[vector, vector, pltpu.VMEM(fine_columns.shape, i32), pltpu.VMEM((CELLS, cells), f32), copies],
     )(pit_counts, own, rhs, reaction, fine_columns, fine_values)
 
     if copied:
@@ -498,23 +544,34 @@
         functools.partial(residual_kernel, devices), shape_of(devices, LANES), "vvvvvv", scratch=[picked]
     )(near, far, own, selected, weighed, local)
 
-    finish_scratch = [ fine_buffer, smoother_buffer, picked, *products, copies]
+    finish_scratch = [picked, *products]
     common = (near, far, own, selected, local)
-    fetched = (fine_values, smoother)
+    fetched = (fine_here, smoother_here)
     if copied:
         gathered = lax.all_to_all(sent, BOTH, 0, 0, tiled=True)
         first3, second2, gathered = lax.optimization_barrier((first3, second2, gathered))
-        pieces = (packed, beside, first2, second2, first3, lax.ppermute(second2, "coarse", swap))
+        second3 = lax.ppermute(second2, "coarse", swap)
+        unknowns = parts * width
+        groups = unknowns // CELLS
+        twos, late = (nbrs + 1) // 2, (nbrs - EARLY + 1) // 2
+        begun = call(
+            first_sweep_kernel,
+            (shape_of(unknowns // LANES, LANES), shape_of(unknowns // LANES, LANES),
+             jax.ShapeDtypeStruct((unknowns, CELLS), bf16), jax.ShapeDtypeStruct((groups, 2 * twos * unknowns), bf16),
+             jax.ShapeDtypeStruct((twos * unknowns - late * width, LANES), bf16)),
+            "vvvvvv",
+            scratch=[pltpu.VMEM((groups, LANES), f32)],
+        )(gathered, packed, beside, first2, second2, first3)
         result, correction = call(
             functools.partial(solve_kernel, devices),
             (shape_of(pairs, LANES), shape_of(width // LANES, LANES)),
-            "vvvvvv" + "vvvvvv" + "aa",
+            "vvvvv" + "vvvvv" + "vvv",
             outs="aa",
             scratch=[
-                pltpu.VMEM((parts, deep, width), bf16), pltpu.VMEM((parts, CELLS, width), bf16),
-                vector, pltpu.VMEM((width // LANES, LANES), f32), *finish_scratch, pltpu.SemaphoreType.DMA((2,)),
+                pltpu.VMEM((late * width, LANES), bf16), pltpu.VMEM((groups, LANES), f32), vector,
+                pltpu.VMEM((width // LANES, LANES), f32), *finish_scratch, pltpu.SemaphoreType.DMA((2,)),
             ],
-        )(gathered, *common, *pieces, *fetched)
+        )(*begun, *common, second3, *fetched)
         correction = correction.reshape(-1)
     else:
         correction, everywhere = coarse_by_parts(
@@ -526,7 +583,7 @@
         order = jnp.concatenate([low, own[2], high], axis=0).astype(i32)
         corr = jnp.repeat(everywhere[order[:, ::CELLS]], CELLS, axis=1)
         result = call(
-            functools.partial(finish_kernel, devices), shape_of(pairs, LANES), "vvvvvvaa", scratch=finish_scratch
+            functools.partial(finish_kernel, devices), shape_of(pairs, LANES), "vvvvvvvv", scratch=finish_scratch
         )(corr, *common, *fetched)
     return result.reshape(-1), correction
 

time: 32.5 us -> 31.6 us (0.972)
  waiting for transfers between devices: 3.47 us -> 2.83 us
    ppermute x1, waiting for transfers between devices: 1.61 us -> 0.97 us  [shards(): second3 = lax.ppermute(second2, 'coarse', swap)]
    pallas_call x4 -> x5, Pallas kernels: 9.49 us -> 9.18 us  [placed(): run(*(pltpu.with_memory_space_constraint(x, pltpu.HBM) if c == 'a' else x...]
  transfers between devices with their start and end apart: 8 -> 8, of which waited for: 4 -> 4; matrix products, arithmetic and copies ran while one was open for 0% -> 0% of each run, Pallas kernels for 8% -> 10%
where the time goes in v5:
time: 31.6 us; the launch traced here: 31.4 us
  blocking collectives  12 us (38%)
  Pallas kernels  9.18 us (29%)
  starting transfers between devices  6.01 us (19%)
  waiting for transfers between devices  2.83 us (9%)
  between operations  1.34 us (4%)
    all_to_all x1, blocking collectives, shards(): gathered = lax.all_to_all(sent, BOTH, 0, 0, tiled=True)  12 us
    pallas_call x5, Pallas kernels, placed(): run(*(pltpu.with_memory_space_constraint(x, pltpu.HBM) if c == 'a' else x...  9.18 us
    ppermute x1, starting transfers between devices, shards(): first2 = lax.ppermute(first, 'coarse', across)  3.03 us
    ppermute x1, starting transfers between devices, shards(): second2 = lax.ppermute(second, 'coarse', across)  1.88 us
    ppermute x1, waiting for transfers between devices, shards(): second3 = lax.ppermute(second2, 'coarse', swap)  0.97 us
    ppermute x1, waiting for transfers between devices, shards(): onward = lax.ppermute(onward, BOTH, partner)  0.67 us
  transfers between devices with their start and end apart: 8, of which 4 were waited for; matrix products, arithmetic and copies ran while one was open for 0% of the time, Pallas kernels for 10%

profile of v5, /device:TPU:0, one launch (start us, length us, event | category | flops | bytes accessed | tf_op | source)
XLA Modules:
  0.0 31.4 jit_solution(16955013685641836983)
XLA Ops:
  0.6 1.6 %shard_map.122 = (f32[3,8,128]{2,1,0:T(8,128)S(1)}, f32[3,8,128]{2,1,0:T(8,128)S(1)}, f32[3,16,128]{2,1,0:T(8,128)S(1)}, bf16[64,2048]{1,0:T(8,128)(2,1)S(1)}, f...) custom-call(f32[16,128]{1,0:T(8,128)} %bitcast.15, f32[16,128]{1,0:T(8,128)} %bitcast.17, ...), custom_call_target="tpu_custom_call" | custom-call | tf_op jit(solution)/shard_map/pallas_call | solution.py:440
  2.2 3.0 %collective-permute-start = (f32[200,256]{1,0:T(8,128)S(1)}, f32[200,256]{1,0:T(8,128)S(1)}, u32[]{:S(2)}, u32[]{:S(2)}) collective-permute-start(f32[200,256]{1,0:T(8,128)S(1)} %get-tuple-element.28), channel_id=1, source_target_pairs={{0,2},{1,3},{2,0},{3,1},{4,6},{5,7},{6,4},{7,5},{8,10},{9,11},{10,... | collective-permute-start | bytes 614408 | tf_op jit(solution)/shard_map/ppermute | solution.py:514
  5.2 0.0 collective-permute-start.1
  5.2 0.5 %collective-permute-start.3 = (f32[3,8,128]{2,1,0:T(8,128)S(1)}, f32[3,8,128]{2,1,0:T(8,128)S(1)}, u32[]{:S(2)}, u32[]{:S(2)}) collective-permute-start(f32[3,8,128]{2,1,0:T(8,128)S(1)} %get-tuple-element.31), channel_id=1, source_target_pairs={{0,1},{1,0},{2,3},{3,2},{4,5},{5,4},{6,7},{7,6},{8,9},{9,8},{10,11... | collective-permute-start | bytes 36872 | tf_op jit(solution)/shard_map/ppermute | solution.py:526
  5.8 0.7 %collective-permute-done.1 = f32[3,8,128]{2,1,0:T(8,128)S(1)} collective-permute-done((f32[3,8,128]{2,1,0:T(8,128)S(1)}, f32[3,8,128]{2,1,0:T(8,128)S(1)}, u32[]{:S(2)}, u32[]{:S(2)}) %collective-permute-start.1) | collective-permute-done | bytes 12320 | tf_op jit(solution)/shard_map/ppermute | solution.py:525
  6.4 0.1 collective-permute-start.2
  7.2 2.1 %shard_map.123 = (bf16[224,128]{1,0:T(8,128)(2,1)S(1)}, f32[112,8,128]{2,1,0:T(8,128)S(1)}, f32[4,16,128]{2,1,0:T(8,128)S(1)}, bf16[7,64,2048]{2,1,0:T(8,128)(2,1)S(1)}) custom-call(s32[1]{0:T(128)S(6)} %copy.14.counts_ref, f32[3,16,128]{2,1,0:T(8,128)S(1)} %get-tuple-element.32.own_ref, f32[16,128]{1,0:T(8,128)} %bitcast.16, f32[16,128]{1,0:T(8,128)} %bitcast.18, ...), custom_call_target="tpu_custom_call" | custom-call | tf_op jit(solution)/shard_map/pallas_call | solution.py:440
  9.3 0.0 collective-permute-done.3.near_ref
  9.3 0.6 %collective-permute-done.2.far_ref = f32[3,8,128]{2,1,0:T(8,128)S(1)} collective-permute-done((f32[3,8,128]{2,1,0:T(8,128)S(1)}, f32[3,8,128]{2,1,0:T(8,128)S(1)}, u32[]{:S(2)}, u32[]{:S(2)}) %collective-permute-start.2) | collective-permute-done | bytes 12320 | tf_op jit(solution)/shard_map/ppermute | solution.py:528
  9.8 0.6 %collective-permute-done.first2_ref = f32[200,256]{1,0:T(8,128)S(1)} collective-permute-done((f32[200,256]{1,0:T(8,128)S(1)}, f32[200,256]{1,0:T(8,128)S(1)}, u32[]{:S(2)}, u32[]{:S(2)}) %collective-permute-start) | collective-permute-done | bytes 204832 | tf_op jit(solution)/shard_map/ppermute | solution.py:514
  10.4 1.9 %collective-permute-start.5 = (f32[320,256]{1,0:T(8,128)S(1)}, f32[320,256]{1,0:T(8,128)S(1)}, u32[]{:S(2)}, u32[]{:S(2)}) collective-permute-start(f32[320,256]{1,0:T(8,128)S(1)} %get-tuple-element.35), channel_id=1, source_target_pairs={{0,2},{1,3},{2,0},{3,1},{4,6},{5,7},{6,4},{7,5},{8,10},{9,11},{10,... | collective-permute-start | bytes 983048 | tf_op jit(solution)/shard_map/ppermute | solution.py:540
  12.3 0.0 collective-permute-start.4
  12.3 0.5 %collective-permute-start.6 = (f32[520,256]{1,0:T(8,128)S(1)}, f32[520,256]{1,0:T(8,128)S(1)}, u32[]{:S(2)}, u32[]{:S(2)}) collective-permute-start(f32[520,256]{1,0:T(8,128)S(1)} %get-tuple-element.42.mine_ref), channel_id=1, source_target_pairs={{0,1},{1,0},{2,3},{3,2},{4,5},{5,4},{6,7},{7,6},{8,9},{9,8},{10,11... | collective-permute-start | bytes 1597448 | tf_op jit(solution)/shard_map/ppermute | solution.py:538
  12.8 0.4 %shard_map.124 = f32[32,128]{1,0:T(8,128)S(1)} custom-call(f32[3,8,128]{2,1,0:T(8,128)S(1)} %collective-permute-done.3.near_ref, f32[3,8,128]{2,1,0:T(8,128)S(1)} %collective-permute-done.2.far_ref, f32[3,16,128]{2,1,0:T(8,128)S(1)} %get-tuple-element.32.own_ref, bf16[224,128]{1,0:T(8,128)(2,1)S(1)} %get-tuple-element.38.selected_ref, ...), custom_call_target="tpu_custom_call" | custom-call | tf_op jit(solution)/shard_map/pallas_call | solution.py:440
  13.2 12.0 %all_to_all.12 = f32[32,1,128]{2,1,0:T(1,128)S(1)} all-to-all(f32[32,1,128]{2,1,0:T(1,128)S(1)} %bitcast.13), channel_id=1, replica_groups=mesh['fine'=8,'coarse'=4] {'fine','coarse'}, dimensions={0} | all-to-all | bytes 32768 | tf_op jit(solution)/shard_map/all_to_all | solution.py:551
  25.2 0.0 collective-permute-done.4.first3_ref
  25.2 0.0 collective-permute-done.5.second2_ref
  25.2 0.0 collective-permute-start.7
  25.2 0.0 collective-permute-done.6.beside_ref
  25.2 0.6 %shard_map.125 = (f32[8,128]{1,0:T(8,128)S(1)}, f32[8,128]{1,0:T(8,128)S(1)}, bf16[1024,64]{1,0:T(8,128)(2,1)S(1)}, bf16[16,8192]{1,0:T(8,128)(2,1)S(1)}, bf16[3328,128]{1,0:T(8,128)(2,1)S(1)}) custom-call(f32[32,128]{1,0:T(8,128)S(1)} %bitcast.12, f32[520,256]{1,0:T(8,128)S(1)} %get-tuple-element.42.mine_ref, ...), custom_call_target="tpu_custom_call" | custom-call | tf_op jit(solution)/shard_map/pallas_call | solution.py:440
  25.9 1.0 %collective-permute-done.7.second3_ref = f32[320,256]{1,0:T(8,128)S(1)} collective-permute-done((f32[320,256]{1,0:T(8,128)S(1)}, f32[320,256]{1,0:T(8,128)S(1)}, u32[]{:S(2)}, u32[]{:S(2)}) %collective-permute-start.7) | collective-permute-done | bytes 327712 | tf_op jit(solution)/shard_map/ppermute | solution.py:553
  26.8 4.5 %shard_map.126 = (f32[16,128]{1,0:T(8,128)}, f32[2,128]{1,0:T(2,128)}) custom-call(f32[8,128]{1,0:T(8,128)S(1)} %get-tuple-element.45.side_ref, f32[8,128]{1,0:T(8,128)S(1)} %get-tuple-element.46.begun_ref, bf16[1024,64]{1,0:T(8,128)(2,1)S(1)} %get-tuple-element.47.inverse_ref, bf16[16,8192]{1,0:T(8,128)(2,1)S(1)} %get-tuple-element.48.target_ref, ...), custom_call_target="tpu_custom_call" | custom-call | tf_op jit(solution)/shard_map/pallas_call | solution.py:440
Async XLA Ops:
  2.2 8.2 %collective-permute-start = (f32[200,256]{1,0:T(8,128)S(1)}, f32[200,256]{1,0:T(8,128)S(1)}, u32[]{:S(2)}, u32[]{:S(2)}) collective-permute-start(f32[200,256]{1,0:T(8,128)S(1)} %get-tuple-element.28), channel_id=1, source_target_pairs={{0,2},{1,3},{2,0},{3,1},{4,6},{5,7},{6,4},{7,5},{8,10},{9,11},{10,... | collective-permute-start | bytes 614408 | tf_op jit(solution)/shard_map/ppermute | solution.py:514
  5.2 1.2 %collective-permute-start.1 = (f32[3,8,128]{2,1,0:T(8,128)S(1)}, f32[3,8,128]{2,1,0:T(8,128)S(1)}, u32[]{:S(2)}, u32[]{:S(2)}) collective-permute-start(f32[3,8,128]{2,1,0:T(8,128)S(1)} %get-tuple-element.30), channel_id=1, source_target_pairs={{0,1},{1,0},{2,3},{3,2},{4,5},{5,4},{6,7},{7,6},{8,9},{9,8},{10,11... | collective-permute-start | bytes 36872 | tf_op jit(solution)/shard_map/ppermute | solution.py:525
  5.2 4.0 %collective-permute-start.3 = (f32[3,8,128]{2,1,0:T(8,128)S(1)}, f32[3,8,128]{2,1,0:T(8,128)S(1)}, u32[]{:S(2)}, u32[]{:S(2)}) collective-permute-start(f32[3,8,128]{2,1,0:T(8,128)S(1)} %get-tuple-element.31), channel_id=1, source_target_pairs={{0,1},{1,0},{2,3},{3,2},{4,5},{5,4},{6,7},{7,6},{8,9},{9,8},{10,11... | collective-permute-start | bytes 36872 | tf_op jit(solution)/shard_map/ppermute | solution.py:526
  6.4 3.4 %collective-permute-start.2 = (f32[3,8,128]{2,1,0:T(8,128)S(1)}, f32[3,8,128]{2,1,0:T(8,128)S(1)}, u32[]{:S(2)}, u32[]{:S(2)}) collective-permute-start(f32[3,8,128]{2,1,0:T(8,128)S(1)} %collective-permute-done.1), channel_id=1, source_target_pairs={{0,2},{1,0},{2,4},{3,1},{4,6},{5,3},{6,8},{7,5},{8,10},{9,7},{10,1... | collective-permute-start | bytes 36872 | tf_op jit(solution)/shard_map/ppermute | solution.py:528
  10.4 14.8 %collective-permute-start.5 = (f32[320,256]{1,0:T(8,128)S(1)}, f32[320,256]{1,0:T(8,128)S(1)}, u32[]{:S(2)}, u32[]{:S(2)}) collective-permute-start(f32[320,256]{1,0:T(8,128)S(1)} %get-tuple-element.35), channel_id=1, source_target_pairs={{0,2},{1,3},{2,0},{3,1},{4,6},{5,7},{6,4},{7,5},{8,10},{9,11},{10,... | collective-permute-start | bytes 983048 | tf_op jit(solution)/shard_map/ppermute | solution.py:540
  12.3 12.9 %collective-permute-start.4 = (f32[200,256]{1,0:T(8,128)S(1)}, f32[200,256]{1,0:T(8,128)S(1)}, u32[]{:S(2)}, u32[]{:S(2)}) collective-permute-start(f32[200,256]{1,0:T(8,128)S(1)} %collective-permute-done.first2_ref), channel_id=1, source_target_pairs={{0,1},{1,0},{2,3},{3,2},{4,5},{5,4},{6,7},{7,6},{8,9},{9,8},{10,11... | collective-permute-start | bytes 614408 | tf_op jit(solution)/shard_map/ppermute | solution.py:541
  12.3 12.9 %collective-permute-start.6 = (f32[520,256]{1,0:T(8,128)S(1)}, f32[520,256]{1,0:T(8,128)S(1)}, u32[]{:S(2)}, u32[]{:S(2)}) collective-permute-start(f32[520,256]{1,0:T(8,128)S(1)} %get-tuple-element.42.mine_ref), channel_id=1, source_target_pairs={{0,1},{1,0},{2,3},{3,2},{4,5},{5,4},{6,7},{7,6},{8,9},{9,8},{10,11... | collective-permute-start | bytes 1597448 | tf_op jit(solution)/shard_map/ppermute | solution.py:538
  25.2 1.6 %collective-permute-start.7 = (f32[320,256]{1,0:T(8,128)S(1)}, f32[320,256]{1,0:T(8,128)S(1)}, u32[]{:S(2)}, u32[]{:S(2)}) collective-permute-start(f32[320,256]{1,0:T(8,128)S(1)} %collective-permute-done.5.second2_ref), channel_id=1, source_target_pairs={{0,1},{1,0},{2,3},{3,2},{4,5},{5,4},{6,7},{7,6},{8,9},{9,8},{10,11... | collective-permute-start | bytes 983048 | tf_op jit(solution)/shard_map/ppermute | solution.py:553

commit v6 on v5

--- a/solution.py
+++ b/solution.py
@@ -73,15 +73,15 @@
     return jnp.where(lane < CELLS, picked[:count], picked[count:])
 
 
-def apply_fine(window, fine_ref, selected, picked_ref, high_ref, low_ref):
-    nbrs, _, width = fine_ref.shape
+def apply_smoothed_fine(window, products_ref, selected, picked_ref, high_ref, low_ref):
+    nbrs, _, width = products_ref.shape
     pairs = width // LANES
     picked_ref[...] = pick(window, selected)
     for p in range(pairs):
         cols = pl.ds(p * LANES, LANES)
         total = None
         for k in range(nbrs):
-            term = fine_ref[k, :, cols].astype(f32) * picked_ref[pl.ds(k * pairs + p, 1), :]
+            term = products_ref[k, :, cols] * picked_ref[pl.ds(k * pairs + p, 1), :]
             total = term if total is None else total + term
         high_ref[:, cols], low_ref[:, cols] = split(total)
     return cell_sums(high_ref, low_ref)
@@ -181,13 +181,14 @@
 
 
 def prepare_kernel(
-    counts_ref, own_ref, rhs_any, reaction_any, columns_any, fine_any, selected_ref, weighed_ref, local_ref, fine_ref,
-    rhs_ref, reaction_ref, columns_ref, wide_ref, sem_ref,
+    counts_ref, own_ref, rhs_any, reaction_any, columns_any, fine_any, smoother_ref, selected_ref, weighed_ref, local_ref,
+    products_ref, rhs_ref, reaction_ref, columns_ref, fine_ref, wide_ref, sem_ref,
 ):
     copies = fetch(
-        sem_ref, (fine_any, fine_ref), (columns_any, columns_ref), (rhs_any, rhs_ref), (reaction_any, reaction_ref)
-    )
-    for copy in copies[1:]:
+        sem_ref, (columns_any, columns_ref), (rhs_any, rhs_ref), (reaction_any, reaction_ref),
+        *((fine_any.at[k], fine_ref.at[k]) for k in range(fine_ref.shape[0])),
+    )
+    for copy in copies[:3]:
         copy.wait()
     pairs = rhs_ref.shape[0]
     nbrs, _, width = fine_ref.shape
@@ -196,8 +197,6 @@
     reaction = jnp.where(agg < counts_ref[0], reaction_ref[...], 0.0)
     local_ref[0] = weights * rhs_ref[...]
     local_ref[1] = weights * reaction
-    local_ref[2] = rhs_ref[...]
-    local_ref[3] = reaction
     selected_ref[...] = selection(columns_ref[...], pairs + 2 * HALO_ROWS, pairs)
     by_agg = jnp.concatenate([weights[:, :CELLS], weights[:, CELLS:]], axis=0)
     row, lane = iota((2 * pairs, width), 0), iota((2 * pairs, width), 1)
@@ -207,16 +206,29 @@
         term = lax.dot_general(part, member, (((0,), (0,)), ((), ())), preferred_element_type=f32)
         wide = term if wide is None else wide + term
     wide_ref[...] = wide
-    copies[0].wait()
-    for p in range(pairs):
-        cols = pl.ds(p * LANES, LANES)
-        scale = wide_ref[:, cols]
-        for k in range(nbrs):
-            term = fine_ref[k, :, cols].astype(f32) * scale
+    for k in range(nbrs):
+        copies[3 + k].wait()
+        for p in range(pairs):
+            cols = pl.ds(p * LANES, LANES)
+            term = fine_ref[k, :, cols].astype(f32) * wide_ref[:, cols]
             total = term[:8]
             for r in range(8, CELLS, 8):
                 total = total + term[r : r + 8]
             weighed_ref[k * pairs + p] = total
+    lane = iota((CELLS, LANES), 1)
+    for p in range(pairs):
+        cols = pl.ds(p * LANES, LANES)
+        left = smoother_ref[:, cols]
+        rights = []
+        for k in range(nbrs):
+            block = fine_ref[k, :, cols]
+            zero = jnp.zeros_like(block)
+            apart = [jnp.where(lane < CELLS, block, zero), jnp.where(lane < CELLS, zero, block)]
+            rights.append(jnp.concatenate(apart, axis=0))
+        both = dot(left, jnp.concatenate(rights, axis=1))
+        for k in range(nbrs):
+            product = both[:, k * LANES : (k + 1) * LANES]
+            products_ref[k, :, cols] = product if k else product + left.astype(f32) * reaction[p : p + 1]
 
 
 def residual_kernel(
@@ -247,15 +259,13 @@
     out_ref[...] = jnp.broadcast_to(row, out_ref.shape)
 
 
-def finish(corr, near_ref, far_ref, own_ref, local_ref, devices, selected_ref, fine_ref, smoother_ref, result_ref,
+def finish(corr, near_ref, far_ref, own_ref, devices, selected_ref, products_ref, result_ref,
            picked_ref, high_ref, low_ref):
     smoothed, weights, _ = window_of(near_ref, far_ref, own_ref, device_index(), devices)
     corrected = smoothed + weights * corr
-    pairs = own_ref.shape[1]
-    mine = corrected[HALO_ROWS : HALO_ROWS + pairs]
-    image = apply_fine(corrected, fine_ref, selected_ref[...], picked_ref, high_ref, low_ref)
-    image = image + local_ref[3] * mine
-    result_ref[...] = mine + apply_smoother(local_ref[2] - image, smoother_ref, high_ref, low_ref)
+    mine = corrected[HALO_ROWS : HALO_ROWS + own_ref.shape[1]]
+    image = apply_smoothed_fine(corrected, products_ref, selected_ref[...], picked_ref, high_ref, low_ref)
+    result_ref[...] = mine + (own_ref[0] - image)
 
 
 def place(group, own_blocks):
@@ -303,9 +313,22 @@
     return turned if count == 2 else jnp.concatenate([turned, jnp.zeros_like(turned)], axis=1)
 
 
+def target_rows(x, target_ref, start, stop, own_blocks, held_ref):
+    groups, half = target_ref.shape[0], target_ref.shape[1] // 2
+    per_part = half // LANES // (groups // own_blocks)
+    per_block = own_blocks // 2
+    masks = [[target_ref[:, pl.ds(t * half + c, LANES)] for c in range(start, stop, LANES)] for t in range(2)]
+
+    def pair_at(chunk):
+        chunk = chunk + start // LANES
+        return chunk // per_part * per_block + chunk % per_block
+
+    return masked_rows(x, masks, pair_at, held_ref)
+
+
 def first_sweep_kernel(
     gathered_ref, mine_ref, beside_ref, first2_ref, second2_ref, first3_ref,
-    side_ref, begun_ref, inverse_ref, target_ref, blocks_ref, held_ref,
+    side_ref, begun_ref, inverse_ref, target_ref, blocks_ref, sums_ref, held_ref,
 ):
     part_refs = (mine_ref, beside_ref, first2_ref, first3_ref)
     width = mine_ref.shape[1]
@@ -341,7 +364,8 @@
     side = dot_t(jnp.concatenate(lefts, axis=1), jnp.concatenate(rights, axis=1))
     side = pairs_of(side[:groups] + side[groups:])
     side_ref[...] = side
-    begun_ref[...] = inverse_product(side, inverse_ref, held_ref)
+    begun = inverse_product(side, inverse_ref, held_ref)
+    begun_ref[...] = begun
 
     row = iota((groups, width), 0)
     number = 2 * (row % pairs) + row // pairs
@@ -361,10 +385,12 @@
             elif i == 2:
                 blocks_ref[rows, :] = slot_pair(second2_ref, (2 * q - early) * CELLS, count)
 
+    sums_ref[...] = dot(target_rows(begun, target_ref, 0, blocks_ref.shape[0], own_blocks, held_ref), blocks_ref[...])
+
 
 def solve_kernel(
-    devices, side_ref, begun_ref, inverse_ref, target_ref, blocks_ref, near_ref, far_ref, own_ref, selected_ref,
-    local_ref, second3_ref, fine_ref, smoother_ref,
+    devices, side_ref, begun_ref, inverse_ref, target_ref, blocks_ref, sums_ref, near_ref, far_ref, own_ref, selected_ref,
+    second3_ref, products_ref,
     out_any, correction_any,
     last_ref, held_ref, result_ref, correction_ref,
     picked_ref, high_ref, low_ref, out_sem_ref,
@@ -376,19 +402,18 @@
     late = second3_ref.shape[0] // CELLS
     for q in range(0, late, 2):
         last_ref[pl.ds(q // 2 * width, width), :] = slot_pair(second3_ref, q * CELLS, min(2, late - q))
-    per_part = half // LANES // (groups // own_blocks)
-    per_block = width // LANES
-
-    def pair_at(chunk):
-        return chunk // per_part * per_block + chunk % per_block
-
     side = side_ref[...]
     correction = begun_ref[...]
     split_at = blocks_ref.shape[0]
-    for _ in range(SWEEPS - 1):
-        masks = [[target_ref[:, pl.ds(t * half + c, LANES)] for c in range(0, half, LANES)] for t in range(2)]
-        spread = masked_rows(correction, masks, pair_at, held_ref)
-        sums = dot(spread[:, :split_at], blocks_ref[...]) + dot(spread[:, split_at:], last_ref[...])
+    for sweep in range(SWEEPS - 1):
+        if sweep == 0:
+            sums = sums_ref[...]
+            spread = target_rows(correction, target_ref, split_at, half, own_blocks, held_ref)
+        else:
+            spread = target_rows(correction, target_ref, 0, half, own_blocks, held_ref)
+            sums = dot(spread[:, :split_at], blocks_ref[...])
+            spread = spread[:, split_at:]
+        sums = sums + dot(spread, last_ref[...])
         image = sums[:groups] + sums[groups : 2 * groups]
         other = sums[2 * groups : 3 * groups] + sums[3 * groups :]
         image = pairs_of(image[:, :CELLS] + other[:, CELLS:])
@@ -407,7 +432,7 @@
     group = group // 2 + group % 2 * pairs
     values = jnp.sum(jnp.where(iota(values.shape, 1) % groups == group, values, 0.0), axis=1, keepdims=True)
     corr = by_half([values[:rows], values[rows:]], (rows, LANES))
-    finish(corr, near_ref, far_ref, own_ref, local_ref, devices, selected_ref, fine_ref, smoother_ref, result_ref,
+    finish(corr, near_ref, far_ref, own_ref, devices, selected_ref, products_ref, result_ref,
            picked_ref, high_ref, low_ref)
     result_copy = pltpu.make_async_copy(result_ref, out_any, out_sem_ref.at[1])
     result_copy.start()
@@ -416,11 +441,10 @@
 
 
 def finish_kernel(
-    devices, corr_ref, near_ref, far_ref, own_ref, selected_ref, local_ref, fine_ref, smoother_ref, result_ref,
-    picked_ref, high_ref, low_ref,
-):
-    finish(corr_ref[...], near_ref, far_ref, own_ref, local_ref, devices, selected_ref, fine_ref, smoother_ref,
-           result_ref, picked_ref, high_ref, low_ref)
+    devices, corr_ref, near_ref, far_ref, own_ref, selected_ref, products_ref, result_ref, picked_ref, high_ref, low_ref,
+):
+    finish(corr_ref[...], near_ref, far_ref, own_ref, devices, selected_ref, products_ref, result_ref,
+           picked_ref, high_ref, low_ref)
 
 
 def call(kernel, out_shape, ins, outs=None, scratch=()):
@@ -526,17 +550,17 @@
     near = lax.ppermute(near, BOTH, partner)
 
     far = lax.ppermute(onward, BOTH, chain)
-    selected, weighed, local, fine_here = call(
+    selected, weighed, local, smoothed_fine = call(
         prepare_kernel,
-        (jax.ShapeDtypeStruct((aggs * nbrs, 4 * rows), bf16), shape_of(nbrs * pairs, 8, LANES), shape_of(4, pairs, LANES),
-         jax.ShapeDtypeStruct(fine_values.shape, bf16)),
-        "svaaaa",
-        scratch=[vector, vector, pltpu.VMEM(fine_columns.shape, i32), pltpu.VMEM((CELLS, cells), f32), copies],
-    )(pit_counts, own, rhs, reaction, fine_columns, fine_values)
+        (jax.ShapeDtypeStruct((aggs * nbrs, 4 * rows), bf16), shape_of(nbrs * pairs, 8, LANES), shape_of(2, pairs, LANES),
+         shape_of(*fine_values.shape)),
+        "svaaaav",
+        scratch=[vector, vector, pltpu.VMEM(fine_columns.shape, i32), pltpu.VMEM(fine_values.shape, bf16), pltpu.VMEM((CELLS, cells), f32), pltpu.SemaphoreType.DMA((3 + nbrs,))],
+    )(pit_counts, own, rhs, reaction, fine_columns, fine_values, smoother_here)
 
     if copied:
         beside = lax.ppermute(packed, "coarse", swap)
-        first2, second, far, near, selected = lax.optimization_barrier((first2, second, far, near, selected))
+        first2, second, far, near, selected, beside = lax.optimization_barrier((first2, second, far, near, selected, beside))
         second2 = lax.ppermute(second, "coarse", across)
         first3 = lax.ppermute(first2, "coarse", swap)
 
@@ -545,8 +569,7 @@
     )(near, far, own, selected, weighed, local)
 
     finish_scratch = [picked, *products]
-    common = (near, far, own, selected, local)
-    fetched = (fine_here, smoother_here)
+    common = (near, far, own, selected)
     if copied:
         gathered = lax.all_to_all(sent, BOTH, 0, 0, tiled=True)
         first3, second2, gathered = lax.optimization_barrier((first3, second2, gathered))
@@ -558,20 +581,20 @@
             first_sweep_kernel,
             (shape_of(unknowns // LANES, LANES), shape_of(unknowns // LANES, LANES),
              jax.ShapeDtypeStruct((unknowns, CELLS), bf16), jax.ShapeDtypeStruct((groups, 2 * twos * unknowns), bf16),
-             jax.ShapeDtypeStruct((twos * unknowns - late * width, LANES), bf16)),
+             jax.ShapeDtypeStruct((twos * unknowns - late * width, LANES), bf16), shape_of(4 * groups, LANES)),
             "vvvvvv",
             scratch=[pltpu.VMEM((groups, LANES), f32)],
         )(gathered, packed, beside, first2, second2, first3)
         result, correction = call(
             functools.partial(solve_kernel, devices),
             (shape_of(pairs, LANES), shape_of(width // LANES, LANES)),
-            "vvvvv" + "vvvvv" + "vvv",
+            "vvvvvv" + "vvvv" + "vv",
             outs="aa",
             scratch=[
                 pltpu.VMEM((late * width, LANES), bf16), pltpu.VMEM((groups, LANES), f32), vector,
                 pltpu.VMEM((width // LANES, LANES), f32), *finish_scratch, pltpu.SemaphoreType.DMA((2,)),
             ],
-        )(*begun, *common, second3, *fetched)
+        )(*begun, *common, second3, smoothed_fine)
         correction = correction.reshape(-1)
     else:
         correction, everywhere = coarse_by_parts(
@@ -583,8 +606,8 @@
         order = jnp.concatenate([low, own[2], high], axis=0).astype(i32)
         corr = jnp.repeat(everywhere[order[:, ::CELLS]], CELLS, axis=1)
         result = call(
-            functools.partial(finish_kernel, devices), shape_of(pairs, LANES), "vvvvvvvv", scratch=finish_scratch
-        )(corr, *common, *fetched)
+            functools.partial(finish_kernel, devices), shape_of(pairs, LANES), "vvvvvv", scratch=finish_scratch
+        )(corr, *common, smoothed_fine)
     return result.reshape(-1), correction
 
 

time: 31.6 us -> 31 us (0.981)
  waiting for transfers between devices: 2.83 us -> 2.19 us
    ppermute x1, starting transfers between devices: 0.08 us -> 0.68 us  [shards(): far = lax.ppermute(onward, BOTH, chain)]
    ppermute x1, starting transfers between devices: 3.03 us -> 2.59 us  [shards(): first2 = lax.ppermute(first, 'coarse', across)]
    ppermute x1, waiting for transfers between devices: 0.58 us -> 0.23 us  [shards(): far = lax.ppermute(onward, BOTH, chain)]
  transfers between devices with their start and end apart: 8 -> 8, of which waited for: 4 -> 4; matrix products, arithmetic and copies ran while one was open for 0% -> 0% of each run, Pallas kernels for 10% -> 12%
where the time goes in v6:
time: 31 us; the launch traced here: 30.8 us
  blocking collectives  11.9 us (38%)
  Pallas kernels  9.21 us (30%)
  starting transfers between devices  6.2 us (20%)
  waiting for transfers between devices  2.19 us (7%)
  between operations  1.33 us (4%)
    all_to_all x1, blocking collectives, shards(): gathered = lax.all_to_all(sent, BOTH, 0, 0, tiled=True)  11.9 us
    pallas_call x5, Pallas kernels, placed(): run(*(pltpu.with_memory_space_constraint(x, pltpu.HBM) if c == 'a' else x...  9.21 us
    ppermute x1, starting transfers between devices, shards(): first2 = lax.ppermute(first, 'coarse', across)  2.59 us
    ppermute x1, starting transfers between devices, shards(): second2 = lax.ppermute(second, 'coarse', across)  1.89 us
    ppermute x1, waiting for transfers between devices, shards(): second3 = lax.ppermute(second2, 'coarse', swap)  0.7 us
    ppermute x1, starting transfers between devices, shards(): far = lax.ppermute(onward, BOTH, chain)  0.68 us
    ppermute x1, waiting for transfers between devices, shards(): onward = lax.ppermute(onward, BOTH, partner)  0.67 us
  transfers between devices with their start and end apart: 8, of which 4 were waited for; matrix products, arithmetic and copies ran while one was open for 0% of the time, Pallas kernels for 12%

profile of v6, /device:TPU:0, one launch (start us, length us, event | category | flops | bytes accessed | tf_op | source)
XLA Modules:
  0.0 30.8 jit_solution(7236968165886887882)
XLA Ops:
  0.6 1.6 %shard_map.122 = (f32[3,8,128]{2,1,0:T(8,128)S(1)}, f32[3,8,128]{2,1,0:T(8,128)S(1)}, f32[3,16,128]{2,1,0:T(8,128)S(1)}, bf16[64,2048]{1,0:T(8,128)(2,1)S(1)}, f...) custom-call(f32[16,128]{1,0:T(8,128)} %bitcast.15, f32[16,128]{1,0:T(8,128)} %bitcast.17, ...), custom_call_target="tpu_custom_call" | custom-call | tf_op jit(solution)/shard_map/pallas_call | solution.py:464
  2.2 0.5 %collective-permute-start.4 = (f32[520,256]{1,0:T(8,128)S(1)}, f32[520,256]{1,0:T(8,128)S(1)}, u32[]{:S(2)}, u32[]{:S(2)}) collective-permute-start(f32[520,256]{1,0:T(8,128)S(1)} %get-tuple-element.37.mine_ref), channel_id=1, source_target_pairs={{0,1},{1,0},{2,3},{3,2},{4,5},{5,4},{6,7},{7,6},{8,9},{9,8},{10,11... | collective-permute-start | bytes 1597448 | tf_op jit(solution)/shard_map/ppermute | solution.py:562
  2.7 2.6 %collective-permute-start = (f32[200,256]{1,0:T(8,128)S(1)}, f32[200,256]{1,0:T(8,128)S(1)}, u32[]{:S(2)}, u32[]{:S(2)}) collective-permute-start(f32[200,256]{1,0:T(8,128)S(1)} %get-tuple-element.30), channel_id=1, source_target_pairs={{0,2},{1,3},{2,0},{3,1},{4,6},{5,7},{6,4},{7,5},{8,10},{9,11},{10,... | collective-permute-start | bytes 614408 | tf_op jit(solution)/shard_map/ppermute | solution.py:538
  5.3 0.2 collective-permute-start.1
  5.5 0.3 %collective-permute-start.3 = (f32[3,8,128]{2,1,0:T(8,128)S(1)}, f32[3,8,128]{2,1,0:T(8,128)S(1)}, u32[]{:S(2)}, u32[]{:S(2)}) collective-permute-start(f32[3,8,128]{2,1,0:T(8,128)S(1)} %get-tuple-element.33), channel_id=1, source_target_pairs={{0,1},{1,0},{2,3},{3,2},{4,5},{5,4},{6,7},{7,6},{8,9},{9,8},{10,11... | collective-permute-start | bytes 36872 | tf_op jit(solution)/shard_map/ppermute | solution.py:550
  5.8 0.7 %collective-permute-done.1 = f32[3,8,128]{2,1,0:T(8,128)S(1)} collective-permute-done((f32[3,8,128]{2,1,0:T(8,128)S(1)}, f32[3,8,128]{2,1,0:T(8,128)S(1)}, u32[]{:S(2)}, u32[]{:S(2)}) %collective-permute-start.1) | collective-permute-done | bytes 12320 | tf_op jit(solution)/shard_map/ppermute | solution.py:549
  6.5 0.7 %collective-permute-start.2 = (f32[3,8,128]{2,1,0:T(8,128)S(1)}, f32[3,8,128]{2,1,0:T(8,128)S(1)}, u32[]{:S(2)}, u32[]{:S(2)}) collective-permute-start(f32[3,8,128]{2,1,0:T(8,128)S(1)} %collective-permute-done.1), channel_id=1, source_target_pairs={{0,2},{1,0},{2,4},{3,1},{4,6},{5,3},{6,8},{7,5},{8,10},{9,7},{10,1... | collective-permute-start | bytes 36872 | tf_op jit(solution)/shard_map/ppermute | solution.py:552
  7.8 2.5 %shard_map.123 = (bf16[224,128]{1,0:T(8,128)(2,1)S(1)}, f32[112,8,128]{2,1,0:T(8,128)S(1)}, f32[2,16,128]{2,1,0:T(8,128)S(1)}, f32[7,64,2048]{2,1,0:T(8,128)S(1)}) custom-call(s32[1]{0:T(128)S(6)} %copy.14.counts_ref, f32[3,16,128]{2,1,0:T(8,128)S(1)} %get-tuple-element.34.own_ref, f32[16,128]{1,0:T(8,128)} %bitcast.16, f32[16,128]{1,0:T(8,128)} %bitcast.18, ...), custom_call_target="tpu_custom_call" | custom-call | tf_op jit(solution)/shard_map/pallas_call | solution.py:464
  10.3 0.0 collective-permute-done.3.near_ref
  10.3 0.2 collective-permute-done.2.far_ref
  10.5 0.6 %collective-permute-done.first2_ref = f32[200,256]{1,0:T(8,128)S(1)} collective-permute-done((f32[200,256]{1,0:T(8,128)S(1)}, f32[200,256]{1,0:T(8,128)S(1)}, u32[]{:S(2)}, u32[]{:S(2)}) %collective-permute-start) | collective-permute-done | bytes 204832 | tf_op jit(solution)/shard_map/ppermute | solution.py:538
  11.1 0.0 collective-permute-done.4.beside_ref
  11.1 1.9 %collective-permute-start.6 = (f32[320,256]{1,0:T(8,128)S(1)}, f32[320,256]{1,0:T(8,128)S(1)}, u32[]{:S(2)}, u32[]{:S(2)}) collective-permute-start(f32[320,256]{1,0:T(8,128)S(1)} %get-tuple-element.39), channel_id=1, source_target_pairs={{0,2},{1,3},{2,0},{3,1},{4,6},{5,7},{6,4},{7,5},{8,10},{9,11},{10,... | collective-permute-start | bytes 983048 | tf_op jit(solution)/shard_map/ppermute | solution.py:564
  13.0 0.0 collective-permute-start.5
  13.0 0.4 %shard_map.124 = f32[32,128]{1,0:T(8,128)S(1)} custom-call(f32[3,8,128]{2,1,0:T(8,128)S(1)} %collective-permute-done.3.near_ref, f32[3,8,128]{2,1,0:T(8,128)S(1)} %collective-permute-done.2.far_ref, f32[3,16,128]{2,1,0:T(8,128)S(1)} %get-tuple-element.34.own_ref, bf16[224,128]{1,0:T(8,128)(2,1)S(1)} %get-tuple-element.42.selected_ref, ...), custom_call_target="tpu_custom_call" | custom-call | tf_op jit(solution)/shard_map/pallas_call | solution.py:464
  13.4 11.9 %all_to_all.12 = f32[32,1,128]{2,1,0:T(1,128)S(1)} all-to-all(f32[32,1,128]{2,1,0:T(1,128)S(1)} %bitcast.13), channel_id=1, replica_groups=mesh['fine'=8,'coarse'=4] {'fine','coarse'}, dimensions={0} | all-to-all | bytes 32768 | tf_op jit(solution)/shard_map/all_to_all | solution.py:574
  25.3 0.0 collective-permute-done.5.first3_ref
  25.3 0.0 collective-permute-done.6.second2_ref
  25.3 0.0 collective-permute-start.7
  25.3 0.9 %shard_map.125 = (f32[8,128]{1,0:T(8,128)S(1)}, f32[8,128]{1,0:T(8,128)S(1)}, bf16[1024,64]{1,0:T(8,128)(2,1)S(1)}, bf16[16,8192]{1,0:T(8,128)(2,1)S(1)}, bf16[3...) custom-call(f32[32,128]{1,0:T(8,128)S(1)} %bitcast.12, f32[520,256]{1,0:T(8,128)S(1)} %get-tuple-element.37.mine_ref, ...), custom_call_target="tpu_custom_call" | custom-call | tf_op jit(solution)/shard_map/pallas_call | solution.py:464
  26.2 0.7 %collective-permute-done.7.second3_ref = f32[320,256]{1,0:T(8,128)S(1)} collective-permute-done((f32[320,256]{1,0:T(8,128)S(1)}, f32[320,256]{1,0:T(8,128)S(1)}, u32[]{:S(2)}, u32[]{:S(2)}) %collective-permute-start.7) | collective-permute-done | bytes 327712 | tf_op jit(solution)/shard_map/ppermute | solution.py:576
  26.9 3.9 %shard_map.126 = (f32[16,128]{1,0:T(8,128)}, f32[2,128]{1,0:T(2,128)}) custom-call(f32[8,128]{1,0:T(8,128)S(1)} %get-tuple-element.49.side_ref, f32[8,128]{1,0:T(8,128)S(1)} %get-tuple-element.50.begun_ref, bf16[1024,64]{1,0:T(8,128)(2,1)S(1)} %get-tuple-element.51.inverse_ref, bf16[16,8192]{1,0:T(8,128)(2,1)S(1)} %get-tuple-element.52.target_ref, ...), custom_call_target="tpu_custom_call" | custom-call | tf_op jit(solution)/shard_map/pallas_call | solution.py:464
Async XLA Ops:
  2.2 8.9 %collective-permute-start.4 = (f32[520,256]{1,0:T(8,128)S(1)}, f32[520,256]{1,0:T(8,128)S(1)}, u32[]{:S(2)}, u32[]{:S(2)}) collective-permute-start(f32[520,256]{1,0:T(8,128)S(1)} %get-tuple-element.37.mine_ref), channel_id=1, source_target_pairs={{0,1},{1,0},{2,3},{3,2},{4,5},{5,4},{6,7},{7,6},{8,9},{9,8},{10,11... | collective-permute-start | bytes 1597448 | tf_op jit(solution)/shard_map/ppermute | solution.py:562
  2.7 8.4 %collective-permute-start = (f32[200,256]{1,0:T(8,128)S(1)}, f32[200,256]{1,0:T(8,128)S(1)}, u32[]{:S(2)}, u32[]{:S(2)}) collective-permute-start(f32[200,256]{1,0:T(8,128)S(1)} %get-tuple-element.30), channel_id=1, source_target_pairs={{0,2},{1,3},{2,0},{3,1},{4,6},{5,7},{6,4},{7,5},{8,10},{9,11},{10,... | collective-permute-start | bytes 614408 | tf_op jit(solution)/shard_map/ppermute | solution.py:538
  5.3 1.2 %collective-permute-start.1 = (f32[3,8,128]{2,1,0:T(8,128)S(1)}, f32[3,8,128]{2,1,0:T(8,128)S(1)}, u32[]{:S(2)}, u32[]{:S(2)}) collective-permute-start(f32[3,8,128]{2,1,0:T(8,128)S(1)} %get-tuple-element.32), channel_id=1, source_target_pairs={{0,1},{1,0},{2,3},{3,2},{4,5},{5,4},{6,7},{7,6},{8,9},{9,8},{10,11... | collective-permute-start | bytes 36872 | tf_op jit(solution)/shard_map/ppermute | solution.py:549
  5.5 4.8 %collective-permute-start.3 = (f32[3,8,128]{2,1,0:T(8,128)S(1)}, f32[3,8,128]{2,1,0:T(8,128)S(1)}, u32[]{:S(2)}, u32[]{:S(2)}) collective-permute-start(f32[3,8,128]{2,1,0:T(8,128)S(1)} %get-tuple-element.33), channel_id=1, source_target_pairs={{0,1},{1,0},{2,3},{3,2},{4,5},{5,4},{6,7},{7,6},{8,9},{9,8},{10,11... | collective-permute-start | bytes 36872 | tf_op jit(solution)/shard_map/ppermute | solution.py:550
  6.5 4.0 %collective-permute-start.2 = (f32[3,8,128]{2,1,0:T(8,128)S(1)}, f32[3,8,128]{2,1,0:T(8,128)S(1)}, u32[]{:S(2)}, u32[]{:S(2)}) collective-permute-start(f32[3,8,128]{2,1,0:T(8,128)S(1)} %collective-permute-done.1), channel_id=1, source_target_pairs={{0,2},{1,0},{2,4},{3,1},{4,6},{5,3},{6,8},{7,5},{8,10},{9,7},{10,1... | collective-permute-start | bytes 36872 | tf_op jit(solution)/shard_map/ppermute | solution.py:552
  11.1 14.2 %collective-permute-start.6 = (f32[320,256]{1,0:T(8,128)S(1)}, f32[320,256]{1,0:T(8,128)S(1)}, u32[]{:S(2)}, u32[]{:S(2)}) collective-permute-start(f32[320,256]{1,0:T(8,128)S(1)} %get-tuple-element.39), channel_id=1, source_target_pairs={{0,2},{1,3},{2,0},{3,1},{4,6},{5,7},{6,4},{7,5},{8,10},{9,11},{10,... | collective-permute-start | bytes 983048 | tf_op jit(solution)/shard_map/ppermute | solution.py:564
  13.0 12.3 %collective-permute-start.5 = (f32[200,256]{1,0:T(8,128)S(1)}, f32[200,256]{1,0:T(8,128)S(1)}, u32[]{:S(2)}, u32[]{:S(2)}) collective-permute-start(f32[200,256]{1,0:T(8,128)S(1)} %collective-permute-done.first2_ref), channel_id=1, source_target_pairs={{0,1},{1,0},{2,3},{3,2},{4,5},{5,4},{6,7},{7,6},{8,9},{9,8},{10,11... | collective-permute-start | bytes 614408 | tf_op jit(solution)/shard_map/ppermute | solution.py:565
  25.3 1.6 %collective-permute-start.7 = (f32[320,256]{1,0:T(8,128)S(1)}, f32[320,256]{1,0:T(8,128)S(1)}, u32[]{:S(2)}, u32[]{:S(2)}) collective-permute-start(f32[320,256]{1,0:T(8,128)S(1)} %collective-permute-done.6.second2_ref), channel_id=1, source_target_pairs={{0,1},{1,0},{2,3},{3,2},{4,5},{5,4},{6,7},{7,6},{8,9},{9,8},{10,11... | collective-permute-start | bytes 983048 | tf_op jit(solution)/shard_map/ppermute | solution.py:576

commit v7 on v6

--- a/solution.py
+++ b/solution.py
@@ -447,7 +447,7 @@
            picked_ref, high_ref, low_ref)
 
 
-def call(kernel, out_shape, ins, outs=None, scratch=()):
+def call(kernel, out_shape, ins, outs=None, scratch=(), cost=None):
     spaces = dict(s=pltpu.SMEM, v=pltpu.VMEM, a=pl.ANY)
     many = isinstance(out_shape, tuple)
     specs = tuple(pl.BlockSpec(memory_space=spaces[c]) for c in outs or "v" * (len(out_shape) if many else 1))
@@ -458,6 +458,7 @@
         out_specs=specs if many else specs[0],
         scratch_shapes=list(scratch),
         compiler_params=pltpu.CompilerParams(vmem_limit_bytes=VMEM_LIMIT),
+        cost_estimate=cost and pl.CostEstimate(flops=cost, bytes_accessed=0, transcendentals=0),
     )
 
     def placed(*operands):
@@ -559,13 +560,13 @@
     )(pit_counts, own, rhs, reaction, fine_columns, fine_values, smoother_here)
 
     if copied:
+        first2, second, selected = lax.optimization_barrier((first2, second, selected))
         beside = lax.ppermute(packed, "coarse", swap)
-        first2, second, far, near, selected, beside = lax.optimization_barrier((first2, second, far, near, selected, beside))
         second2 = lax.ppermute(second, "coarse", across)
         first3 = lax.ppermute(first2, "coarse", swap)
 
     sent = call(
-        functools.partial(residual_kernel, devices), shape_of(devices, LANES), "vvvvvv", scratch=[picked]
+        functools.partial(residual_kernel, devices), shape_of(devices, LANES), "vvvvvv", scratch=[picked], cost=10_000_000_000
     )(near, far, own, selected, weighed, local)
 
     finish_scratch = [picked, *products]

time: 31 us -> 30.1 us (0.971)
  blocking collectives: 11.9 us -> 10.9 us
  starting transfers between devices: 6.2 us -> 6.67 us
  waiting for transfers between devices: 2.19 us -> 1.78 us
    all_to_all x1, blocking collectives: 11.9 us -> 10.9 us  [shards(): gathered = lax.all_to_all(sent, BOTH, 0, 0, tiled=True)]
    ppermute x1, starting transfers between devices: 1.89 us -> 2.61 us  [shards(): second2 = lax.ppermute(second, 'coarse', across)]
    ppermute x1, starting transfers between devices: 0.68 us -> 0.08 us  [shards(): far = lax.ppermute(onward, BOTH, chain)]
    ppermute x1, starting transfers between devices: 2.59 us -> 3.03 us  [shards(): first2 = lax.ppermute(first, 'coarse', across)]
  transfers between devices with their start and end apart: 8 -> 8, of which waited for: 4 -> 3; matrix products, arithmetic and copies ran while one was open for 0% -> 0% of each run, Pallas kernels for 12% -> 13%
where the time goes in v7:
time: 30.1 us; the launch traced here: 29.9 us
  blocking collectives  10.9 us (36%)
  Pallas kernels  9.2 us (31%)
  starting transfers between devices  6.67 us (22%)
  waiting for transfers between devices  1.78 us (6%)
  between operations  1.33 us (4%)
    all_to_all x1, blocking collectives, shards(): gathered = lax.all_to_all(sent, BOTH, 0, 0, tiled=True)  10.9 us
    pallas_call x5, Pallas kernels, placed(): run(*(pltpu.with_memory_space_constraint(x, pltpu.HBM) if c == 'a' else x...  9.2 us
    ppermute x1, starting transfers between devices, shards(): first2 = lax.ppermute(first, 'coarse', across)  3.03 us
    ppermute x1, starting transfers between devices, shards(): second2 = lax.ppermute(second, 'coarse', across)  2.61 us
    ppermute x1, waiting for transfers between devices, shards(): second3 = lax.ppermute(second2, 'coarse', swap)  0.69 us
    ppermute x1, waiting for transfers between devices, shards(): onward = lax.ppermute(onward, BOTH, partner)  0.67 us
  transfers between devices with their start and end apart: 8, of which 3 were waited for; matrix products, arithmetic and copies ran while one was open for 0% of the time, Pallas kernels for 13%

profile of v7, /device:TPU:0, one launch (start us, length us, event | category | flops | bytes accessed | tf_op | source)
XLA Modules:
  0.0 29.9 jit_solution(14856404662017203911)
XLA Ops:
  0.6 1.6 %shard_map.122 = (f32[3,8,128]{2,1,0:T(8,128)S(1)}, f32[3,8,128]{2,1,0:T(8,128)S(1)}, f32[3,16,128]{2,1,0:T(8,128)S(1)}, bf16[64,2048]{1,0:T(8,128)(2,1)S(1)}, f...) custom-call(f32[16,128]{1,0:T(8,128)} %bitcast.15, f32[16,128]{1,0:T(8,128)} %bitcast.17, ...), custom_call_target="tpu_custom_call" | custom-call | tf_op jit(solution)/shard_map/pallas_call | solution.py:465
  2.2 3.0 %collective-permute-start = (f32[200,256]{1,0:T(8,128)S(1)}, f32[200,256]{1,0:T(8,128)S(1)}, u32[]{:S(2)}, u32[]{:S(2)}) collective-permute-start(f32[200,256]{1,0:T(8,128)S(1)} %get-tuple-element.27), channel_id=1, source_target_pairs={{0,2},{1,3},{2,0},{3,1},{4,6},{5,7},{6,4},{7,5},{8,10},{9,11},{10,... | collective-permute-start | bytes 614408 | tf_op jit(solution)/shard_map/ppermute | solution.py:539
  5.2 0.0 collective-permute-start.4
  5.2 0.5 %collective-permute-start.3 = (f32[3,8,128]{2,1,0:T(8,128)S(1)}, f32[3,8,128]{2,1,0:T(8,128)S(1)}, u32[]{:S(2)}, u32[]{:S(2)}) collective-permute-start(f32[3,8,128]{2,1,0:T(8,128)S(1)} %get-tuple-element.34), channel_id=1, source_target_pairs={{0,1},{1,0},{2,3},{3,2},{4,5},{5,4},{6,7},{7,6},{8,9},{9,8},{10,11... | collective-permute-start | bytes 36872 | tf_op jit(solution)/shard_map/ppermute | solution.py:551
  5.8 0.7 %collective-permute-done.4 = f32[3,8,128]{2,1,0:T(8,128)S(1)} collective-permute-done((f32[3,8,128]{2,1,0:T(8,128)S(1)}, f32[3,8,128]{2,1,0:T(8,128)S(1)}, u32[]{:S(2)}, u32[]{:S(2)}) %collective-permute-start.4) | collective-permute-done | bytes 12320 | tf_op jit(solution)/shard_map/ppermute | solution.py:550
  6.4 0.1 collective-permute-start.5
  6.5 0.4 %collective-permute-start.6 = (f32[520,256]{1,0:T(8,128)S(1)}, f32[520,256]{1,0:T(8,128)S(1)}, u32[]{:S(2)}, u32[]{:S(2)}) collective-permute-start(f32[520,256]{1,0:T(8,128)S(1)} %get-tuple-element.40.mine_ref), channel_id=1, source_target_pairs={{0,1},{1,0},{2,3},{3,2},{4,5},{5,4},{6,7},{7,6},{8,9},{9,8},{10,11... | collective-permute-start | bytes 1597448 | tf_op jit(solution)/shard_map/ppermute | solution.py:564
  7.6 2.5 %shard_map.123 = (bf16[224,128]{1,0:T(8,128)(2,1)S(1)}, f32[112,8,128]{2,1,0:T(8,128)S(1)}, f32[2,16,128]{2,1,0:T(8,128)S(1)}, f32[7,64,2048]{2,1,0:T(8,128)S(1)}) custom-call(s32[1]{0:T(128)S(6)} %copy.14.counts_ref, f32[3,16,128]{2,1,0:T(8,128)S(1)} %get-tuple-element.29.own_ref, f32[16,128]{1,0:T(8,128)} %bitcast.16, f32[16,128]{1,0:T(8,128)} %bitcast.18, ...), custom_call_target="tpu_custom_call" | custom-call | tf_op jit(solution)/shard_map/pallas_call | solution.py:465
  10.0 0.4 %collective-permute-done.first2_ref = f32[200,256]{1,0:T(8,128)S(1)} collective-permute-done((f32[200,256]{1,0:T(8,128)S(1)}, f32[200,256]{1,0:T(8,128)S(1)}, u32[]{:S(2)}, u32[]{:S(2)}) %collective-permute-start) | collective-permute-done | bytes 204832 | tf_op jit(solution)/shard_map/ppermute | solution.py:539
  10.4 0.0 collective-permute-start.1
  10.5 2.6 %collective-permute-start.2 = (f32[320,256]{1,0:T(8,128)S(1)}, f32[320,256]{1,0:T(8,128)S(1)}, u32[]{:S(2)}, u32[]{:S(2)}) collective-permute-start(f32[320,256]{1,0:T(8,128)S(1)} %get-tuple-element.33), channel_id=1, source_target_pairs={{0,2},{1,3},{2,0},{3,1},{4,6},{5,7},{6,4},{7,5},{8,10},{9,11},{10,... | collective-permute-start | bytes 983048 | tf_op jit(solution)/shard_map/ppermute | solution.py:565
  13.1 0.0 collective-permute-done.3.near_ref
  13.1 0.0 collective-permute-done.5.far_ref
  13.1 0.4 %shard_map.124 = f32[32,128]{1,0:T(8,128)S(1)} custom-call(f32[3,8,128]{2,1,0:T(8,128)S(1)} %collective-permute-done.3.near_ref, f32[3,8,128]{2,1,0:T(8,128)S(1)} %collective-permute-done.5.far_ref, f32[3,16,128]{2,1,0:T(8,128)S(1)} %get-tuple-element.29.own_ref, bf16[224,128]{1,0:T(8,128)(2,1)S(1)} %get-tuple-element.36.selected_ref, ...), custom_call_target="tpu_custom_call" | custom-call | flops 10000000000 | tf_op jit(solution)/shard_map/pallas_call | solution.py:465
  13.4 10.9 %all_to_all.12 = f32[32,1,128]{2,1,0:T(1,128)S(1)} all-to-all(f32[32,1,128]{2,1,0:T(1,128)S(1)} %bitcast.13), channel_id=1, replica_groups=mesh['fine'=8,'coarse'=4] {'fine','coarse'}, dimensions={0} | all-to-all | bytes 32768 | tf_op jit(solution)/shard_map/all_to_all | solution.py:575
  24.4 0.0 collective-permute-done.1.first3_ref
  24.4 0.0 collective-permute-done.2.second2_ref
  24.4 0.0 collective-permute-start.7
  24.4 0.0 collective-permute-done.6.beside_ref
  24.4 0.9 %shard_map.125 = (f32[8,128]{1,0:T(8,128)S(1)}, f32[8,128]{1,0:T(8,128)S(1)}, bf16[1024,64]{1,0:T(8,128)(2,1)S(1)}, bf16[16,8192]{1,0:T(8,128)(2,1)S(1)}, bf16[3...) custom-call(f32[32,128]{1,0:T(8,128)S(1)} %bitcast.12, f32[520,256]{1,0:T(8,128)S(1)} %get-tuple-element.40.mine_ref, ...), custom_call_target="tpu_custom_call" | custom-call | tf_op jit(solution)/shard_map/pallas_call | solution.py:465
  25.3 0.7 %collective-permute-done.7.second3_ref = f32[320,256]{1,0:T(8,128)S(1)} collective-permute-done((f32[320,256]{1,0:T(8,128)S(1)}, f32[320,256]{1,0:T(8,128)S(1)}, u32[]{:S(2)}, u32[]{:S(2)}) %collective-permute-start.7) | collective-permute-done | bytes 327712 | tf_op jit(solution)/shard_map/ppermute | solution.py:577
  26.0 3.9 %shard_map.126 = (f32[16,128]{1,0:T(8,128)}, f32[2,128]{1,0:T(2,128)}) custom-call(f32[8,128]{1,0:T(8,128)S(1)} %get-tuple-element.43.side_ref, f32[8,128]{1,0:T(8,128)S(1)} %get-tuple-element.44.begun_ref, bf16[1024,64]{1,0:T(8,128)(2,1)S(1)} %get-tuple-element.45.inverse_ref, bf16[16,8192]{1,0:T(8,128)(2,1)S(1)} %get-tuple-element.46.target_ref, ...), custom_call_target="tpu_custom_call" | custom-call | tf_op jit(solution)/shard_map/pallas_call | solution.py:465
Async XLA Ops:
  2.2 8.2 %collective-permute-start = (f32[200,256]{1,0:T(8,128)S(1)}, f32[200,256]{1,0:T(8,128)S(1)}, u32[]{:S(2)}, u32[]{:S(2)}) collective-permute-start(f32[200,256]{1,0:T(8,128)S(1)} %get-tuple-element.27), channel_id=1, source_target_pairs={{0,2},{1,3},{2,0},{3,1},{4,6},{5,7},{6,4},{7,5},{8,10},{9,11},{10,... | collective-permute-start | bytes 614408 | tf_op jit(solution)/shard_map/ppermute | solution.py:539
  5.2 1.2 %collective-permute-start.4 = (f32[3,8,128]{2,1,0:T(8,128)S(1)}, f32[3,8,128]{2,1,0:T(8,128)S(1)}, u32[]{:S(2)}, u32[]{:S(2)}) collective-permute-start(f32[3,8,128]{2,1,0:T(8,128)S(1)} %get-tuple-element.35), channel_id=1, source_target_pairs={{0,1},{1,0},{2,3},{3,2},{4,5},{5,4},{6,7},{7,6},{8,9},{9,8},{10,11... | collective-permute-start | bytes 36872 | tf_op jit(solution)/shard_map/ppermute | solution.py:550
  5.2 7.8 %collective-permute-start.3 = (f32[3,8,128]{2,1,0:T(8,128)S(1)}, f32[3,8,128]{2,1,0:T(8,128)S(1)}, u32[]{:S(2)}, u32[]{:S(2)}) collective-permute-start(f32[3,8,128]{2,1,0:T(8,128)S(1)} %get-tuple-element.34), channel_id=1, source_target_pairs={{0,1},{1,0},{2,3},{3,2},{4,5},{5,4},{6,7},{7,6},{8,9},{9,8},{10,11... | collective-permute-start | bytes 36872 | tf_op jit(solution)/shard_map/ppermute | solution.py:551
  6.4 6.6 %collective-permute-start.5 = (f32[3,8,128]{2,1,0:T(8,128)S(1)}, f32[3,8,128]{2,1,0:T(8,128)S(1)}, u32[]{:S(2)}, u32[]{:S(2)}) collective-permute-start(f32[3,8,128]{2,1,0:T(8,128)S(1)} %collective-permute-done.4), channel_id=1, source_target_pairs={{0,2},{1,0},{2,4},{3,1},{4,6},{5,3},{6,8},{7,5},{8,10},{9,7},{10,1... | collective-permute-start | bytes 36872 | tf_op jit(solution)/shard_map/ppermute | solution.py:553
  6.5 17.9 %collective-permute-start.6 = (f32[520,256]{1,0:T(8,128)S(1)}, f32[520,256]{1,0:T(8,128)S(1)}, u32[]{:S(2)}, u32[]{:S(2)}) collective-permute-start(f32[520,256]{1,0:T(8,128)S(1)} %get-tuple-element.40.mine_ref), channel_id=1, source_target_pairs={{0,1},{1,0},{2,3},{3,2},{4,5},{5,4},{6,7},{7,6},{8,9},{9,8},{10,11... | collective-permute-start | bytes 1597448 | tf_op jit(solution)/shard_map/ppermute | solution.py:564
  10.4 13.9 %collective-permute-start.1 = (f32[200,256]{1,0:T(8,128)S(1)}, f32[200,256]{1,0:T(8,128)S(1)}, u32[]{:S(2)}, u32[]{:S(2)}) collective-permute-start(f32[200,256]{1,0:T(8,128)S(1)} %collective-permute-done.first2_ref), channel_id=1, source_target_pairs={{0,1},{1,0},{2,3},{3,2},{4,5},{5,4},{6,7},{7,6},{8,9},{9,8},{10,11... | collective-permute-start | bytes 614408 | tf_op jit(solution)/shard_map/ppermute | solution.py:566
  10.5 13.9 %collective-permute-start.2 = (f32[320,256]{1,0:T(8,128)S(1)}, f32[320,256]{1,0:T(8,128)S(1)}, u32[]{:S(2)}, u32[]{:S(2)}) collective-permute-start(f32[320,256]{1,0:T(8,128)S(1)} %get-tuple-element.33), channel_id=1, source_target_pairs={{0,2},{1,3},{2,0},{3,1},{4,6},{5,7},{6,4},{7,5},{8,10},{9,11},{10,... | collective-permute-start | bytes 983048 | tf_op jit(solution)/shard_map/ppermute | solution.py:565
  24.4 1.6 %collective-permute-start.7 = (f32[320,256]{1,0:T(8,128)S(1)}, f32[320,256]{1,0:T(8,128)S(1)}, u32[]{:S(2)}, u32[]{:S(2)}) collective-permute-start(f32[320,256]{1,0:T(8,128)S(1)} %collective-permute-done.2.second2_ref), channel_id=1, source_target_pairs={{0,1},{1,0},{2,3},{3,2},{4,5},{5,4},{6,7},{7,6},{8,9},{9,8},{10,11... | collective-permute-start | bytes 983048 | tf_op jit(solution)/shard_map/ppermute | solution.py:577

commit v8 on v7

--- a/solution.py
+++ b/solution.py
@@ -11,7 +11,7 @@
 LANES = 128
 HALO_ROWS = 8
 SWEEPS = 4
-EARLY = 2
+EARLY = 0
 BOTH = ("fine", "coarse")
 f32, bf16, i32 = jnp.float32, jnp.bfloat16, jnp.int32
 VMEM_LIMIT = 24 * 1024 * 1024
@@ -54,15 +54,15 @@
 def selection(columns, half_rows, pairs):
     nbrs, aggs = columns.shape
     at, who = iota((pairs, aggs), 1), iota((pairs, aggs), 0)
-    entry = iota((pairs, 4 * half_rows), 1) % (2 * half_rows)
-    parts = []
-    for half in range(2):
-        for k in range(nbrs):
-            chosen = jnp.where(at == 2 * who + half, columns[k : k + 1].astype(f32), 0.0)
-            block = jnp.sum(chosen, axis=1, keepdims=True).astype(i32)
-            place = block // 2 + jnp.where(block % 2 == half, 0, half_rows)
-            parts.append((entry == place).astype(bf16))
-    return jnp.concatenate(parts, axis=0)
+    chosen = [
+        jnp.where(at == 2 * who + half, columns[k : k + 1].astype(f32), 0.0)
+        for half in range(2)
+        for k in range(nbrs)
+    ]
+    block = dot(jnp.concatenate(chosen, axis=0).astype(bf16), jnp.ones((aggs, 4 * half_rows), bf16)).astype(i32)
+    half = iota(block.shape, 0) // (nbrs * pairs)
+    place = block // 2 + jnp.where(block % 2 == half, 0, half_rows)
+    return (iota(block.shape, 1) % (2 * half_rows) == place).astype(bf16)
 
 
 def pick(window, selected):
@@ -181,23 +181,16 @@
 
 
 def prepare_kernel(
-    counts_ref, own_ref, rhs_any, reaction_any, columns_any, fine_any, smoother_ref, selected_ref, weighed_ref, local_ref,
-    products_ref, rhs_ref, reaction_ref, columns_ref, fine_ref, wide_ref, sem_ref,
+    counts_ref, own_ref, rhs_any, reaction_any, columns_any, fine_any, selected_ref, weighed_ref, local_ref,
+    masked_ref, fine_ref, rhs_ref, reaction_ref, columns_ref, wide_ref, sem_ref,
 ):
     copies = fetch(
         sem_ref, (columns_any, columns_ref), (rhs_any, rhs_ref), (reaction_any, reaction_ref),
         *((fine_any.at[k], fine_ref.at[k]) for k in range(fine_ref.shape[0])),
     )
-    for copy in copies[:3]:
-        copy.wait()
-    pairs = rhs_ref.shape[0]
     nbrs, _, width = fine_ref.shape
+    pairs = width // LANES
     weights = own_ref[1]
-    agg = 2 * iota((pairs, LANES), 0) + iota((pairs, LANES), 1) // CELLS
-    reaction = jnp.where(agg < counts_ref[0], reaction_ref[...], 0.0)
-    local_ref[0] = weights * rhs_ref[...]
-    local_ref[1] = weights * reaction
-    selected_ref[...] = selection(columns_ref[...], pairs + 2 * HALO_ROWS, pairs)
     by_agg = jnp.concatenate([weights[:, :CELLS], weights[:, CELLS:]], axis=0)
     row, lane = iota((2 * pairs, width), 0), iota((2 * pairs, width), 1)
     member = (lane // CELLS == 2 * (row % pairs) + row // pairs).astype(bf16)
@@ -206,6 +199,14 @@
         term = lax.dot_general(part, member, (((0,), (0,)), ((), ())), preferred_element_type=f32)
         wide = term if wide is None else wide + term
     wide_ref[...] = wide
+    for copy in copies[:3]:
+        copy.wait()
+    agg = 2 * iota((pairs, LANES), 0) + iota((pairs, LANES), 1) // CELLS
+    reaction = jnp.where(agg < counts_ref[0], reaction_ref[...], 0.0)
+    local_ref[0] = weights * rhs_ref[...]
+    local_ref[1] = weights * reaction
+    masked_ref[...] = reaction
+    selected_ref[...] = selection(columns_ref[...], pairs + 2 * HALO_ROWS, pairs)
     for k in range(nbrs):
         copies[3 + k].wait()
         for p in range(pairs):
@@ -215,6 +216,11 @@
             for r in range(8, CELLS, 8):
                 total = total + term[r : r + 8]
             weighed_ref[k * pairs + p] = total
+
+
+def products_kernel(reaction_ref, fine_ref, smoother_ref, products_ref):
+    nbrs, _, width = fine_ref.shape
+    pairs = width // LANES
     lane = iota((CELLS, LANES), 1)
     for p in range(pairs):
         cols = pl.ds(p * LANES, LANES)
@@ -228,7 +234,7 @@
         both = dot(left, jnp.concatenate(rights, axis=1))
         for k in range(nbrs):
             product = both[:, k * LANES : (k + 1) * LANES]
-            products_ref[k, :, cols] = product if k else product + left.astype(f32) * reaction[p : p + 1]
+            products_ref[k, :, cols] = product if k else product + left.astype(f32) * reaction_ref[p : p + 1, :]
 
 
 def residual_kernel(
@@ -550,23 +556,26 @@
     onward = lax.ppermute(onward, BOTH, partner)
     near = lax.ppermute(near, BOTH, partner)
 
+    if copied:
+        second, onward = lax.optimization_barrier((second, onward))
     far = lax.ppermute(onward, BOTH, chain)
-    selected, weighed, local, smoothed_fine = call(
+    selected, weighed, local, masked, fine_here = call(
         prepare_kernel,
         (jax.ShapeDtypeStruct((aggs * nbrs, 4 * rows), bf16), shape_of(nbrs * pairs, 8, LANES), shape_of(2, pairs, LANES),
-         shape_of(*fine_values.shape)),
-        "svaaaav",
-        scratch=[vector, vector, pltpu.VMEM(fine_columns.shape, i32), pltpu.VMEM(fine_values.shape, bf16), pltpu.VMEM((CELLS, cells), f32), pltpu.SemaphoreType.DMA((3 + nbrs,))],
-    )(pit_counts, own, rhs, reaction, fine_columns, fine_values, smoother_here)
+         shape_of(pairs, LANES), jax.ShapeDtypeStruct(fine_values.shape, bf16)),
+        "svaaaa",
+        scratch=[vector, vector, pltpu.VMEM(fine_columns.shape, i32), pltpu.VMEM((CELLS, cells), f32), pltpu.SemaphoreType.DMA((3 + nbrs,))],
+        cost=10_000_000_000,
+    )(pit_counts, own, rhs, reaction, fine_columns, fine_values)
+    smoothed_fine = call(products_kernel, shape_of(*fine_values.shape), "vvv")(masked, fine_here, smoother_here)
 
     if copied:
-        first2, second, selected = lax.optimization_barrier((first2, second, selected))
         beside = lax.ppermute(packed, "coarse", swap)
         second2 = lax.ppermute(second, "coarse", across)
         first3 = lax.ppermute(first2, "coarse", swap)
 
     sent = call(
-        functools.partial(residual_kernel, devices), shape_of(devices, LANES), "vvvvvv", scratch=[picked], cost=10_000_000_000
+        functools.partial(residual_kernel, devices), shape_of(devices, LANES), "vvvvvv", scratch=[picked], cost=None
     )(near, far, own, selected, weighed, local)
 
     finish_scratch = [picked, *products]

time: 30.1 us -> 29.4 us (0.977)
  waiting for transfers between devices: 1.78 us -> 0.1 us
  blocking collectives: 10.9 us -> 11.9 us
    all_to_all x1, blocking collectives: 10.9 us -> 11.9 us  [shards(): gathered = lax.all_to_all(sent, BOTH, 0, 0, tiled=True)]
    ppermute x1, waiting for transfers between devices: 0.67 us -> 0.01 us  [shards(): onward = lax.ppermute(onward, BOTH, partner)]
    ppermute x1, waiting for transfers between devices: 0.69 us -> 0.07 us  [shards(): second3 = lax.ppermute(second2, 'coarse', swap)]
    ppermute x1, starting transfers between devices: 0.43 us -> 0.01 us  [shards(): beside = lax.ppermute(packed, 'coarse', swap)]
    ppermute x1, waiting for transfers between devices: 0.4 us -> 0.01 us  [shards(): first2 = lax.ppermute(first, 'coarse', across)]
    pallas_call x5 -> x6, Pallas kernels: 9.2 us -> 9.22 us  [placed(): run(*(pltpu.with_memory_space_constraint(x, pltpu.HBM) if c == 'a' else x...]
  transfers between devices with their start and end apart: 8 -> 8, of which waited for: 3 -> 1; matrix products, arithmetic and copies ran while one was open for 0% -> 0% of each run, Pallas kernels for 13% -> 13%
where the time goes in v8:
time: 29.4 us; the launch traced here: 29.1 us
  blocking collectives  11.9 us (40%)
  Pallas kernels  9.22 us (31%)
  starting transfers between devices  6.56 us (22%)
  between operations  1.35 us (5%)
    all_to_all x1, blocking collectives, shards(): gathered = lax.all_to_all(sent, BOTH, 0, 0, tiled=True)  11.9 us
    pallas_call x6, Pallas kernels, placed(): run(*(pltpu.with_memory_space_constraint(x, pltpu.HBM) if c == 'a' else x...  9.22 us
    ppermute x1, starting transfers between devices, shards(): first2 = lax.ppermute(first, 'coarse', across)  3.03 us
    ppermute x1, starting transfers between devices, shards(): second2 = lax.ppermute(second, 'coarse', across)  2.8 us
  transfers between devices with their start and end apart: 8, of which 1 were waited for; matrix products, arithmetic and copies ran while one was open for 0% of the time, Pallas kernels for 13%

profile of v8, /device:TPU:0, one launch (start us, length us, event | category | flops | bytes accessed | tf_op | source)
XLA Modules:
  0.0 29.1 jit_solution(12292079265851431174)
XLA Ops:
  0.6 1.6 %shard_map.122 = (f32[3,8,128]{2,1,0:T(8,128)S(1)}, f32[3,8,128]{2,1,0:T(8,128)S(1)}, f32[3,16,128]{2,1,0:T(8,128)S(1)}, bf16[64,2048]{1,0:T(8,128)(2,1)S(1)}, f...) custom-call(f32[16,128]{1,0:T(8,128)} %bitcast.16, f32[16,128]{1,0:T(8,128)} %bitcast.15, ...), custom_call_target="tpu_custom_call" | custom-call | tf_op jit(solution)/shard_map/pallas_call | solution.py:471
  2.2 3.0 %collective-permute-start = (f32[72,256]{1,0:T(8,128)S(1)}, f32[72,256]{1,0:T(8,128)S(1)}, u32[]{:S(2)}, u32[]{:S(2)}) collective-permute-start(f32[72,256]{1,0:T(8,128)S(1)} %get-tuple-element.27), channel_id=1, source_target_pairs={{0,2},{1,3},{2,0},{3,1},{4,6},{5,7},{6,4},{7,5},{8,10},{9,11},{10,... | collective-permute-start | bytes 221192 | tf_op jit(solution)/shard_map/ppermute | solution.py:545
  5.2 0.0 collective-permute-start.2
  5.2 0.5 %collective-permute-start.4 = (f32[3,8,128]{2,1,0:T(8,128)S(1)}, f32[3,8,128]{2,1,0:T(8,128)S(1)}, u32[]{:S(2)}, u32[]{:S(2)}) collective-permute-start(f32[3,8,128]{2,1,0:T(8,128)S(1)} %get-tuple-element.31), channel_id=1, source_target_pairs={{0,1},{1,0},{2,3},{3,2},{4,5},{5,4},{6,7},{7,6},{8,9},{9,8},{10,11... | collective-permute-start | bytes 36872 | tf_op jit(solution)/shard_map/ppermute | solution.py:557
  5.8 0.0 collective-permute-start.6
  6.4 0.0 collective-permute-done.2
  6.4 0.2 collective-permute-start.5
  6.6 2.8 %collective-permute-start.3 = (f32[448,256]{1,0:T(8,128)S(1)}, f32[448,256]{1,0:T(8,128)S(1)}, u32[]{:S(2)}, u32[]{:S(2)}) collective-permute-start(f32[448,256]{1,0:T(8,128)S(1)} %get-tuple-element.30), channel_id=1, source_target_pairs={{0,2},{1,3},{2,0},{3,1},{4,6},{5,7},{6,4},{7,5},{8,10},{9,11},{10,... | collective-permute-start | bytes 1376264 | tf_op jit(solution)/shard_map/ppermute | solution.py:574
  9.4 0.0 collective-permute-done.first2_ref
  9.4 0.0 collective-permute-start.1
  9.4 1.6 %shard_map.123 = (bf16[224,128]{1,0:T(8,128)(2,1)S(1)}, f32[112,8,128]{2,1,0:T(8,128)S(1)}, f32[2,16,128]{2,1,0:T(8,128)S(1)}, f32[16,128]{1,0:T(8,128)S(1)}, bf16[7,64,2048]{2,1,0:T(8,128)(2,1)S(1)}) custom-call(s32[1]{0:T(128)S(6)} %copy.14.counts_ref, f32[3,16,128]{2,1,0:T(8,128)S(1)} %get-tuple-element.33.own_ref, f32[16,128]{1,0:T(8,128)} %bitcast.17, ...), custom_call_target="tpu_custom_call" | custom-call | flops 10000000000 | tf_op jit(solution)/shard_map/pallas_call | solution.py:471
  11.1 0.0 collective-permute-done.4.near_ref
  11.1 0.0 collective-permute-done.5.far_ref
  11.1 0.4 %shard_map.124 = f32[32,128]{1,0:T(8,128)S(1)} custom-call(f32[3,8,128]{2,1,0:T(8,128)S(1)} %collective-permute-done.4.near_ref, f32[3,8,128]{2,1,0:T(8,128)S(1)} %collective-permute-done.5.far_ref, f32[3,16,128]{2,1,0:T(8,128)S(1)} %get-tuple-element.33.own_ref, bf16[224,128]{1,0:T(8,128)(2,1)S(1)} %get-tuple-element.34.selected_ref, ...), custom_call_target="tpu_custom_call" | custom-call | tf_op jit(solution)/shard_map/pallas_call | solution.py:471
  11.5 11.9 %all_to_all.12 = f32[32,1,128]{2,1,0:T(1,128)S(1)} all-to-all(f32[32,1,128]{2,1,0:T(1,128)S(1)} %bitcast.13), channel_id=1, replica_groups=mesh['fine'=8,'coarse'=4] {'fine','coarse'}, dimensions={0} | all-to-all | bytes 32768 | tf_op jit(solution)/shard_map/all_to_all | solution.py:584
  23.4 0.0 collective-permute-done.1.first3_ref
  23.4 0.0 collective-permute-done.3.second2_ref
  23.4 0.0 collective-permute-start.7
  23.4 0.8 %shard_map.126.products_ref = f32[7,64,2048]{2,1,0:T(8,128)S(1)} custom-call(f32[16,128]{1,0:T(8,128)S(1)} %get-tuple-element.47.reaction_ref, bf16[7,64,2048]{2,1,0:T(8,128)(2,1)S(1)} %get-tuple-element.48.fine_ref, bf16[64,2048]{1,0:T(8,128)(2,1)S(1)} %get-tuple-element.49.smoother_ref), custom_call_target="tpu_custom_call" | custom-call | tf_op jit(solution)/shard_map/pallas_call | solution.py:471
  24.2 0.0 collective-permute-done.6.beside_ref
  24.2 0.9 %shard_map.125 = (f32[8,128]{1,0:T(8,128)S(1)}, f32[8,128]{1,0:T(8,128)S(1)}, bf16[1024,64]{1,0:T(8,128)(2,1)S(1)}, bf16[16,8192]{1,0:T(8,128)(2,1)S(1)}, bf16[3...) custom-call(f32[32,128]{1,0:T(8,128)S(1)} %bitcast.12, f32[520,256]{1,0:T(8,128)S(1)} %get-tuple-element.38.mine_ref, ...), custom_call_target="tpu_custom_call" | custom-call | tf_op jit(solution)/shard_map/pallas_call | solution.py:471
  25.1 0.1 collective-permute-done.7.second3_ref
  25.2 3.9 %shard_map.127 = (f32[16,128]{1,0:T(8,128)}, f32[2,128]{1,0:T(2,128)}) custom-call(f32[8,128]{1,0:T(8,128)S(1)} %get-tuple-element.41.side_ref, f32[8,128]{1,0:T(8,128)S(1)} %get-tuple-element.42.begun_ref, bf16[1024,64]{1,0:T(8,128)(2,1)S(1)} %get-tuple-element.43.inverse_ref, bf16[16,8192]{1,0:T(8,128)(2,1)S(1)} %get-tuple-element.44.target_ref, ...), custom_call_target="tpu_custom_call" | custom-call | tf_op jit(solution)/shard_map/pallas_call | solution.py:471
Async XLA Ops:
  2.2 7.2 %collective-permute-start = (f32[72,256]{1,0:T(8,128)S(1)}, f32[72,256]{1,0:T(8,128)S(1)}, u32[]{:S(2)}, u32[]{:S(2)}) collective-permute-start(f32[72,256]{1,0:T(8,128)S(1)} %get-tuple-element.27), channel_id=1, source_target_pairs={{0,2},{1,3},{2,0},{3,1},{4,6},{5,7},{6,4},{7,5},{8,10},{9,11},{10,... | collective-permute-start | bytes 221192 | tf_op jit(solution)/shard_map/ppermute | solution.py:545
  5.2 1.2 %collective-permute-start.2 = (f32[3,8,128]{2,1,0:T(8,128)S(1)}, f32[3,8,128]{2,1,0:T(8,128)S(1)}, u32[]{:S(2)}, u32[]{:S(2)}) collective-permute-start(f32[3,8,128]{2,1,0:T(8,128)S(1)} %get-tuple-element.29), channel_id=1, source_target_pairs={{0,1},{1,0},{2,3},{3,2},{4,5},{5,4},{6,7},{7,6},{8,9},{9,8},{10,11... | collective-permute-start | bytes 36872 | tf_op jit(solution)/shard_map/ppermute | solution.py:556
  5.2 5.8 %collective-permute-start.4 = (f32[3,8,128]{2,1,0:T(8,128)S(1)}, f32[3,8,128]{2,1,0:T(8,128)S(1)}, u32[]{:S(2)}, u32[]{:S(2)}) collective-permute-start(f32[3,8,128]{2,1,0:T(8,128)S(1)} %get-tuple-element.31), channel_id=1, source_target_pairs={{0,1},{1,0},{2,3},{3,2},{4,5},{5,4},{6,7},{7,6},{8,9},{9,8},{10,11... | collective-permute-start | bytes 36872 | tf_op jit(solution)/shard_map/ppermute | solution.py:557
  5.8 18.5 %collective-permute-start.6 = (f32[520,256]{1,0:T(8,128)S(1)}, f32[520,256]{1,0:T(8,128)S(1)}, u32[]{:S(2)}, u32[]{:S(2)}) collective-permute-start(f32[520,256]{1,0:T(8,128)S(1)} %get-tuple-element.38.mine_ref), channel_id=1, source_target_pairs={{0,1},{1,0},{2,3},{3,2},{4,5},{5,4},{6,7},{7,6},{8,9},{9,8},{10,11... | collective-permute-start | bytes 1597448 | tf_op jit(solution)/shard_map/ppermute | solution.py:573
  6.4 4.7 %collective-permute-start.5 = (f32[3,8,128]{2,1,0:T(8,128)S(1)}, f32[3,8,128]{2,1,0:T(8,128)S(1)}, u32[]{:S(2)}, u32[]{:S(2)}) collective-permute-start(f32[3,8,128]{2,1,0:T(8,128)S(1)} %collective-permute-done.2), channel_id=1, source_target_pairs={{0,2},{1,0},{2,4},{3,1},{4,6},{5,3},{6,8},{7,5},{8,10},{9,7},{10,1... | collective-permute-start | bytes 36872 | tf_op jit(solution)/shard_map/ppermute | solution.py:561
  6.6 16.8 %collective-permute-start.3 = (f32[448,256]{1,0:T(8,128)S(1)}, f32[448,256]{1,0:T(8,128)S(1)}, u32[]{:S(2)}, u32[]{:S(2)}) collective-permute-start(f32[448,256]{1,0:T(8,128)S(1)} %get-tuple-element.30), channel_id=1, source_target_pairs={{0,2},{1,3},{2,0},{3,1},{4,6},{5,7},{6,4},{7,5},{8,10},{9,11},{10,... | collective-permute-start | bytes 1376264 | tf_op jit(solution)/shard_map/ppermute | solution.py:574
  9.4 14.0 %collective-permute-start.1 = (f32[72,256]{1,0:T(8,128)S(1)}, f32[72,256]{1,0:T(8,128)S(1)}, u32[]{:S(2)}, u32[]{:S(2)}) collective-permute-start(f32[72,256]{1,0:T(8,128)S(1)} %collective-permute-done.first2_ref), channel_id=1, source_target_pairs={{0,1},{1,0},{2,3},{3,2},{4,5},{5,4},{6,7},{7,6},{8,9},{9,8},{10,11... | collective-permute-start | bytes 221192 | tf_op jit(solution)/shard_map/ppermute | solution.py:575
  23.4 1.8 %collective-permute-start.7 = (f32[448,256]{1,0:T(8,128)S(1)}, f32[448,256]{1,0:T(8,128)S(1)}, u32[]{:S(2)}, u32[]{:S(2)}) collective-permute-start(f32[448,256]{1,0:T(8,128)S(1)} %collective-permute-done.3.second2_ref), channel_id=1, source_target_pairs={{0,1},{1,0},{2,3},{3,2},{4,5},{5,4},{6,7},{7,6},{8,9},{9,8},{10,11... | collective-permute-start | bytes 1376264 | tf_op jit(solution)/shard_map/ppermute | solution.py:586

commit v9 on v8

--- a/solution.py
+++ b/solution.py
@@ -554,10 +554,11 @@
         target = d + 2 if d % 2 == 0 else d - 2
         chain.append((d, target if 0 <= target < devices else d ^ 1))
     onward = lax.ppermute(onward, BOTH, partner)
+    near, onward = lax.optimization_barrier((near, onward))
     near = lax.ppermute(near, BOTH, partner)
 
     if copied:
-        second, onward = lax.optimization_barrier((second, onward))
+        second, packed, onward = lax.optimization_barrier((second, packed, onward))
     far = lax.ppermute(onward, BOTH, chain)
     selected, weighed, local, masked, fine_here = call(
         prepare_kernel,
@@ -572,7 +573,6 @@
     if copied:
         beside = lax.ppermute(packed, "coarse", swap)
         second2 = lax.ppermute(second, "coarse", across)
-        first3 = lax.ppermute(first2, "coarse", swap)
 
     sent = call(
         functools.partial(residual_kernel, devices), shape_of(devices, LANES), "vvvvvv", scratch=[picked], cost=None
@@ -581,6 +581,8 @@
     finish_scratch = [picked, *products]
     common = (near, far, own, selected)
     if copied:
+        first2, _ = lax.optimization_barrier((first2, sent))
+        first3 = lax.ppermute(first2, "coarse", swap)
         gathered = lax.all_to_all(sent, BOTH, 0, 0, tiled=True)
         first3, second2, gathered = lax.optimization_barrier((first3, second2, gathered))
         second3 = lax.ppermute(second2, "coarse", swap)

time: 29.4 us -> 29.5 us (level)
    ppermute x1, starting transfers between devices: 0.01 us -> 0.52 us  [shards(): onward = lax.ppermute(onward, BOTH, partner)]
    ppermute x1, starting transfers between devices: 3.03 us -> 2.59 us  [shards(): first2 = lax.ppermute(first, 'coarse', across)]
    ppermute x1, starting transfers between devices: 0.51 us -> 0.13 us  [shards(): near = lax.ppermute(near, BOTH, partner)]
    ppermute x1, starting transfers between devices: 2.8 us -> 2.45 us  [shards(): second2 = lax.ppermute(second, 'coarse', across)]
where the time goes in v9:
time: 29.5 us; the launch traced here: 29.3 us
  blocking collectives  11.9 us (40%)
  Pallas kernels  9.2 us (31%)
  starting transfers between devices  6.7 us (23%)
  between operations  1.36 us (5%)
    all_to_all x1, blocking collectives, shards(): gathered = lax.all_to_all(sent, BOTH, 0, 0, tiled=True)  11.9 us
    pallas_call x6, Pallas kernels, placed(): run(*(pltpu.with_memory_space_constraint(x, pltpu.HBM) if c == 'a' else x...  9.2 us
    ppermute x1, starting transfers between devices, shards(): first2 = lax.ppermute(first, 'coarse', across)  2.59 us
    ppermute x1, starting transfers between devices, shards(): second2 = lax.ppermute(second, 'coarse', across)  2.45 us
  transfers between devices with their start and end apart: 8, of which 1 were waited for; matrix products, arithmetic and copies ran while one was open for 0% of the time, Pallas kernels for 13%

profile of v9, /device:TPU:0, one launch (start us, length us, event | category | flops | bytes accessed | tf_op | source)
XLA Modules:
  0.0 29.3 jit_solution(16026419594899183322)
XLA Ops:
  0.6 1.6 %shard_map.122 = (f32[3,8,128]{2,1,0:T(8,128)S(1)}, f32[3,8,128]{2,1,0:T(8,128)S(1)}, f32[3,16,128]{2,1,0:T(8,128)S(1)}, bf16[64,2048]{1,0:T(8,128)(2,1)S(1)}, f...) custom-call(f32[16,128]{1,0:T(8,128)} %bitcast.16, f32[16,128]{1,0:T(8,128)} %bitcast.15, ...), custom_call_target="tpu_custom_call" | custom-call | tf_op jit(solution)/shard_map/pallas_call | solution.py:471
  2.2 0.5 %collective-permute-start.1 = (f32[3,8,128]{2,1,0:T(8,128)S(1)}, f32[3,8,128]{2,1,0:T(8,128)S(1)}, u32[]{:S(2)}, u32[]{:S(2)}) collective-permute-start(f32[3,8,128]{2,1,0:T(8,128)S(1)} %get-tuple-element.33), channel_id=1, source_target_pairs={{0,1},{1,0},{2,3},{3,2},{4,5},{5,4},{6,7},{7,6},{8,9},{9,8},{10,11... | collective-permute-start | bytes 36872 | tf_op jit(solution)/shard_map/ppermute | solution.py:556
  2.7 2.6 %collective-permute-start = (f32[72,256]{1,0:T(8,128)S(1)}, f32[72,256]{1,0:T(8,128)S(1)}, u32[]{:S(2)}, u32[]{:S(2)}) collective-permute-start(f32[72,256]{1,0:T(8,128)S(1)} %get-tuple-element.31), channel_id=1, source_target_pairs={{0,2},{1,3},{2,0},{3,1},{4,6},{5,7},{6,4},{7,5},{8,10},{9,11},{10,... | collective-permute-start | bytes 221192 | tf_op jit(solution)/shard_map/ppermute | solution.py:545
  6.0 0.0 collective-permute-done.1
  6.0 0.4 %collective-permute-start.3 = (f32[3,8,128]{2,1,0:T(8,128)S(1)}, f32[3,8,128]{2,1,0:T(8,128)S(1)}, u32[]{:S(2)}, u32[]{:S(2)}) collective-permute-start(f32[3,8,128]{2,1,0:T(8,128)S(1)} %collective-permute-done.1), channel_id=1, source_target_pairs={{0,2},{1,0},{2,4},{3,1},{4,6},{5,3},{6,8},{7,5},{8,10},{9,7},{10,1... | collective-permute-start | bytes 36872 | tf_op jit(solution)/shard_map/ppermute | solution.py:562
  6.4 0.1 collective-permute-start.2
  6.5 2.4 %collective-permute-start.5 = (f32[448,256]{1,0:T(8,128)S(1)}, f32[448,256]{1,0:T(8,128)S(1)}, u32[]{:S(2)}, u32[]{:S(2)}) collective-permute-start(f32[448,256]{1,0:T(8,128)S(1)} %get-tuple-element.44), channel_id=1, source_target_pairs={{0,2},{1,3},{2,0},{3,1},{4,6},{5,7},{6,4},{7,5},{8,10},{9,11},{10,... | collective-permute-start | bytes 1376264 | tf_op jit(solution)/shard_map/ppermute | solution.py:575
  9.0 1.6 %shard_map.123 = (bf16[224,128]{1,0:T(8,128)(2,1)S(1)}, f32[112,8,128]{2,1,0:T(8,128)S(1)}, f32[2,16,128]{2,1,0:T(8,128)S(1)}, f32[16,128]{1,0:T(8,128)S(1)}, bf16[7,64,2048]{2,1,0:T(8,128)(2,1)S(1)}) custom-call(s32[1]{0:T(128)S(6)} %copy.14.counts_ref, f32[3,16,128]{2,1,0:T(8,128)S(1)} %get-tuple-element.39.own_ref, f32[16,128]{1,0:T(8,128)} %bitcast.17, ...), custom_call_target="tpu_custom_call" | custom-call | flops 10000000000 | tf_op jit(solution)/shard_map/pallas_call | solution.py:471
  10.6 0.0 collective-permute-done.3.far_ref
  10.6 0.0 collective-permute-done.2.near_ref
  10.6 0.4 %shard_map.124 = f32[32,128]{1,0:T(8,128)S(1)} custom-call(f32[3,8,128]{2,1,0:T(8,128)S(1)} %collective-permute-done.2.near_ref, f32[3,8,128]{2,1,0:T(8,128)S(1)} %collective-permute-done.3.far_ref, f32[3,16,128]{2,1,0:T(8,128)S(1)} %get-tuple-element.39.own_ref, bf16[224,128]{1,0:T(8,128)(2,1)S(1)} %get-tuple-element.40.selected_ref, ...), custom_call_target="tpu_custom_call" | custom-call | tf_op jit(solution)/shard_map/pallas_call | solution.py:471
  11.0 0.0 collective-permute-done.first2_ref
  11.0 0.3 %collective-permute-start.4 = (f32[72,256]{1,0:T(8,128)S(1)}, f32[72,256]{1,0:T(8,128)S(1)}, u32[]{:S(2)}, u32[]{:S(2)}) collective-permute-start(f32[72,256]{1,0:T(8,128)S(1)} %collective-permute-done.first2_ref), channel_id=1, source_target_pairs={{0,1},{1,0},{2,3},{3,2},{4,5},{5,4},{6,7},{7,6},{8,9},{9,8},{10,11... | collective-permute-start | bytes 221192 | tf_op jit(solution)/shard_map/ppermute | solution.py:585
  11.3 0.3 collective-permute-start.6
  11.6 11.9 %all_to_all.12 = f32[32,1,128]{2,1,0:T(1,128)S(1)} all-to-all(f32[32,1,128]{2,1,0:T(1,128)S(1)} %bitcast.13), channel_id=1, replica_groups=mesh['fine'=8,'coarse'=4] {'fine','coarse'}, dimensions={0} | all-to-all | bytes 32768 | tf_op jit(solution)/shard_map/all_to_all | solution.py:586
  23.5 0.0 collective-permute-done.4.first3_ref
  23.5 0.0 collective-permute-done.5.second2_ref
  23.5 0.0 collective-permute-start.7
  23.5 0.8 %shard_map.126.products_ref = f32[7,64,2048]{2,1,0:T(8,128)S(1)} custom-call(f32[16,128]{1,0:T(8,128)S(1)} %get-tuple-element.55.reaction_ref, bf16[7,64,2048]{2,1,0:T(8,128)(2,1)S(1)} %get-tuple-element.56.fine_ref, bf16[64,2048]{1,0:T(8,128)(2,1)S(1)} %get-tuple-element.57.smoother_ref), custom_call_target="tpu_custom_call" | custom-call | tf_op jit(solution)/shard_map/pallas_call | solution.py:471
  24.4 0.0 collective-permute-done.6.beside_ref
  24.4 0.9 %shard_map.125 = (f32[8,128]{1,0:T(8,128)S(1)}, f32[8,128]{1,0:T(8,128)S(1)}, bf16[1024,64]{1,0:T(8,128)(2,1)S(1)}, bf16[16,8192]{1,0:T(8,128)(2,1)S(1)}, bf16[3...) custom-call(f32[32,128]{1,0:T(8,128)S(1)} %bitcast.12, f32[520,256]{1,0:T(8,128)S(1)} %get-tuple-element.46.mine_ref, ...), custom_call_target="tpu_custom_call" | custom-call | tf_op jit(solution)/shard_map/pallas_call | solution.py:471
  25.3 0.1 collective-permute-done.7.second3_ref
  25.4 3.9 %shard_map.127 = (f32[16,128]{1,0:T(8,128)}, f32[2,128]{1,0:T(2,128)}) custom-call(f32[8,128]{1,0:T(8,128)S(1)} %get-tuple-element.49.side_ref, f32[8,128]{1,0:T(8,128)S(1)} %get-tuple-element.50.begun_ref, bf16[1024,64]{1,0:T(8,128)(2,1)S(1)} %get-tuple-element.51.inverse_ref, bf16[16,8192]{1,0:T(8,128)(2,1)S(1)} %get-tuple-element.52.target_ref, ...), custom_call_target="tpu_custom_call" | custom-call | tf_op jit(solution)/shard_map/pallas_call | solution.py:471
Async XLA Ops:
  2.2 3.8 %collective-permute-start.1 = (f32[3,8,128]{2,1,0:T(8,128)S(1)}, f32[3,8,128]{2,1,0:T(8,128)S(1)}, u32[]{:S(2)}, u32[]{:S(2)}) collective-permute-start(f32[3,8,128]{2,1,0:T(8,128)S(1)} %get-tuple-element.33), channel_id=1, source_target_pairs={{0,1},{1,0},{2,3},{3,2},{4,5},{5,4},{6,7},{7,6},{8,9},{9,8},{10,11... | collective-permute-start | bytes 36872 | tf_op jit(solution)/shard_map/ppermute | solution.py:556
  2.7 8.3 %collective-permute-start = (f32[72,256]{1,0:T(8,128)S(1)}, f32[72,256]{1,0:T(8,128)S(1)}, u32[]{:S(2)}, u32[]{:S(2)}) collective-permute-start(f32[72,256]{1,0:T(8,128)S(1)} %get-tuple-element.31), channel_id=1, source_target_pairs={{0,2},{1,3},{2,0},{3,1},{4,6},{5,7},{6,4},{7,5},{8,10},{9,11},{10,... | collective-permute-start | bytes 221192 | tf_op jit(solution)/shard_map/ppermute | solution.py:545
  6.0 4.6 %collective-permute-start.3 = (f32[3,8,128]{2,1,0:T(8,128)S(1)}, f32[3,8,128]{2,1,0:T(8,128)S(1)}, u32[]{:S(2)}, u32[]{:S(2)}) collective-permute-start(f32[3,8,128]{2,1,0:T(8,128)S(1)} %collective-permute-done.1), channel_id=1, source_target_pairs={{0,2},{1,0},{2,4},{3,1},{4,6},{5,3},{6,8},{7,5},{8,10},{9,7},{10,1... | collective-permute-start | bytes 36872 | tf_op jit(solution)/shard_map/ppermute | solution.py:562
  6.4 4.2 %collective-permute-start.2 = (f32[3,8,128]{2,1,0:T(8,128)S(1)}, f32[3,8,128]{2,1,0:T(8,128)S(1)}, u32[]{:S(2)}, u32[]{:S(2)}) collective-permute-start(f32[3,8,128]{2,1,0:T(8,128)S(1)} %get-tuple-element.34), channel_id=1, source_target_pairs={{0,1},{1,0},{2,3},{3,2},{4,5},{5,4},{6,7},{7,6},{8,9},{9,8},{10,11... | collective-permute-start | bytes 36872 | tf_op jit(solution)/shard_map/ppermute | solution.py:558
  6.5 17.0 %collective-permute-start.5 = (f32[448,256]{1,0:T(8,128)S(1)}, f32[448,256]{1,0:T(8,128)S(1)}, u32[]{:S(2)}, u32[]{:S(2)}) collective-permute-start(f32[448,256]{1,0:T(8,128)S(1)} %get-tuple-element.44), channel_id=1, source_target_pairs={{0,2},{1,3},{2,0},{3,1},{4,6},{5,7},{6,4},{7,5},{8,10},{9,11},{10,... | collective-permute-start | bytes 1376264 | tf_op jit(solution)/shard_map/ppermute | solution.py:575
  11.0 12.5 %collective-permute-start.4 = (f32[72,256]{1,0:T(8,128)S(1)}, f32[72,256]{1,0:T(8,128)S(1)}, u32[]{:S(2)}, u32[]{:S(2)}) collective-permute-start(f32[72,256]{1,0:T(8,128)S(1)} %collective-permute-done.first2_ref), channel_id=1, source_target_pairs={{0,1},{1,0},{2,3},{3,2},{4,5},{5,4},{6,7},{7,6},{8,9},{9,8},{10,11... | collective-permute-start | bytes 221192 | tf_op jit(solution)/shard_map/ppermute | solution.py:585
  11.3 13.1 %collective-permute-start.6 = (f32[520,256]{1,0:T(8,128)S(1)}, f32[520,256]{1,0:T(8,128)S(1)}, u32[]{:S(2)}, u32[]{:S(2)}) collective-permute-start(f32[520,256]{1,0:T(8,128)S(1)} %get-tuple-element.46.mine_ref), channel_id=1, source_target_pairs={{0,1},{1,0},{2,3},{3,2},{4,5},{5,4},{6,7},{7,6},{8,9},{9,8},{10,11... | collective-permute-start | bytes 1597448 | tf_op jit(solution)/shard_map/ppermute | solution.py:574
  23.5 1.8 %collective-permute-start.7 = (f32[448,256]{1,0:T(8,128)S(1)}, f32[448,256]{1,0:T(8,128)S(1)}, u32[]{:S(2)}, u32[]{:S(2)}) collective-permute-start(f32[448,256]{1,0:T(8,128)S(1)} %collective-permute-done.5.second2_ref), channel_id=1, source_target_pairs={{0,1},{1,0},{2,3},{3,2},{4,5},{5,4},{6,7},{7,6},{8,9},{9,8},{10,11... | collective-permute-start | bytes 1376264 | tf_op jit(solution)/shard_map/ppermute | solution.py:588

commit v10 on v9

--- a/solution.py
+++ b/solution.py
@@ -573,6 +573,7 @@
     if copied:
         beside = lax.ppermute(packed, "coarse", swap)
         second2 = lax.ppermute(second, "coarse", across)
+        first3 = lax.ppermute(first2, "coarse", swap)
 
     sent = call(
         functools.partial(residual_kernel, devices), shape_of(devices, LANES), "vvvvvv", scratch=[picked], cost=None
@@ -581,8 +582,6 @@
     finish_scratch = [picked, *products]
     common = (near, far, own, selected)
     if copied:
-        first2, _ = lax.optimization_barrier((first2, sent))
-        first3 = lax.ppermute(first2, "coarse", swap)
         gathered = lax.all_to_all(sent, BOTH, 0, 0, tiled=True)
         first3, second2, gathered = lax.optimization_barrier((first3, second2, gathered))
         second3 = lax.ppermute(second2, "coarse", swap)

time: 29.5 us -> 29.3 us (level)
  waiting for transfers between devices: 0.09 us -> 0.61 us
  blocking collectives: 11.9 us -> 11.4 us
    ppermute x1, waiting for transfers between devices: 0.01 us -> 0.52 us  [shards(): onward = lax.ppermute(onward, BOTH, partner)]
    ppermute x1, starting transfers between devices: 0.52 us -> 0.01 us  [shards(): onward = lax.ppermute(onward, BOTH, partner)]
    all_to_all x1, blocking collectives: 11.9 us -> 11.4 us  [shards(): gathered = lax.all_to_all(sent, BOTH, 0, 0, tiled=True)]
    ppermute x1, starting transfers between devices: 2.59 us -> 3.03 us  [shards(): first2 = lax.ppermute(first, 'coarse', across)]
    ppermute x1, starting transfers between devices: 0.44 us -> 0.08 us  [shards(): far = lax.ppermute(onward, BOTH, chain)]
    ppermute x1, starting transfers between devices: 0.13 us -> 0.43 us  [shards(): near = lax.ppermute(near, BOTH, partner)]
  transfers between devices with their start and end apart: 8 -> 8, of which waited for: 1 -> 2; matrix products, arithmetic and copies ran while one was open for 0% -> 0% of each run, Pallas kernels for 13% -> 13%
where the time goes in v10:
time: 29.3 us; the launch traced here: 29.1 us
  blocking collectives  11.4 us (39%)
  Pallas kernels  9.22 us (31%)
  starting transfers between devices  6.5 us (22%)
  between operations  1.35 us (5%)
  waiting for transfers between devices  0.61 us (2%)
    all_to_all x1, blocking collectives, shards(): gathered = lax.all_to_all(sent, BOTH, 0, 0, tiled=True)  11.4 us
    pallas_call x6, Pallas kernels, placed(): run(*(pltpu.with_memory_space_constraint(x, pltpu.HBM) if c == 'a' else x...  9.22 us
    ppermute x1, starting transfers between devices, shards(): first2 = lax.ppermute(first, 'coarse', across)  3.03 us
    ppermute x1, starting transfers between devices, shards(): second2 = lax.ppermute(second, 'coarse', across)  2.45 us
  transfers between devices with their start and end apart: 8, of which 2 were waited for; matrix products, arithmetic and copies ran while one was open for 0% of the time, Pallas kernels for 13%

profile of v10, /device:TPU:0, one launch (start us, length us, event | category | flops | bytes accessed | tf_op | source)
XLA Modules:
  0.0 29.1 jit_solution(15511924027568351066)
XLA Ops:
  0.6 1.6 %shard_map.122 = (f32[3,8,128]{2,1,0:T(8,128)S(1)}, f32[3,8,128]{2,1,0:T(8,128)S(1)}, f32[3,16,128]{2,1,0:T(8,128)S(1)}, bf16[64,2048]{1,0:T(8,128)(2,1)S(1)}, f...) custom-call(f32[16,128]{1,0:T(8,128)} %bitcast.16, f32[16,128]{1,0:T(8,128)} %bitcast.15, ...), custom_call_target="tpu_custom_call" | custom-call | tf_op jit(solution)/shard_map/pallas_call | solution.py:471
  2.2 3.0 %collective-permute-start = (f32[72,256]{1,0:T(8,128)S(1)}, f32[72,256]{1,0:T(8,128)S(1)}, u32[]{:S(2)}, u32[]{:S(2)}) collective-permute-start(f32[72,256]{1,0:T(8,128)S(1)} %get-tuple-element.30), channel_id=1, source_target_pairs={{0,2},{1,3},{2,0},{3,1},{4,6},{5,7},{6,4},{7,5},{8,10},{9,11},{10,... | collective-permute-start | bytes 221192 | tf_op jit(solution)/shard_map/ppermute | solution.py:545
  5.2 0.0 collective-permute-start.2
  5.9 0.5 %collective-permute-done.2 = f32[3,8,128]{2,1,0:T(8,128)S(1)} collective-permute-done((f32[3,8,128]{2,1,0:T(8,128)S(1)}, f32[3,8,128]{2,1,0:T(8,128)S(1)}, u32[]{:S(2)}, u32[]{:S(2)}) %collective-permute-start.2) | collective-permute-done | bytes 12320 | tf_op jit(solution)/shard_map/ppermute | solution.py:556
  6.4 0.1 collective-permute-start.5
  6.5 0.4 %collective-permute-start.4 = (f32[3,8,128]{2,1,0:T(8,128)S(1)}, f32[3,8,128]{2,1,0:T(8,128)S(1)}, u32[]{:S(2)}, u32[]{:S(2)}) collective-permute-start(f32[3,8,128]{2,1,0:T(8,128)S(1)} %get-tuple-element.37), channel_id=1, source_target_pairs={{0,1},{1,0},{2,3},{3,2},{4,5},{5,4},{6,7},{7,6},{8,9},{9,8},{10,11... | collective-permute-start | bytes 36872 | tf_op jit(solution)/shard_map/ppermute | solution.py:558
  6.9 2.4 %collective-permute-start.3 = (f32[448,256]{1,0:T(8,128)S(1)}, f32[448,256]{1,0:T(8,128)S(1)}, u32[]{:S(2)}, u32[]{:S(2)}) collective-permute-start(f32[448,256]{1,0:T(8,128)S(1)} %get-tuple-element.36), channel_id=1, source_target_pairs={{0,2},{1,3},{2,0},{3,1},{4,6},{5,7},{6,4},{7,5},{8,10},{9,11},{10,... | collective-permute-start | bytes 1376264 | tf_op jit(solution)/shard_map/ppermute | solution.py:575
  9.4 0.2 collective-permute-start.6
  9.6 0.0 collective-permute-done.first2_ref
  9.6 0.3 collective-permute-start.1
  9.9 1.6 %shard_map.123 = (bf16[224,128]{1,0:T(8,128)(2,1)S(1)}, f32[112,8,128]{2,1,0:T(8,128)S(1)}, f32[2,16,128]{2,1,0:T(8,128)S(1)}, f32[16,128]{1,0:T(8,128)S(1)}, bf16[7,64,2048]{2,1,0:T(8,128)(2,1)S(1)}) custom-call(s32[1]{0:T(128)S(6)} %copy.14.counts_ref, f32[3,16,128]{2,1,0:T(8,128)S(1)} %get-tuple-element.39.own_ref, f32[16,128]{1,0:T(8,128)} %bitcast.17, ...), custom_call_target="tpu_custom_call" | custom-call | flops 10000000000 | tf_op jit(solution)/shard_map/pallas_call | solution.py:471
  11.5 0.0 collective-permute-done.5.far_ref
  11.5 0.0 collective-permute-done.4.near_ref
  11.5 0.4 %shard_map.124 = f32[32,128]{1,0:T(8,128)S(1)} custom-call(f32[3,8,128]{2,1,0:T(8,128)S(1)} %collective-permute-done.4.near_ref, f32[3,8,128]{2,1,0:T(8,128)S(1)} %collective-permute-done.5.far_ref, f32[3,16,128]{2,1,0:T(8,128)S(1)} %get-tuple-element.39.own_ref, bf16[224,128]{1,0:T(8,128)(2,1)S(1)} %get-tuple-element.40.selected_ref, ...), custom_call_target="tpu_custom_call" | custom-call | tf_op jit(solution)/shard_map/pallas_call | solution.py:471
  11.9 11.4 %all_to_all.12 = f32[32,1,128]{2,1,0:T(1,128)S(1)} all-to-all(f32[32,1,128]{2,1,0:T(1,128)S(1)} %bitcast.13), channel_id=1, replica_groups=mesh['fine'=8,'coarse'=4] {'fine','coarse'}, dimensions={0} | all-to-all | bytes 32768 | tf_op jit(solution)/shard_map/all_to_all | solution.py:585
  23.3 0.0 collective-permute-done.1.first3_ref
  23.3 0.0 collective-permute-done.3.second2_ref
  23.3 0.0 collective-permute-start.7
  23.4 0.8 %shard_map.126.products_ref = f32[7,64,2048]{2,1,0:T(8,128)S(1)} custom-call(f32[16,128]{1,0:T(8,128)S(1)} %get-tuple-element.53.reaction_ref, bf16[7,64,2048]{2,1,0:T(8,128)(2,1)S(1)} %get-tuple-element.54.fine_ref, bf16[64,2048]{1,0:T(8,128)(2,1)S(1)} %get-tuple-element.55.smoother_ref), custom_call_target="tpu_custom_call" | custom-call | tf_op jit(solution)/shard_map/pallas_call | solution.py:471
  24.2 0.0 collective-permute-done.6.beside_ref
  24.2 0.9 %shard_map.125 = (f32[8,128]{1,0:T(8,128)S(1)}, f32[8,128]{1,0:T(8,128)S(1)}, bf16[1024,64]{1,0:T(8,128)(2,1)S(1)}, bf16[16,8192]{1,0:T(8,128)(2,1)S(1)}, bf16[3...) custom-call(f32[32,128]{1,0:T(8,128)S(1)} %bitcast.12, f32[520,256]{1,0:T(8,128)S(1)} %get-tuple-element.44.mine_ref, ...), custom_call_target="tpu_custom_call" | custom-call | tf_op jit(solution)/shard_map/pallas_call | solution.py:471
  25.1 0.1 collective-permute-done.7.second3_ref
  25.2 3.9 %shard_map.127 = (f32[16,128]{1,0:T(8,128)}, f32[2,128]{1,0:T(2,128)}) custom-call(f32[8,128]{1,0:T(8,128)S(1)} %get-tuple-element.47.side_ref, f32[8,128]{1,0:T(8,128)S(1)} %get-tuple-element.48.begun_ref, bf16[1024,64]{1,0:T(8,128)(2,1)S(1)} %get-tuple-element.49.inverse_ref, bf16[16,8192]{1,0:T(8,128)(2,1)S(1)} %get-tuple-element.50.target_ref, ...), custom_call_target="tpu_custom_call" | custom-call | tf_op jit(solution)/shard_map/pallas_call | solution.py:471
Async XLA Ops:
  2.2 7.4 %collective-permute-start = (f32[72,256]{1,0:T(8,128)S(1)}, f32[72,256]{1,0:T(8,128)S(1)}, u32[]{:S(2)}, u32[]{:S(2)}) collective-permute-start(f32[72,256]{1,0:T(8,128)S(1)} %get-tuple-element.30), channel_id=1, source_target_pairs={{0,2},{1,3},{2,0},{3,1},{4,6},{5,7},{6,4},{7,5},{8,10},{9,11},{10,... | collective-permute-start | bytes 221192 | tf_op jit(solution)/shard_map/ppermute | solution.py:545
  5.2 1.2 %collective-permute-start.2 = (f32[3,8,128]{2,1,0:T(8,128)S(1)}, f32[3,8,128]{2,1,0:T(8,128)S(1)}, u32[]{:S(2)}, u32[]{:S(2)}) collective-permute-start(f32[3,8,128]{2,1,0:T(8,128)S(1)} %get-tuple-element.34), channel_id=1, source_target_pairs={{0,1},{1,0},{2,3},{3,2},{4,5},{5,4},{6,7},{7,6},{8,9},{9,8},{10,11... | collective-permute-start | bytes 36872 | tf_op jit(solution)/shard_map/ppermute | solution.py:556
  6.4 5.1 %collective-permute-start.5 = (f32[3,8,128]{2,1,0:T(8,128)S(1)}, f32[3,8,128]{2,1,0:T(8,128)S(1)}, u32[]{:S(2)}, u32[]{:S(2)}) collective-permute-start(f32[3,8,128]{2,1,0:T(8,128)S(1)} %collective-permute-done.2), channel_id=1, source_target_pairs={{0,2},{1,0},{2,4},{3,1},{4,6},{5,3},{6,8},{7,5},{8,10},{9,7},{10,1... | collective-permute-start | bytes 36872 | tf_op jit(solution)/shard_map/ppermute | solution.py:562
  6.5 5.0 %collective-permute-start.4 = (f32[3,8,128]{2,1,0:T(8,128)S(1)}, f32[3,8,128]{2,1,0:T(8,128)S(1)}, u32[]{:S(2)}, u32[]{:S(2)}) collective-permute-start(f32[3,8,128]{2,1,0:T(8,128)S(1)} %get-tuple-element.37), channel_id=1, source_target_pairs={{0,1},{1,0},{2,3},{3,2},{4,5},{5,4},{6,7},{7,6},{8,9},{9,8},{10,11... | collective-permute-start | bytes 36872 | tf_op jit(solution)/shard_map/ppermute | solution.py:558
  6.9 16.4 %collective-permute-start.3 = (f32[448,256]{1,0:T(8,128)S(1)}, f32[448,256]{1,0:T(8,128)S(1)}, u32[]{:S(2)}, u32[]{:S(2)}) collective-permute-start(f32[448,256]{1,0:T(8,128)S(1)} %get-tuple-element.36), channel_id=1, source_target_pairs={{0,2},{1,3},{2,0},{3,1},{4,6},{5,7},{6,4},{7,5},{8,10},{9,11},{10,... | collective-permute-start | bytes 1376264 | tf_op jit(solution)/shard_map/ppermute | solution.py:575
  9.4 14.8 %collective-permute-start.6 = (f32[520,256]{1,0:T(8,128)S(1)}, f32[520,256]{1,0:T(8,128)S(1)}, u32[]{:S(2)}, u32[]{:S(2)}) collective-permute-start(f32[520,256]{1,0:T(8,128)S(1)} %get-tuple-element.44.mine_ref), channel_id=1, source_target_pairs={{0,1},{1,0},{2,3},{3,2},{4,5},{5,4},{6,7},{7,6},{8,9},{9,8},{10,11... | collective-permute-start | bytes 1597448 | tf_op jit(solution)/shard_map/ppermute | solution.py:574
  9.6 13.7 %collective-permute-start.1 = (f32[72,256]{1,0:T(8,128)S(1)}, f32[72,256]{1,0:T(8,128)S(1)}, u32[]{:S(2)}, u32[]{:S(2)}) collective-permute-start(f32[72,256]{1,0:T(8,128)S(1)} %collective-permute-done.first2_ref), channel_id=1, source_target_pairs={{0,1},{1,0},{2,3},{3,2},{4,5},{5,4},{6,7},{7,6},{8,9},{9,8},{10,11... | collective-permute-start | bytes 221192 | tf_op jit(solution)/shard_map/ppermute | solution.py:576
  23.3 1.8 %collective-permute-start.7 = (f32[448,256]{1,0:T(8,128)S(1)}, f32[448,256]{1,0:T(8,128)S(1)}, u32[]{:S(2)}, u32[]{:S(2)}) collective-permute-start(f32[448,256]{1,0:T(8,128)S(1)} %collective-permute-done.3.second2_ref), channel_id=1, source_target_pairs={{0,1},{1,0},{2,3},{3,2},{4,5},{5,4},{6,7},{7,6},{8,9},{9,8},{10,11... | collective-permute-start | bytes 1376264 | tf_op jit(solution)/shard_map/ppermute | solution.py:587
